TPU v7x, 32 devices: a whole 2x2x4 slice. The times are simulated.
32 devices in a mesh: case: 2 (over y), row: 4 (over z), col: 2 (over x), band: 2 (over core).
Axes of the slice: x: 2, y: 2, z: 4, core: 2. Of those that a mesh axis runs over, the one named last changes fastest.
Arguments:
- positions: float32 [3, 4096], P(None, ('case', 'row', 'col')), parts along dimension 1, as said below
- normals: float32 [3, 4096], P(None, ('case', 'row', 'col')), parts along dimension 1, as said below
- areas: float32 [4096], P(('case', 'row', 'col')), parts along dimension 0, as said below
- emission: float32 [64, 4096], P('band', ('case', 'row', 'col')), parts along dimension 1, may hold values from 0.2 to 2
- reflect: float32 [64, 4096], P('band', ('case', 'row', 'col')), parts along dimension 1, may hold values from 0.2 to 0.9
- pair_row: int32 [512], P(('case', 'row', 'col')), parts along dimension 0, may hold values from 0 to 15, as said below
- pair_col: int32 [512], P(('case', 'row', 'col')), parts along dimension 0, may hold values from 0 to 15, as said below
- pair_live: int32 [512], P(('case', 'row', 'col')), parts along dimension 0, may hold values from 0 to 1, as said below
Outputs:
- radiosity: float32 [64, 4096], P('band', ('case', 'row', 'col')), parts along dimension 1
There are 2 independent parts, one for each index of `case`. A program takes and returns all parts, laid end to end along the dimension named above; each array names one. Nothing has to cross between parts.
Inputs may be any that keep to these rules, and one draw needn't show every extreme that they name: `pair_row`: blocks are numbered so that device r * 2 + c of the row and col axes owns blocks of segment r * 2 + c (2 each). The 32 slots of that device hold every ordered pair (p, q) with p in blocks r * 4 to r * 4 + 3 and q a block whose segment is congruent to c modulo 2, exactly once, its live slots first. Each unordered visible block pair is live in exactly one slot of a part, in one of its two orders. At most 31 slots of one device are live, and some device has exactly that many. `pair_col`: second block of the slot's pair, as described for pair_row. `pair_live`: live slots come first on each device. `positions`: patch centres. `normals`: unit vectors. `areas`: Positive.
All inputs are finite; a program needn't handle non-finite values.
Results may differ from a plain program's by a relative error of at most 0.0003.
Values may be sent and summed in bfloat16 or wider, within the bound.
No kernel may reach another device: no remote copies, remote signals or barrier semaphores. Data moves between devices by JAX's collectives and lax.ppermute only.
A program may use at most 64 MiB of HBM per device.

v0:
```python
import math

import jax
import jax.numpy as jnp
from jax import lax
from jax.sharding import PartitionSpec as P

BLOCK = 128
ITERS = 2


SOFTEN = 0.02


def form_tiles(near, far):
    offset = far[0:3, :, None, :] - near[0:3, :, :, None]
    leaving = jnp.sum(near[3:6, :, :, None] * offset, axis=0)
    arriving = -jnp.sum(far[3:6, :, None, :] * offset, axis=0)
    spacing = jnp.sum(offset * offset, axis=0) + SOFTEN
    return jax.nn.relu(leaving) * jax.nn.relu(arriving) / (math.pi * spacing * spacing)


def shards(positions, normals, areas, emission, reflect, pair_row, pair_col, pair_live):
    patch_dev = areas.shape[0]
    own_blocks = patch_dev // BLOCK
    n_row = lax.axis_size("row")
    n_col = lax.axis_size("col")
    row_blocks = own_blocks * n_col
    col_blocks = own_blocks * n_row
    all_blocks = row_blocks * n_row
    band_half = emission.shape[0]
    row_here = lax.axis_index("row")
    col_here = lax.axis_index("col")
    geometry = jnp.concatenate([positions, normals], axis=0)
    geo_rows = lax.all_gather(geometry, "col", axis=1, tiled=True).reshape(6, row_blocks, BLOCK)
    geo_cols = lax.all_gather(geometry, "row", axis=1, tiled=True).reshape(6, col_blocks, BLOCK)
    slots = pair_row.shape[0]
    rows_seen, cols_seen, live_seen = (
        lax.all_gather(pair_row, ("row", "col"), axis=0, tiled=True),
        lax.all_gather(pair_col, ("row", "col"), axis=0, tiled=True),
        lax.all_gather(pair_live, ("row", "col"), axis=0, tiled=True),
    )
    seen = jnp.zeros((all_blocks * all_blocks,), jnp.int32)
    seen = seen.at[rows_seen * all_blocks + cols_seen].max(live_seen)
    seen = seen.at[cols_seen * all_blocks + rows_seen].max(live_seen)
    near_grid = row_here * row_blocks + jnp.arange(row_blocks, dtype=jnp.int32)
    far_local = jnp.arange(col_blocks, dtype=jnp.int32)
    far_grid = (far_local // own_blocks * n_col + col_here) * own_blocks + far_local % own_blocks
    flags = seen[(near_grid[:, None] * all_blocks + far_grid[None, :]).reshape(-1)]
    order = jnp.argsort(1 - flags, stable=True)
    near_index = order // col_blocks
    far_index = order % col_blocks
    live_float = flags[order].astype(jnp.float32)
    live_count = jnp.sum(flags)
    group_size = math.gcd(slots, 32)
    turns = (live_count + group_size - 1) // group_size
    stored_init = jnp.zeros((1, 1, 1), jnp.bfloat16)
    stored = stored_init
    radiosity = emission
    for sweep in range(ITERS):
        weighted = (areas[None, :] * radiosity).astype(jnp.bfloat16)
        w_cols = lax.all_gather(weighted, "row", axis=1, tiled=True).reshape(
            band_half, col_blocks, BLOCK
        )

        def one_turn(turn_index, state_now):
            acc_rows, acc_cols, kept = state_now
            first_slot = turn_index * group_size
            near_now = lax.dynamic_slice_in_dim(near_index, first_slot, group_size)
            far_now = lax.dynamic_slice_in_dim(far_index, first_slot, group_size)
            live_now = lax.dynamic_slice_in_dim(live_float, first_slot, group_size)
            tiles_now = form_tiles(geo_rows[:, near_now], geo_cols[:, far_now]).astype(jnp.bfloat16)
            far_weights = w_cols[:, far_now]
            to_rows = jnp.einsum(
                "buv,kbv->kbu", tiles_now, far_weights, preferred_element_type=jnp.float32
            )
            acc_rows = acc_rows.at[:, near_now].add(to_rows * live_now[None, :, None])
            return (acc_rows, acc_cols, kept)

        zero_rows = jnp.zeros((band_half, row_blocks, BLOCK), jnp.float32)
        zero_cols = jnp.zeros((1, 1, 1), jnp.float32)
        acc_rows, acc_cols, stored = lax.fori_loop(
            0, turns, one_turn, (zero_rows, zero_cols, stored)
        )
        row_sum = lax.psum_scatter(
            acc_rows.reshape(band_half, row_blocks * BLOCK), "col", scatter_dimension=1, tiled=True
        )
        radiosity = emission + reflect * row_sum
    return radiosity


def solution(mesh):
    return jax.shard_map(
        shards,
        mesh=mesh,
        in_specs=(
            P(None, ("case", "row", "col")),
            P(None, ("case", "row", "col")),
            P(("case", "row", "col")),
            P("band", ("case", "row", "col")),
            P("band", ("case", "row", "col")),
            P(("case", "row", "col")),
            P(("case", "row", "col")),
            P(("case", "row", "col")),
        ),
        out_specs=P("band", ("case", "row", "col")),
        check_vma=False,
    )
```

profile of v0, /device:TPU:0, one launch (start us, length us, event | category | flops | bytes accessed | tf_op | source)
XLA Modules:
  0.0 123.6 jit_solution(9434387843018294891)
XLA Ops:
  6.5 0.0 copy-start.4
  6.5 0.0 reduce-scatter.3.cloned.1.call-start
  6.6 0.1 broadcast_add_fusion
  6.7 0.1 add.198
  6.8 1.2 dynamic-slice
  8.6 0.9 dynamic-update-slice
  9.5 0.8 dynamic-update-slice.1
  10.3 0.8 dynamic-update-slice.2
  11.1 13.1 %all-reduce.3 = (s32[256]{0:T(256)S(1)}, s32[256]{0:T(256)S(1)}, s32[256]{0:T(256)S(1)}) all-reduce(s32[256]{0:T(256)S(1)} %dynamic-update-slice.1, s32[256]{0:T(256)S(1)} %dynamic-update-slice, s32[256]{0:T(256)S(1)} %dynamic-update-slice.2), channel_id=1, replica_groups=mesh['case'=2,'row'=4,'col'=2,'band'=2] {'row','col'}, use_global_device_ids=true, to_apply=%add.1 | all-reduce | flops 768 | bytes 6144
  24.2 2.3 %scatter_custom_fusion.2 = s32[256]{0:T(256)S(1)} fusion(s32[256]{0:T(256)S(1)} %get-tuple-element.199, s32[256]{0:T(256)S(1)} %get-tuple-element.185, s32[]{:T(128)} %copy.83), kind=kCustom, calls=%fused_computation.83 | custom fusion | flops 256 | bytes 1028 | tf_op jit(solution)/shard_map/scatter-max | solution.py:44
  26.5 2.3 %scatter_fusion.2 = s32[256]{0:T(256)S(1)} fusion(s32[256]{0:T(256)S(1)} %scatter_custom_fusion.2, s32[256]{0:T(256)S(1)} %get-tuple-element.198, s32[256]{0:T(256)S(1)} %get-tuple-element.185), kind=kCustom, calls=%fused_computation.11 | custom fusion | flops 256 | bytes 4096 | tf_op jit(solution)/shard_map/scatter-max | solution.py:45
  28.9 0.7 gather_fusion.6
  29.6 0.6 broadcast_subtract_fusion
  30.8 0.0 copy-done.3
  30.8 0.0 copy-done.4
  30.8 4.4 %all_gather.25 = f32[6,512]{1,0:T(8,128)S(1)} all-gather(f32[6,256]{1,0:T(8,128)S(1)} %pad_maximum_fusion), channel_id=1, replica_groups=mesh['case'=2,'row'=4,'col'=2,'band'=2] {'col'}, dimensions={1}, use_global_device_ids=true | all-gather | bytes 18432 | tf_op jit(solution)/shard_map/all_gather | solution.py:35
  35.2 13.1 %all_gather.26 = f32[6,1024]{1,0:T(8,128)S(1)} all-gather(f32[6,256]{1,0:T(8,128)S(1)} %pad_maximum_fusion), channel_id=1, replica_groups=mesh['case'=2,'row'=4,'col'=2,'band'=2] {'row'}, dimensions={1}, use_global_device_ids=true | all-gather | bytes 30720 | tf_op jit(solution)/shard_map/all_gather | solution.py:36
  48.2 1.6 %sort.17 = (s32[32]{0:T(128)}, s32[32]{0:T(128)S(1)}) sort(s32[32]{0:T(128)S(1)} %get-tuple-element.203, s32[32]{0:T(128)S(1)} %iota.18), dimensions={0}, to_apply=%region_3.4 | sort | flops 160 | bytes 512 | tf_op jit(solution)/shard_map/jit(argsort)/sort | solution.py:50
  49.9 0.7 gather_fusion.7
  50.6 0.0 copy-done
  50.6 0.0 copy-done.2
  50.6 13.1 %all_gather.24 = bf16[32,1024]{1,0:T(8,128)(2,1)S(1)} all-gather(bf16[32,256]{1,0:T(8,128)(2,1)S(1)} %multiply_convert_fusion.1), channel_id=1, replica_groups=mesh['case'=2,'row'=4,'col'=2,'band'=2] {'row'}, dimensions={1}, use_global_device_ids=true | all-gather | bytes 81920 | tf_op jit(solution)/shard_map/all_gather | solution.py:62
  63.8 0.0 copy-start.1
  63.8 9.0 %while.20 = (s32[]{:T(128)}, f32[32,4,128]{2,0,1:T(8,128)S(1)}, s32[]{:T(128)}, s32[32]{0:T(128)S(1)}, s32[32]{0:T(128)S(1)}, /*index=5*/bf16[32,8,128]{2,0,1:T(...) while((s32[]{:T(128)}, f32[32,4,128]{2,0,1:T(8,128)S(1)}, ...), condition=%wide.region_9.10_spmd, body=%wide.region_4.9_spmd.sunk | while | flops 47974592 | bytes 16852452 | solution.py:82
  63.9 0.6 gather_fusion
  64.5 0.6 gather_fusion.1
  65.2 0.6 gather_fusion.2
  65.8 4.3 %fusion.56 = (f32[32,128,128]{2,1,0:T(8,128)S(1)}, f32[32,128,128]{2,1,0:T(8,128)S(1)}, f32[32,128,128]{2,1,0:T(8,128)S(1)}) fusion(f32[3,32,128]{2,1,0:T(8,128)S(1)} %copy.52, f32[3,32,128]{2,1,0:T(8,128)S(1)} %copy.53, f32[3,32,128]{2,1,0:T(8,128)S(1)} %copy.54, f32[3,32,128]{2,1,0:T(8,128)S(1)} %copy.55), kind=kLoop, calls=%fused_computation.15.clone.1 | loop fusion | flops 9437184 | bytes 6488064 | tf_op jit(solution)/shard_map/while/body/reduce_sum | solution.py:17
  70.1 0.8 convolution_multiply_fusion.4
  70.9 1.9 %scatter_fusion = f32[32,4,128]{2,0,1:T(8,128)S(1)} fusion(f32[32,4,128]{2,0,1:T(8,128)S(1)} %get-tuple-element.364, s32[32]{0:T(128)S(1)} %get-tuple-element.326, f32[32,32,128]{2,1,0:T(8,128)S(1)} %convolution_multiply_fusion.4), kind=kCustom, calls=%fused_computation.8.clone.1 | custom fusion | flops 131072 | bytes 1572992 | tf_op jit(solution)/shard_map/while/body/scatter-add | solution.py:77
  72.8 0.6 copy_bitcast_fusion.1
  73.4 0.0 reduce-scatter.3.cloned.1.call-update
  73.4 0.0 reduce-scatter.5.cloned.1.call-start
  73.5 8.3 %reduce-scatter.3.cloned.1.call-done = f32[32,256]{1,0:T(8,128)} async-done(((f32[32,512]{1,0:T(8,128)}), f32[32,256]{1,0:T(8,128)}) %reduce-scatter.3.cloned.1.call-update) | async-done | bytes 32784 | tf_op jit(solution)/shard_map/reduce_scatter | solution.py:85
  81.7 0.0 copy-done.1
  81.7 0.8 multiply_convert_fusion
  82.5 13.2 %all_gather.27 = bf16[32,1024]{1,0:T(8,128)(2,1)S(1)} all-gather(bf16[32,256]{1,0:T(8,128)(2,1)S(1)} %multiply_convert_fusion), channel_id=1, replica_groups=mesh['case'=2,'row'=4,'col'=2,'band'=2] {'row'}, dimensions={1}, use_global_device_ids=true | all-gather | bytes 81920 | tf_op jit(solution)/shard_map/all_gather | solution.py:62
  95.8 9.0 %while.21 = (s32[]{:T(128)}, f32[32,4,128]{2,0,1:T(8,128)S(1)}, s32[]{:T(128)}, s32[32]{0:T(128)S(1)}, s32[32]{0:T(128)S(1)}, /*index=5*/bf16[32,8,128]{2,0,1:T(...) while((s32[]{:T(128)}, f32[32,4,128]{2,0,1:T(8,128)S(1)}, ...), condition=%wide.region_16.17_spmd, body=%wide.region_11.16_spmd.sunk | while | flops 47974592 | bytes 16852452 | solution.py:82
  95.8 0.6 gather_fusion.3
  96.5 0.6 gather_fusion.4
  97.1 0.6 gather_fusion.5
  97.7 4.3 %fusion.62 = (f32[32,128,128]{2,1,0:T(8,128)S(1)}, f32[32,128,128]{2,1,0:T(8,128)S(1)}, f32[32,128,128]{2,1,0:T(8,128)S(1)}) fusion(f32[3,32,128]{2,1,0:T(8,128)S(1)} %copy.56, f32[3,32,128]{2,1,0:T(8,128)S(1)} %copy.57, f32[3,32,128]{2,1,0:T(8,128)S(1)} %copy.58, f32[3,32,128]{2,1,0:T(8,128)S(1)} %copy.59), kind=kLoop, calls=%fused_computation.35.clone.1 | loop fusion | flops 9437184 | bytes 6488064 | tf_op jit(solution)/shard_map/while/body/reduce_sum | solution.py:17
  102.1 0.8 convolution_multiply_fusion.5
  102.9 1.9 %scatter_fusion.1 = f32[32,4,128]{2,0,1:T(8,128)S(1)} fusion(f32[32,4,128]{2,0,1:T(8,128)S(1)} %get-tuple-element.394, s32[32]{0:T(128)S(1)} %get-tuple-element.344, f32[32,32,128]{2,1,0:T(8,128)S(1)} %convolution_multiply_fusion.5), kind=kCustom, calls=%fused_computation.9.clone.1 | custom fusion | flops 131072 | bytes 1572992 | tf_op jit(solution)/shard_map/while/body/scatter-add | solution.py:77
  104.8 0.6 copy_bitcast_fusion
  105.4 0.0 reduce-scatter.5.cloned.1.call-update
  105.4 9.9 %reduce-scatter.5.cloned.1.call-done = f32[32,256]{1,0:T(8,128)} async-done(((f32[32,512]{1,0:T(8,128)}), f32[32,256]{1,0:T(8,128)}) %reduce-scatter.5.cloned.1.call-update) | async-done | bytes 32784 | tf_op jit(solution)/shard_map/reduce_scatter | solution.py:85
  115.3 1.4 %multiply_add_fusion = f32[32,256]{1,0:T(8,128)} fusion(f32[32,256]{1,0:T(8,128)S(1)} %copy-done, f32[32,256]{1,0:T(8,128)S(1)} %copy-done.1, f32[32,256]{1,0:T(8,128)} %reduce-scatter.5.cloned.1.call-done), kind=kLoop, calls=%fused_computation.56 | loop fusion | flops 16384 | bytes 131072 | tf_op jit(solution)/shard_map/add | solution.py:88
  (39 shorter events, 0.3 us)
Async XLA Ops:
  6.5 24.2 %copy-start.3 = (f32[3,256]{1,0:T(4,128)S(1)}, f32[3,256]{1,0:T(4,128)}, u32[]{:S(2)}) copy-start(f32[3,256]{1,0:T(4,128)} %param.13) | copy-start | bytes 9220
  6.5 24.2 %copy-start.4 = (f32[3,256]{1,0:T(4,128)S(1)}, f32[3,256]{1,0:T(4,128)}, u32[]{:S(2)}) copy-start(f32[3,256]{1,0:T(4,128)} %param.12) | copy-start | bytes 9220
  6.5 44.0 %copy-start = (f32[32,256]{1,0:T(8,128)S(1)}, f32[32,256]{1,0:T(8,128)}, u32[]{:S(2)}) copy-start(f32[32,256]{1,0:T(8,128)} %param.15) | copy-start | bytes 98308
  6.5 44.0 %copy-start.2 = (f32[256]{0:T(256)S(1)}, f32[256]{0:T(256)}, u32[]{:S(2)}) copy-start(f32[256]{0:T(256)} %param.14) | copy-start | bytes 3076
  6.5 75.2 %reduce-scatter.3.cloned.1.call-start = ((), (), s32[]{:S(2)}) async-start(), calls=%async_computation.2 | async-start | bytes 98304 | tf_op jit(solution)/shard_map/reduce_scatter | solution.py:85
  63.8 18.0 %copy-start.1 = (f32[32,256]{1,0:T(8,128)S(1)}, f32[32,256]{1,0:T(8,128)}, u32[]{:S(2)}) copy-start(f32[32,256]{1,0:T(8,128)} %param.16) | copy-start | bytes 98308
  73.4 41.9 %reduce-scatter.5.cloned.1.call-start = ((), (), s32[]{:S(2)}) async-start(), calls=%async_computation.3 | async-start | bytes 98304 | tf_op jit(solution)/shard_map/reduce_scatter | solution.py:85
Sparse Core Ops, SparseCore 0:
  73.6 8.1 reduce-scatter.2
  105.5 9.7 reduce-scatter.4
where the time goes:
time: 124 us
  blocking collectives  56.8 us (46%)
  other arithmetic  21.6 us (17%)
  waiting for transfers between devices  18.2 us (15%)
  between operations  14.7 us (12%)
  local copies, waits for them, and re-layouts  10.3 us (8%)
  matrix products  1.58 us (1%)
    all_gather x2, blocking collectives, shards(): lax.all_gather(weighted, 'row', axis=1, tiled=True)  26.3 us
    reduce_scatter x2, waiting for transfers between devices, shards(): lax.psum_scatter(acc_rows.reshape(band_half, row_blocks * BLOCK), 'col',...  18.2 us
    all_gather x1, blocking collectives, shards(): lax.all_gather(geometry, 'row', axis=1, tiled=True)  13.1 us
    unnamed x1, blocking collectives  13.1 us
    reduce_sum x2, other arithmetic, form_tiles(): leaving = jnp.sum(near[3:6, :, :, None] * offset, axis=0)  8.64 us
    all_gather x1, blocking collectives, shards(): lax.all_gather(geometry, 'col', axis=1, tiled=True)  4.36 us
    unnamed x14, local copies, waits for them, and re-layouts  3.79 us
    scatter-add x2, other arithmetic, one_turn(): acc_rows = acc_rows.at[:, near_now].add(to_rows * live_now[None, :, None])  3.78 us
  transfers between devices with their start and end apart: 2, of which 2 were waited for; matrix products, arithmetic and copies ran while one was open for 0% of the time, Pallas kernels for 0%

commit v1 on v0

--- a/solution.py
+++ b/solution.py
@@ -1,8 +1,11 @@
+import functools
 import math
 
 import jax
 import jax.numpy as jnp
 from jax import lax
+from jax.experimental import pallas as pl
+from jax.experimental.pallas import tpu as pltpu
 from jax.sharding import PartitionSpec as P
 
 BLOCK = 128
@@ -10,6 +13,202 @@
 
 
 SOFTEN = 0.02
+
+PAD_ROWS = 16
+GEO_ROWS = 18
+
+
+def bit_reverse(value, bits):
+    out = value * 0
+    for bit in range(bits):
+        out = out | (((value >> bit) & 1) << (bits - 1 - bit))
+    return out
+
+
+def pack_kernel(col_bits, n_far, pos, nrm, area, emi, ref, prow, pcol, plive, out):
+    seg = (lax.axis_index("row") << col_bits) | lax.axis_index("col")
+    bands, width = emi.shape
+    a = area[...]
+    out[0:bands, :] = (a * emi[...]).astype(jnp.bfloat16)
+    out[bands : 2 * bands, :] = (a * ref[...]).astype(jnp.bfloat16)
+    geo = jnp.concatenate([pos[...], nrm[...]], axis=0)
+    high = geo.astype(jnp.bfloat16).astype(jnp.float32)
+    rest = geo - high
+    middle = rest.astype(jnp.bfloat16).astype(jnp.float32)
+    low = rest - middle
+    lane = lax.broadcasted_iota(jnp.int32, (1, width), 1)
+    col_mask = (1 << col_bits) - 1
+
+    def add_slot(i, flags):
+        p, q = prow[i], pcol[i]
+        near = ((((p >> 1) ^ seg) & col_mask) << 1) | (p & 1)
+        far = ((((q >> 1) ^ seg) >> col_bits) << 1) | (q & 1)
+        return flags + jnp.where(lane == near * n_far + far, plive[i], 0)
+
+    flags = lax.fori_loop(0, prow.shape[0], add_slot, jnp.zeros((1, width), jnp.int32), unroll=True)
+    tail = jnp.zeros((2 * PAD_ROWS - GEO_ROWS - 1, width), jnp.float32)
+    out[2 * bands : 2 * bands + 2 * PAD_ROWS, :] = jnp.concatenate(
+        [high, middle, low, flags.astype(jnp.float32), tail], axis=0
+    ).astype(jnp.bfloat16)
+
+
+def main_kernel(
+    n_seg, seg_bits, col_bits, n_far, emi, ref, low_half, high_half, out,
+    held, far_rep, near_col, tiles, sums, flag_vec, flag_sm, sems,
+):
+    bands, width = emi.shape
+    half = n_seg // 2
+    n_pairs = n_seg * (n_seg + 1) // 2
+    halves = width // BLOCK
+    first = pltpu.make_async_copy(low_half, held.at[0:half], sems.at[0])
+    second = pltpu.make_async_copy(high_half, held.at[half:n_seg], sems.at[1])
+    first.start()
+    second.start()
+    sums[...] = jnp.zeros_like(sums)
+    first.wait()
+    second.wait()
+    geo_at = 2 * bands
+    for k in range(n_seg):
+        piece = held[k, geo_at : geo_at + 2 * PAD_ROWS, :].astype(jnp.float32)
+        flag_vec[k : k + 1, :] = piece[GEO_ROWS : GEO_ROWS + 1, 0:BLOCK].astype(jnp.int32)
+    flag_copy = pltpu.make_async_copy(flag_vec, flag_sm, sems.at[2])
+    flag_copy.start()
+    for k in range(n_seg):
+        piece = held[k, geo_at : geo_at + 2 * PAD_ROWS, :].astype(jnp.float32)
+        geo = (piece[0:6] + piece[6:12]) + piece[12:18]
+        near_col[k, :, 0:8] = jnp.transpose(
+            jnp.concatenate([geo, jnp.zeros((2, width), jnp.float32)], axis=0)
+        )
+        for c in range(6):
+            row = geo[c : c + 1]
+            if c >= 3:
+                row = row * (-1.0 / math.pi)
+            far_rep[k, c] = jnp.broadcast_to(row, (8, width))
+    flag_copy.wait()
+    col_mask = (1 << col_bits) - 1
+
+    def pair_of(t):
+        t = jnp.int32(t)
+        shift = t // n_seg
+        near = t % n_seg
+        return near, (near + shift) % n_seg
+
+    def live(near_at, far_at, i, j):
+        near = bit_reverse(near_at, seg_bits)
+        far = bit_reverse(far_at, seg_bits)
+        holder = (near & ~col_mask) | (far & col_mask)
+        apart = near ^ far
+        index = ((((apart & col_mask) << 1) | i) * n_far) + (((apart >> col_bits) << 1) | j)
+        return flag_sm[bit_reverse(holder, seg_bits), index]
+
+    def form(t):
+        near_at, far_at = pair_of(t)
+        for j in range(halves):
+            cols = slice(j * BLOCK, (j + 1) * BLOCK)
+            fx, fy, fz = (far_rep[far_at, c, :, cols] for c in range(3))
+            bare = [far_rep[far_at, c, :, cols] for c in range(3, 6)]
+            for i in range(halves):
+                flag = live(near_at, far_at, i, j) | live(far_at, near_at, j, i)
+                gx, gy, gz = (v * flag.astype(jnp.float32) for v in bare)
+                for strip in range(BLOCK // 16):
+                    parts = []
+                    for part in range(2):
+                        at = i * BLOCK + strip * 16 + part * 8
+                        cols_now = near_col[near_at, at : at + 8, :]
+                        px, py, pz, nx, ny, nz = (
+                            jnp.broadcast_to(cols_now[:, c : c + 1], (8, BLOCK)) for c in range(6)
+                        )
+                        dx, dy, dz = fx - px, fy - py, fz - pz
+                        leaving = nx * dx + ny * dy + nz * dz
+                        arriving = gx * dx + gy * dy + gz * dz
+                        spacing = dx * dx + dy * dy + dz * dz + SOFTEN
+                        inverse = pl.reciprocal(spacing, approx=True)
+                        inverse = inverse * (2.0 - spacing * inverse)
+                        product = jnp.maximum(leaving, 0.0) * jnp.maximum(arriving, 0.0)
+                        parts.append(product * inverse * inverse)
+                    at = i * BLOCK + strip * 16
+                    tiles[t, at : at + 16, cols] = jnp.concatenate(parts, axis=0).astype(jnp.bfloat16)
+
+    def apply(t):
+        near_at, far_at = pair_of(t)
+        tile = tiles[t]
+        to_near = lax.dot_general(
+            held[far_at, 0:bands, :], tile, (((1,), (1,)), ((), ())), preferred_element_type=jnp.float32
+        )
+        to_far = lax.dot_general(
+            held[near_at, 0:bands, :], tile, (((1,), (0,)), ((), ())), preferred_element_type=jnp.float32
+        )
+        sums[near_at] = sums[near_at] + to_near
+        mirrored = (near_at != far_at).astype(jnp.float32)
+        sums[far_at] = sums[far_at] + to_far * mirrored
+
+    form(0)
+
+    def step(t, carry):
+        apply(t - 1)
+        form(t)
+        return carry
+
+    lax.fori_loop(1, n_pairs, step, 0)
+    apply(n_pairs - 1)
+    total = jnp.zeros((bands, width), jnp.float32)
+    for k in range(n_seg):
+        base = held[k, 0:bands, :].astype(jnp.float32)
+        gain = held[k, bands : 2 * bands, :].astype(jnp.float32)
+        weighted = (base + gain * sums[k]).astype(jnp.bfloat16)
+        if k <= half:
+            tile, over = tiles[k * n_seg], 1
+        else:
+            tile, over = tiles[(n_seg - k) * n_seg + k], 0
+        total += lax.dot_general(
+            weighted, tile, (((1,), (over,)), ((), ())), preferred_element_type=jnp.float32
+        )
+    out[...] = emi[...] + ref[...] * total
+
+
+def one_exchange(positions, normals, areas, emission, reflect, pair_row, pair_col, pair_live):
+    n_row = lax.axis_size("row")
+    n_col = lax.axis_size("col")
+    n_seg = n_row * n_col
+    seg_bits = n_seg.bit_length() - 1
+    col_bits = n_col.bit_length() - 1
+    bands, width = emission.shape
+    n_far = width // BLOCK * n_row
+    rows = 2 * bands + 2 * PAD_ROWS
+    vmem = pl.BlockSpec(memory_space=pltpu.VMEM)
+    smem = pl.BlockSpec(memory_space=pltpu.SMEM)
+    hbm = pl.BlockSpec(memory_space=pl.ANY)
+    packed = pl.pallas_call(
+        functools.partial(pack_kernel, col_bits, n_far),
+        out_shape=jax.ShapeDtypeStruct((rows, width), jnp.bfloat16),
+        in_specs=[vmem] * 5 + [smem] * 3,
+        out_specs=vmem,
+    )(positions, normals, areas.reshape(1, width), emission, reflect, pair_row, pair_col, pair_live)
+    gathered = packed[None]
+    for bit in reversed(range(seg_bits)):
+        arrived = lax.ppermute(
+            gathered, ("row", "col"), [(i, i ^ (1 << bit)) for i in range(n_seg)]
+        )
+        if bit:
+            gathered = jnp.concatenate([gathered, arrived])
+    n_pairs = n_seg * (n_seg + 1) // 2
+    return pl.pallas_call(
+        functools.partial(main_kernel, n_seg, seg_bits, col_bits, n_far),
+        out_shape=jax.ShapeDtypeStruct((bands, width), jnp.float32),
+        in_specs=[vmem, vmem, hbm, hbm],
+        out_specs=vmem,
+        scratch_shapes=[
+            pltpu.VMEM((n_seg, rows, width), jnp.bfloat16),
+            pltpu.VMEM((n_seg, 6, 8, width), jnp.float32),
+            pltpu.VMEM((n_seg, width, BLOCK), jnp.float32),
+            pltpu.VMEM((n_pairs, width, width), jnp.bfloat16),
+            pltpu.VMEM((n_seg, bands, width), jnp.float32),
+            pltpu.VMEM((n_seg, BLOCK), jnp.int32),
+            pltpu.SMEM((n_seg, BLOCK), jnp.int32),
+            pltpu.SemaphoreType.DMA((3,)),
+        ],
+        compiler_params=pltpu.CompilerParams(vmem_limit_bytes=40 * 1024 * 1024),
+    )(emission, reflect, gathered, arrived)
 
 
 def form_tiles(near, far):
@@ -20,7 +219,7 @@
     return jax.nn.relu(leaving) * jax.nn.relu(arriving) / (math.pi * spacing * spacing)
 
 
-def shards(positions, normals, areas, emission, reflect, pair_row, pair_col, pair_live):
+def two_exchanges(positions, normals, areas, emission, reflect, pair_row, pair_col, pair_live):
     patch_dev = areas.shape[0]
     own_blocks = patch_dev // BLOCK
     n_row = lax.axis_size("row")
@@ -89,6 +288,15 @@
     return radiosity
 
 
+def shards(positions, normals, areas, emission, reflect, pair_row, pair_col, pair_live):
+    n_row, n_col = lax.axis_size("row"), lax.axis_size("col")
+    n_seg = n_row * n_col
+    powers = n_row & (n_row - 1) == 0 and n_col & (n_col - 1) == 0
+    small = areas.shape[0] == 2 * BLOCK and 2 <= n_seg <= 16
+    plan = one_exchange if powers and small else two_exchanges
+    return plan(positions, normals, areas, emission, reflect, pair_row, pair_col, pair_live)
+
+
 def solution(mesh):
     return jax.shard_map(
         shards,

time: 124 us -> 49.6 us (0.40)
  blocking collectives: 56.8 us -> 0 us
  Pallas kernels: 0 us -> 31.2 us
  other arithmetic: 21.6 us -> 0.83 us
  between operations: 14.7 us -> 0.03 us
  local copies, waits for them, and re-layouts: 10.3 us -> 0.02 us
  waiting for transfers between devices: 18.2 us -> 10.2 us
  starting transfers between devices: 0.07 us -> 7.13 us
  matrix products: 1.58 us -> 0 us
    all_gather x4 -> x0, blocking collectives: 43.8 us -> none  [the longest x2 26.3 us: shards(): lax.all_gather(weighted, 'row', axis=1, tiled=True)]
    pallas_call x0 -> x2, Pallas kernels: none -> 31.2 us  [the longest x1 29.6 us: one_exchange(): pl.pallas_call(functools.partial(main_kernel, n_seg, seg_bits, col_bits,...]
    reduce_scatter x2 -> x0, waiting for transfers between devices: 18.2 us -> none  [shards(): lax.psum_scatter(acc_rows.reshape(band_half, row_blocks * BLOCK), 'col',...]
    unnamed x1 -> x0, blocking collectives: 13.1 us -> none
    ppermute x0 -> x3, waiting for transfers between devices: none -> 10.2 us  [one_exchange(): lax.ppermute(gathered, ('row', 'col'), [(i, i ^ 1 << bit) for i in range(...]
    reduce_sum x2 -> x0, other arithmetic: 8.64 us -> none  [form_tiles(): leaving = jnp.sum(near[3:6, :, :, None] * offset, axis=0)]
    ppermute x0 -> x3, starting transfers between devices: none -> 7.13 us  [one_exchange(): lax.ppermute(gathered, ('row', 'col'), [(i, i ^ 1 << bit) for i in range(...]
    gather x8 -> x0, local copies, waits for them, and re-layouts: 4.95 us -> none  [the longest x2 1.21 us: one_turn(): far_weights = w_cols[:, far_now]]
  transfers between devices with their start and end apart: 2 -> 3, of which waited for: 2 -> 3; matrix products, arithmetic and copies ran while one was open for 0% -> 0% of each run, Pallas kernels for 0% -> 0%
where the time goes in v1:
time: 49.6 us; the launch traced here: 49.4 us
  Pallas kernels  31.2 us (63%)
  waiting for transfers between devices  10.2 us (21%)
  starting transfers between devices  7.13 us (14%)
  other arithmetic  0.83 us (2%)
    pallas_call x1, Pallas kernels, one_exchange(): pl.pallas_call(functools.partial(main_kernel, n_seg, seg_bits, col_bits,...  29.6 us
    ppermute x3, waiting for transfers between devices, one_exchange(): lax.ppermute(gathered, ('row', 'col'), [(i, i ^ 1 << bit) for i in range(...  10.2 us
    ppermute x3, starting transfers between devices, one_exchange(): lax.ppermute(gathered, ('row', 'col'), [(i, i ^ 1 << bit) for i in range(...  7.13 us
    pallas_call x1, Pallas kernels, one_exchange(): pl.pallas_call(functools.partial(pack_kernel, col_bits, n_far), out_shape...  1.62 us
  transfers between devices with their start and end apart: 3, of which 3 were waited for; matrix products, arithmetic and copies ran while one was open for 0% of the time, Pallas kernels for 0%

profile of v1, /device:TPU:0, one launch (start us, length us, event | category | flops | bytes accessed | tf_op | source)
XLA Modules:
  0.0 49.4 jit_solution(7094126942781817832)
XLA Ops:
  0.0 1.6 %shard_map.82 = bf16[96,256]{1,0:T(8,128)(2,1)} custom-call(f32[3,256]{1,0:T(4,128)} %pos.1, f32[3,256]{1,0:T(4,128)} %nrm.1, f32[1,256]{1,0:T(1,128)} %bitcast.5, f32[32,256]{1,0:T(8,128)} %emi.3, f32[32,256]{1,0:T(8,128)} %ref.3, s32[32]{0:T(128)} %prow.1, s32[32]{0:T(128)} %pcol.1, s32[32]{0:T(128)} %plive.1), custom_call_target="tpu_custom_call" | custom-call | tf_op jit(solution)/shard_map/pallas_call | solution.py:181
  1.6 0.0 copy-start.2
  1.6 4.0 %collective-permute-start = (bf16[1,96,256]{2,1,0:T(8,128)(2,1)}, bf16[1,96,256]{2,1,0:T(8,128)(2,1)S(1)}, u32[]{:S(2)}, u32[]{:S(2)}) collective-permute-start(bf16[1,96,256]{2,1,0:T(8,128)(2,1)} %bitcast.2), channel_id=1, source_target_pairs={{0,8},{2,10},{4,12},{6,14},{8,0},{10,2},{12,4},{14,6},{1,9},{3,11}... | collective-permute-start | bytes 147464 | tf_op jit(solution)/shard_map/ppermute | solution.py:189
  5.7 2.9 %collective-permute-done = bf16[1,96,256]{2,1,0:T(8,128)(2,1)S(1)} collective-permute-done((bf16[1,96,256]{2,1,0:T(8,128)(2,1)}, bf16[1,96,256]{2,1,0:T(8,128)(2,1)S(1)}, u32[]{:S(2)}, u32[]{:S(2)}) %collective-permute-start) | collective-permute-done | bytes 49184 | tf_op jit(solution)/shard_map/ppermute | solution.py:189
  8.5 0.8 %pad_maximum_fusion.1 = bf16[2,96,256]{2,1,0:T(8,128)(2,1)S(1)} fusion(bf16[1,96,256]{2,1,0:T(8,128)(2,1)S(1)} %collective-permute-done, bf16[1,96,256]{2,1,0:T(8,128)(2,1)} %bitcast.3), kind=kLoop, calls=%fused_computation.1 | loop fusion | flops 49152 | bytes 196608 | tf_op jit(solution)/shard_map/concatenate | solution.py:193
  9.3 0.0 copy-start
  9.4 0.0 copy-start.1
  9.4 1.4 %collective-permute-start.1 = (bf16[2,96,256]{2,1,0:T(8,128)(2,1)S(1)}, bf16[2,96,256]{2,1,0:T(8,128)(2,1)S(1)}, u32[]{:S(2)}, u32[]{:S(2)}) collective-permute-start(bf16[2,96,256]{2,1,0:T(8,128)(2,1)S(1)} %pad_maximum_fusion.1), channel_id=1, source_target_pairs={{0,4},{2,6},{4,0},{6,2},{8,12},{10,14},{12,8},{14,10},{1,5},{3,7},... | collective-permute-start | bytes 294920 | tf_op jit(solution)/shard_map/ppermute | solution.py:189
  10.7 3.3 %collective-permute-done.1 = bf16[2,96,256]{2,1,0:T(8,128)(2,1)S(1)} collective-permute-done((bf16[2,96,256]{2,1,0:T(8,128)(2,1)S(1)}, bf16[2,96,256]{2,1,0:T(8,128)(2,1)S(1)}, u32[]{:S(2)}, u32[]{:S(2)}) %collective-permute-start.1) | collective-permute-done | bytes 98336 | tf_op jit(solution)/shard_map/ppermute | solution.py:189
  14.1 0.0 copy-done.2
  14.1 1.7 %collective-permute-start.2 = (bf16[4,96,256]{2,1,0:T(8,128)(2,1)S(1)}, bf16[4,96,256]{2,1,0:T(8,128)(2,1)S(1)}, u32[]{:S(2)}, u32[]{:S(2)}) collective-permute-start(bf16[4,96,256]{2,1,0:T(8,128)(2,1)S(1)} %pad_maximum_fusion.low_half), channel_id=1, source_target_pairs={{0,2},{2,0},{4,6},{6,4},{8,10},{10,8},{12,14},{14,12},{1,3},{3,1},... | collective-permute-start | bytes 589832 | tf_op jit(solution)/shard_map/ppermute | solution.py:189
  15.8 4.0 %collective-permute-done.2.high_half = bf16[4,96,256]{2,1,0:T(8,128)(2,1)S(1)} collective-permute-done((bf16[4,96,256]{2,1,0:T(8,128)(2,1)S(1)}, bf16[4,96,256]{2,1,0:T(8,128)(2,1)S(1)}, u32[]{:S(2)}, u32[]{:S(2)}) %collective-permute-start.2) | collective-permute-done | bytes 196640 | tf_op jit(solution)/shard_map/ppermute | solution.py:189
  19.8 0.0 copy-done
  19.8 0.0 copy-done.1
  19.8 29.6 %shard_map.83 = f32[32,256]{1,0:T(8,128)} custom-call(f32[32,256]{1,0:T(8,128)S(1)} %copy-done, f32[32,256]{1,0:T(8,128)S(1)} %copy-done.1, bf16[4,96,256]{2,1,0:T(8,128)(2,1)S(1)} %pad_maximum_fusion.low_half, bf16[4,96,256]{2,1,0:T(8,128)(2,1)S(1)} %collective-permute-done.2.high_half), custom_call_target="tpu_custom_call" | custom-call | tf_op jit(solution)/shard_map/pallas_call | solution.py:195
  (1 shorter events, 0.0 us)
Async XLA Ops:
  1.6 12.4 %copy-start.2 = (bf16[96,256]{1,0:T(8,128)(2,1)S(1)}, bf16[96,256]{1,0:T(8,128)(2,1)}, u32[]{:S(2)}) copy-start(bf16[96,256]{1,0:T(8,128)(2,1)} %shard_map.82) | copy-start | bytes 147460
  1.6 6.9 %collective-permute-start = (bf16[1,96,256]{2,1,0:T(8,128)(2,1)}, bf16[1,96,256]{2,1,0:T(8,128)(2,1)S(1)}, u32[]{:S(2)}, u32[]{:S(2)}) collective-permute-start(bf16[1,96,256]{2,1,0:T(8,128)(2,1)} %bitcast.2), channel_id=1, source_target_pairs={{0,8},{2,10},{4,12},{6,14},{8,0},{10,2},{12,4},{14,6},{1,9},{3,11}... | collective-permute-start | bytes 147464 | tf_op jit(solution)/shard_map/ppermute | solution.py:189
  9.3 10.5 %copy-start = (f32[32,256]{1,0:T(8,128)S(1)}, f32[32,256]{1,0:T(8,128)}, u32[]{:S(2)}) copy-start(f32[32,256]{1,0:T(8,128)} %emi.3) | copy-start | bytes 98308
  9.4 10.5 %copy-start.1 = (f32[32,256]{1,0:T(8,128)S(1)}, f32[32,256]{1,0:T(8,128)}, u32[]{:S(2)}) copy-start(f32[32,256]{1,0:T(8,128)} %ref.3) | copy-start | bytes 98308
  9.4 4.7 %collective-permute-start.1 = (bf16[2,96,256]{2,1,0:T(8,128)(2,1)S(1)}, bf16[2,96,256]{2,1,0:T(8,128)(2,1)S(1)}, u32[]{:S(2)}, u32[]{:S(2)}) collective-permute-start(bf16[2,96,256]{2,1,0:T(8,128)(2,1)S(1)} %pad_maximum_fusion.1), channel_id=1, source_target_pairs={{0,4},{2,6},{4,0},{6,2},{8,12},{10,14},{12,8},{14,10},{1,5},{3,7},... | collective-permute-start | bytes 294920 | tf_op jit(solution)/shard_map/ppermute | solution.py:189
  14.1 5.7 %collective-permute-start.2 = (bf16[4,96,256]{2,1,0:T(8,128)(2,1)S(1)}, bf16[4,96,256]{2,1,0:T(8,128)(2,1)S(1)}, u32[]{:S(2)}, u32[]{:S(2)}) collective-permute-start(bf16[4,96,256]{2,1,0:T(8,128)(2,1)S(1)} %pad_maximum_fusion.low_half), channel_id=1, source_target_pairs={{0,2},{2,0},{4,6},{6,4},{8,10},{10,8},{12,14},{14,12},{1,3},{3,1},... | collective-permute-start | bytes 589832 | tf_op jit(solution)/shard_map/ppermute | solution.py:189

commit v2 on v1

--- a/solution.py
+++ b/solution.py
@@ -14,8 +14,8 @@
 
 SOFTEN = 0.02
 
-PAD_ROWS = 16
-GEO_ROWS = 18
+GEO_ROWS = 32
+FLAG_ROW = 6
 
 
 def bit_reverse(value, bits):
@@ -23,6 +23,13 @@
     for bit in range(bits):
         out = out | (((value >> bit) & 1) << (bits - 1 - bit))
     return out
+
+
+def three_pieces(x):
+    high = x.astype(jnp.bfloat16).astype(jnp.float32)
+    rest = x - high
+    middle = rest.astype(jnp.bfloat16).astype(jnp.float32)
+    return high, middle, rest - middle
 
 
 def pack_kernel(col_bits, n_far, pos, nrm, area, emi, ref, prow, pcol, plive, out):
@@ -31,11 +38,6 @@
     a = area[...]
     out[0:bands, :] = (a * emi[...]).astype(jnp.bfloat16)
     out[bands : 2 * bands, :] = (a * ref[...]).astype(jnp.bfloat16)
-    geo = jnp.concatenate([pos[...], nrm[...]], axis=0)
-    high = geo.astype(jnp.bfloat16).astype(jnp.float32)
-    rest = geo - high
-    middle = rest.astype(jnp.bfloat16).astype(jnp.float32)
-    low = rest - middle
     lane = lax.broadcasted_iota(jnp.int32, (1, width), 1)
     col_mask = (1 << col_bits) - 1
 
@@ -46,15 +48,28 @@
         return flags + jnp.where(lane == near * n_far + far, plive[i], 0)
 
     flags = lax.fori_loop(0, prow.shape[0], add_slot, jnp.zeros((1, width), jnp.int32), unroll=True)
-    tail = jnp.zeros((2 * PAD_ROWS - GEO_ROWS - 1, width), jnp.float32)
-    out[2 * bands : 2 * bands + 2 * PAD_ROWS, :] = jnp.concatenate(
-        [high, middle, low, flags.astype(jnp.float32), tail], axis=0
+    geo = jnp.concatenate(
+        [pos[...], nrm[...], flags.astype(jnp.float32), jnp.zeros((1, width), jnp.float32)], axis=0
+    )
+    out[2 * bands : 2 * bands + GEO_ROWS, :] = jnp.concatenate(
+        [*three_pieces(geo), jnp.zeros((8, width), jnp.float32)], axis=0
     ).astype(jnp.bfloat16)
+
+
+def near_stack(x):
+    high, middle, low = three_pieces(x)
+    return jnp.concatenate([high, high, middle, high, low, middle], axis=0)
+
+
+def far_stack(x):
+    high, middle, low = three_pieces(x)
+    return jnp.concatenate([high, middle, high, low, high, middle], axis=0).astype(jnp.bfloat16)
 
 
 def main_kernel(
     n_seg, seg_bits, col_bits, n_far, emi, ref, low_half, high_half, out,
-    held, far_rep, near_col, tiles, sums, flag_vec, flag_sm, sems,
+    held, geo_all, centre, far_rep, near_pos, near_rep, near_leave, near_arrive, leave_even,
+    arrive_even, leave_odd, arrive_odd, tiles, sums, flag_vec, flag_sm, sems,
 ):
     bands, width = emi.shape
     half = n_seg // 2
@@ -65,25 +80,30 @@
     first.start()
     second.start()
     sums[...] = jnp.zeros_like(sums)
+    tiles[n_pairs] = jnp.zeros((width, width), jnp.bfloat16)
     first.wait()
     second.wait()
     geo_at = 2 * bands
     for k in range(n_seg):
-        piece = held[k, geo_at : geo_at + 2 * PAD_ROWS, :].astype(jnp.float32)
-        flag_vec[k : k + 1, :] = piece[GEO_ROWS : GEO_ROWS + 1, 0:BLOCK].astype(jnp.int32)
+        piece = held[k, geo_at : geo_at + GEO_ROWS, :].astype(jnp.float32)
+        geo = (piece[0:8] + piece[8:16]) + piece[16:24]
+        geo_all[k] = geo
+        flag_vec[k : k + 1, :] = geo[FLAG_ROW : FLAG_ROW + 1, 0:BLOCK].astype(jnp.int32)
     flag_copy = pltpu.make_async_copy(flag_vec, flag_sm, sems.at[2])
     flag_copy.start()
+    row = lax.broadcasted_iota(jnp.int32, (8, width), 0)
     for k in range(n_seg):
-        piece = held[k, geo_at : geo_at + 2 * PAD_ROWS, :].astype(jnp.float32)
-        geo = (piece[0:6] + piece[6:12]) + piece[12:18]
-        near_col[k, :, 0:8] = jnp.transpose(
-            jnp.concatenate([geo, jnp.zeros((2, width), jnp.float32)], axis=0)
-        )
-        for c in range(6):
-            row = geo[c : c + 1]
-            if c >= 3:
-                row = row * (-1.0 / math.pi)
-            far_rep[k, c] = jnp.broadcast_to(row, (8, width))
+        geo = geo_all[k]
+        for c in range(3):
+            far_rep[k, c] = jnp.broadcast_to(geo[c : c + 1], (8, width))
+        near_pos[k, :, 0:8] = jnp.transpose(geo)
+        middle = jnp.broadcast_to(geo[:, 0:1], (8, width))
+        centre[k] = middle
+        offset = jnp.where(row < 3, geo - middle, 0.0)
+        normal = jnp.where(row < 3, pltpu.roll(geo, 5, 0), 0.0)
+        along = jnp.sum(normal * offset, axis=0, keepdims=True)
+        near_leave[k] = jnp.transpose(near_stack(jnp.where(row == 3, -along, normal))).astype(jnp.bfloat16)
+        near_arrive[k] = jnp.transpose(near_stack(jnp.where(row == 3, 1.0, -offset))).astype(jnp.bfloat16)
     flag_copy.wait()
     col_mask = (1 << col_bits) - 1
 
@@ -101,33 +121,61 @@
         index = ((((apart & col_mask) << 1) | i) * n_far) + (((apart >> col_bits) << 1) | j)
         return flag_sm[bit_reverse(holder, seg_bits), index]
 
-    def form(t):
+    def project(t, leave, arrive):
         near_at, far_at = pair_of(t)
-        for j in range(halves):
-            cols = slice(j * BLOCK, (j + 1) * BLOCK)
-            fx, fy, fz = (far_rep[far_at, c, :, cols] for c in range(3))
-            bare = [far_rep[far_at, c, :, cols] for c in range(3, 6)]
-            for i in range(halves):
-                flag = live(near_at, far_at, i, j) | live(far_at, near_at, j, i)
-                gx, gy, gz = (v * flag.astype(jnp.float32) for v in bare)
-                for strip in range(BLOCK // 16):
-                    parts = []
-                    for part in range(2):
-                        at = i * BLOCK + strip * 16 + part * 8
-                        cols_now = near_col[near_at, at : at + 8, :]
-                        px, py, pz, nx, ny, nz = (
-                            jnp.broadcast_to(cols_now[:, c : c + 1], (8, BLOCK)) for c in range(6)
-                        )
-                        dx, dy, dz = fx - px, fy - py, fz - pz
-                        leaving = nx * dx + ny * dy + nz * dz
-                        arriving = gx * dx + gy * dy + gz * dz
-                        spacing = dx * dx + dy * dy + dz * dz + SOFTEN
-                        inverse = pl.reciprocal(spacing, approx=True)
-                        inverse = inverse * (2.0 - spacing * inverse)
-                        product = jnp.maximum(leaving, 0.0) * jnp.maximum(arriving, 0.0)
-                        parts.append(product * inverse * inverse)
-                    at = i * BLOCK + strip * 16
-                    tiles[t, at : at + 16, cols] = jnp.concatenate(parts, axis=0).astype(jnp.bfloat16)
+        geo = geo_all[far_at]
+        offset = jnp.where(row < 3, geo - centre[near_at], 0.0)
+        normal = jnp.where(row < 3, pltpu.roll(geo, 5, 0), 0.0) * (-1.0 / math.pi)
+        along = jnp.sum(normal * offset, axis=0, keepdims=True)
+        leave[...] = jnp.dot(
+            near_leave[near_at], far_stack(jnp.where(row == 3, 1.0, offset)),
+            preferred_element_type=jnp.float32,
+        )
+        arrive[...] = jnp.dot(
+            near_arrive[near_at], far_stack(jnp.where(row == 3, along, normal)),
+            preferred_element_type=jnp.float32,
+        )
+
+    def form(t, leave, arrive, fresh):
+        near_at, far_at = pair_of(t)
+        flags = [
+            [
+                (live(near_at, far_at, i, j) | live(far_at, near_at, j, i)).astype(jnp.float32)
+                for j in range(halves)
+            ]
+            for i in range(halves)
+        ]
+        fars = [
+            [far_rep[far_at, c, :, j * BLOCK : (j + 1) * BLOCK] for c in range(3)]
+            for j in range(halves)
+        ]
+        for strip in range(width // 16):
+            i = strip * 16 // BLOCK
+            nears = []
+            for part in range(2):
+                at = strip * 16 + part * 8
+                if fresh:
+                    cols_now = near_pos[near_at, at : at + 8, :]
+                    now = [jnp.broadcast_to(cols_now[:, c : c + 1], (8, BLOCK)) for c in range(3)]
+                    for c in range(3):
+                        near_rep[near_at, c, at : at + 8, :] = now[c]
+                else:
+                    now = [near_rep[near_at, c, at : at + 8, :] for c in range(3)]
+                nears.append(now)
+            for j in range(halves):
+                cols = slice(j * BLOCK, (j + 1) * BLOCK)
+                parts = []
+                for part in range(2):
+                    at = strip * 16 + part * 8
+                    dx, dy, dz = (f - n for f, n in zip(fars[j], nears[part]))
+                    spacing = dx * dx + dy * dy + dz * dz + SOFTEN
+                    inverse = 1.0 / spacing
+                    product = jnp.maximum(leave[at : at + 8, cols], 0.0) * jnp.maximum(
+                        arrive[at : at + 8, cols], 0.0
+                    )
+                    parts.append(product * inverse * inverse)
+                strip_now = jnp.concatenate(parts, axis=0).astype(jnp.bfloat16)
+                tiles[t, strip * 16 : strip * 16 + 16, cols] = strip_now * flags[i][j].astype(jnp.bfloat16)
 
     def apply(t):
         near_at, far_at = pair_of(t)
@@ -142,14 +190,18 @@
         mirrored = (near_at != far_at).astype(jnp.float32)
         sums[far_at] = sums[far_at] + to_far * mirrored
 
-    form(0)
-
-    def step(t, carry):
-        apply(t - 1)
-        form(t)
+    def two_steps(fresh, i, carry):
+        for part, (now, later) in enumerate(((even, odd), (odd, even))):
+            t = 2 * i + part
+            apply(jnp.where(t == 0, n_pairs, t - 1))
+            project(t + 1, *later)
+            form(t, *now, fresh)
         return carry
 
-    lax.fori_loop(1, n_pairs, step, 0)
+    even, odd = (leave_even, arrive_even), (leave_odd, arrive_odd)
+    project(0, *even)
+    lax.fori_loop(0, n_seg // 2, functools.partial(two_steps, True), 0)
+    lax.fori_loop(n_seg // 2, n_pairs // 2, functools.partial(two_steps, False), 0)
     apply(n_pairs - 1)
     total = jnp.zeros((bands, width), jnp.float32)
     for k in range(n_seg):
@@ -166,6 +218,26 @@
     out[...] = emi[...] + ref[...] * total
 
 
+def main_scratch(n_seg, rows, bands, width):
+    n_pairs = n_seg * (n_seg + 1) // 2
+    return [
+        pltpu.VMEM((n_seg, rows, width), jnp.bfloat16),
+        pltpu.VMEM((n_seg, 8, width), jnp.float32),
+        pltpu.VMEM((n_seg, 8, width), jnp.float32),
+        pltpu.VMEM((n_seg, 3, 8, width), jnp.float32),
+        pltpu.VMEM((n_seg, width, BLOCK), jnp.float32),
+        pltpu.VMEM((n_seg, 3, width, BLOCK), jnp.float32),
+        pltpu.VMEM((n_seg, width, 48), jnp.bfloat16),
+        pltpu.VMEM((n_seg, width, 48), jnp.bfloat16),
+        *[pltpu.VMEM((width, width), jnp.float32)] * 4,
+        pltpu.VMEM((n_pairs + 1, width, width), jnp.bfloat16),
+        pltpu.VMEM((n_seg, bands, width), jnp.float32),
+        pltpu.VMEM((n_seg, BLOCK), jnp.int32),
+        pltpu.SMEM((n_seg, BLOCK), jnp.int32),
+        pltpu.SemaphoreType.DMA((3,)),
+    ]
+
+
 def one_exchange(positions, normals, areas, emission, reflect, pair_row, pair_col, pair_live):
     n_row = lax.axis_size("row")
     n_col = lax.axis_size("col")
@@ -174,7 +246,7 @@
     col_bits = n_col.bit_length() - 1
     bands, width = emission.shape
     n_far = width // BLOCK * n_row
-    rows = 2 * bands + 2 * PAD_ROWS
+    rows = 2 * bands + GEO_ROWS
     vmem = pl.BlockSpec(memory_space=pltpu.VMEM)
     smem = pl.BlockSpec(memory_space=pltpu.SMEM)
     hbm = pl.BlockSpec(memory_space=pl.ANY)
@@ -191,22 +263,12 @@
         )
         if bit:
             gathered = jnp.concatenate([gathered, arrived])
-    n_pairs = n_seg * (n_seg + 1) // 2
     return pl.pallas_call(
         functools.partial(main_kernel, n_seg, seg_bits, col_bits, n_far),
         out_shape=jax.ShapeDtypeStruct((bands, width), jnp.float32),
         in_specs=[vmem, vmem, hbm, hbm],
         out_specs=vmem,
-        scratch_shapes=[
-            pltpu.VMEM((n_seg, rows, width), jnp.bfloat16),
-            pltpu.VMEM((n_seg, 6, 8, width), jnp.float32),
-            pltpu.VMEM((n_seg, width, BLOCK), jnp.float32),
-            pltpu.VMEM((n_pairs, width, width), jnp.bfloat16),
-            pltpu.VMEM((n_seg, bands, width), jnp.float32),
-            pltpu.VMEM((n_seg, BLOCK), jnp.int32),
-            pltpu.SMEM((n_seg, BLOCK), jnp.int32),
-            pltpu.SemaphoreType.DMA((3,)),
-        ],
+        scratch_shapes=main_scratch(n_seg, rows, bands, width),
         compiler_params=pltpu.CompilerParams(vmem_limit_bytes=40 * 1024 * 1024),
     )(emission, reflect, gathered, arrived)
 
@@ -292,7 +354,7 @@
     n_row, n_col = lax.axis_size("row"), lax.axis_size("col")
     n_seg = n_row * n_col
     powers = n_row & (n_row - 1) == 0 and n_col & (n_col - 1) == 0
-    small = areas.shape[0] == 2 * BLOCK and 2 <= n_seg <= 16
+    small = areas.shape[0] == 2 * BLOCK and 4 <= n_seg <= 16
     plan = one_exchange if powers and small else two_exchanges
     return plan(positions, normals, areas, emission, reflect, pair_row, pair_col, pair_live)
 

time: 49.6 us -> 32.4 us (0.65)
  Pallas kernels: 31.2 us -> 13.9 us
    pallas_call x1, Pallas kernels: 29.6 us -> 12.3 us  [one_exchange(): pl.pallas_call(functools.partial(main_kernel, n_seg, seg_bits, col_bits,...]
where the time goes in v2:
time: 32.4 us; the launch traced here: 32.1 us
  Pallas kernels  13.9 us (43%)
  waiting for transfers between devices  10.2 us (31%)
  starting transfers between devices  7.13 us (22%)
  other arithmetic  0.83 us (3%)
    pallas_call x1, Pallas kernels, one_exchange(): pl.pallas_call(functools.partial(main_kernel, n_seg, seg_bits, col_bits,...  12.3 us
    ppermute x3, waiting for transfers between devices, one_exchange(): lax.ppermute(gathered, ('row', 'col'), [(i, i ^ 1 << bit) for i in range(...  10.2 us
    ppermute x3, starting transfers between devices, one_exchange(): lax.ppermute(gathered, ('row', 'col'), [(i, i ^ 1 << bit) for i in range(...  7.13 us
    pallas_call x1, Pallas kernels, one_exchange(): pl.pallas_call(functools.partial(pack_kernel, col_bits, n_far), out_shape...  1.63 us
    concatenate x2, other arithmetic, one_exchange(): gathered = jnp.concatenate([gathered, arrived])  0.83 us
  transfers between devices with their start and end apart: 3, of which 3 were waited for; matrix products, arithmetic and copies ran while one was open for 0% of the time, Pallas kernels for 0%

profile of v2, /device:TPU:0, one launch (start us, length us, event | category | flops | bytes accessed | tf_op | source)
XLA Modules:
  0.0 32.1 jit_solution(7424184794396478927)
XLA Ops:
  0.0 1.6 %shard_map.82 = bf16[96,256]{1,0:T(8,128)(2,1)} custom-call(f32[3,256]{1,0:T(4,128)} %pos.1, f32[3,256]{1,0:T(4,128)} %nrm.1, f32[1,256]{1,0:T(1,128)} %bitcast.5, f32[32,256]{1,0:T(8,128)} %emi.3, f32[32,256]{1,0:T(8,128)} %ref.3, s32[32]{0:T(128)} %prow.1, s32[32]{0:T(128)} %pcol.1, s32[32]{0:T(128)} %plive.1), custom_call_target="tpu_custom_call" | custom-call | tf_op jit(solution)/shard_map/pallas_call | solution.py:253
  1.6 0.0 copy-start.2
  1.6 4.0 %collective-permute-start = (bf16[1,96,256]{2,1,0:T(8,128)(2,1)}, bf16[1,96,256]{2,1,0:T(8,128)(2,1)S(1)}, u32[]{:S(2)}, u32[]{:S(2)}) collective-permute-start(bf16[1,96,256]{2,1,0:T(8,128)(2,1)} %bitcast.2), channel_id=1, source_target_pairs={{0,8},{2,10},{4,12},{6,14},{8,0},{10,2},{12,4},{14,6},{1,9},{3,11}... | collective-permute-start | bytes 147464 | tf_op jit(solution)/shard_map/ppermute | solution.py:261
  5.7 2.9 %collective-permute-done = bf16[1,96,256]{2,1,0:T(8,128)(2,1)S(1)} collective-permute-done((bf16[1,96,256]{2,1,0:T(8,128)(2,1)}, bf16[1,96,256]{2,1,0:T(8,128)(2,1)S(1)}, u32[]{:S(2)}, u32[]{:S(2)}) %collective-permute-start) | collective-permute-done | bytes 49184 | tf_op jit(solution)/shard_map/ppermute | solution.py:261
  8.5 0.8 %pad_maximum_fusion.1 = bf16[2,96,256]{2,1,0:T(8,128)(2,1)S(1)} fusion(bf16[1,96,256]{2,1,0:T(8,128)(2,1)S(1)} %collective-permute-done, bf16[1,96,256]{2,1,0:T(8,128)(2,1)} %bitcast.3), kind=kLoop, calls=%fused_computation.1 | loop fusion | flops 49152 | bytes 196608 | tf_op jit(solution)/shard_map/concatenate | solution.py:265
  9.4 0.0 copy-start
  9.4 0.0 copy-start.1
  9.4 1.4 %collective-permute-start.1 = (bf16[2,96,256]{2,1,0:T(8,128)(2,1)S(1)}, bf16[2,96,256]{2,1,0:T(8,128)(2,1)S(1)}, u32[]{:S(2)}, u32[]{:S(2)}) collective-permute-start(bf16[2,96,256]{2,1,0:T(8,128)(2,1)S(1)} %pad_maximum_fusion.1), channel_id=1, source_target_pairs={{0,4},{2,6},{4,0},{6,2},{8,12},{10,14},{12,8},{14,10},{1,5},{3,7},... | collective-permute-start | bytes 294920 | tf_op jit(solution)/shard_map/ppermute | solution.py:261
  10.8 3.3 %collective-permute-done.1 = bf16[2,96,256]{2,1,0:T(8,128)(2,1)S(1)} collective-permute-done((bf16[2,96,256]{2,1,0:T(8,128)(2,1)S(1)}, bf16[2,96,256]{2,1,0:T(8,128)(2,1)S(1)}, u32[]{:S(2)}, u32[]{:S(2)}) %collective-permute-start.1) | collective-permute-done | bytes 98336 | tf_op jit(solution)/shard_map/ppermute | solution.py:261
  14.1 0.0 copy-done.2
  14.1 1.7 %collective-permute-start.2 = (bf16[4,96,256]{2,1,0:T(8,128)(2,1)S(1)}, bf16[4,96,256]{2,1,0:T(8,128)(2,1)S(1)}, u32[]{:S(2)}, u32[]{:S(2)}) collective-permute-start(bf16[4,96,256]{2,1,0:T(8,128)(2,1)S(1)} %pad_maximum_fusion.low_half), channel_id=1, source_target_pairs={{0,2},{2,0},{4,6},{6,4},{8,10},{10,8},{12,14},{14,12},{1,3},{3,1},... | collective-permute-start | bytes 589832 | tf_op jit(solution)/shard_map/ppermute | solution.py:261
  15.8 4.0 %collective-permute-done.2.high_half = bf16[4,96,256]{2,1,0:T(8,128)(2,1)S(1)} collective-permute-done((bf16[4,96,256]{2,1,0:T(8,128)(2,1)S(1)}, bf16[4,96,256]{2,1,0:T(8,128)(2,1)S(1)}, u32[]{:S(2)}, u32[]{:S(2)}) %collective-permute-start.2) | collective-permute-done | bytes 196640 | tf_op jit(solution)/shard_map/ppermute | solution.py:261
  19.8 0.0 copy-done
  19.8 0.0 copy-done.1
  19.8 12.3 %shard_map.83 = f32[32,256]{1,0:T(8,128)} custom-call(f32[32,256]{1,0:T(8,128)S(1)} %copy-done, f32[32,256]{1,0:T(8,128)S(1)} %copy-done.1, bf16[4,96,256]{2,1,0:T(8,128)(2,1)S(1)} %pad_maximum_fusion.low_half, bf16[4,96,256]{2,1,0:T(8,128)(2,1)S(1)} %collective-permute-done.2.high_half), custom_call_target="tpu_custom_call" | custom-call | tf_op jit(solution)/shard_map/pallas_call | solution.py:266
  (1 shorter events, 0.0 us)
Async XLA Ops:
  1.6 12.4 %copy-start.2 = (bf16[96,256]{1,0:T(8,128)(2,1)S(1)}, bf16[96,256]{1,0:T(8,128)(2,1)}, u32[]{:S(2)}) copy-start(bf16[96,256]{1,0:T(8,128)(2,1)} %shard_map.82) | copy-start | bytes 147460
  1.6 6.9 %collective-permute-start = (bf16[1,96,256]{2,1,0:T(8,128)(2,1)}, bf16[1,96,256]{2,1,0:T(8,128)(2,1)S(1)}, u32[]{:S(2)}, u32[]{:S(2)}) collective-permute-start(bf16[1,96,256]{2,1,0:T(8,128)(2,1)} %bitcast.2), channel_id=1, source_target_pairs={{0,8},{2,10},{4,12},{6,14},{8,0},{10,2},{12,4},{14,6},{1,9},{3,11}... | collective-permute-start | bytes 147464 | tf_op jit(solution)/shard_map/ppermute | solution.py:261
  9.4 10.5 %copy-start = (f32[32,256]{1,0:T(8,128)S(1)}, f32[32,256]{1,0:T(8,128)}, u32[]{:S(2)}) copy-start(f32[32,256]{1,0:T(8,128)} %emi.3) | copy-start | bytes 98308
  9.4 10.5 %copy-start.1 = (f32[32,256]{1,0:T(8,128)S(1)}, f32[32,256]{1,0:T(8,128)}, u32[]{:S(2)}) copy-start(f32[32,256]{1,0:T(8,128)} %ref.3) | copy-start | bytes 98308
  9.4 4.7 %collective-permute-start.1 = (bf16[2,96,256]{2,1,0:T(8,128)(2,1)S(1)}, bf16[2,96,256]{2,1,0:T(8,128)(2,1)S(1)}, u32[]{:S(2)}, u32[]{:S(2)}) collective-permute-start(bf16[2,96,256]{2,1,0:T(8,128)(2,1)S(1)} %pad_maximum_fusion.1), channel_id=1, source_target_pairs={{0,4},{2,6},{4,0},{6,2},{8,12},{10,14},{12,8},{14,10},{1,5},{3,7},... | collective-permute-start | bytes 294920 | tf_op jit(solution)/shard_map/ppermute | solution.py:261
  14.1 5.7 %collective-permute-start.2 = (bf16[4,96,256]{2,1,0:T(8,128)(2,1)S(1)}, bf16[4,96,256]{2,1,0:T(8,128)(2,1)S(1)}, u32[]{:S(2)}, u32[]{:S(2)}) collective-permute-start(bf16[4,96,256]{2,1,0:T(8,128)(2,1)S(1)} %pad_maximum_fusion.low_half), channel_id=1, source_target_pairs={{0,2},{2,0},{4,6},{6,4},{8,10},{10,8},{12,14},{14,12},{1,3},{3,1},... | collective-permute-start | bytes 589832 | tf_op jit(solution)/shard_map/ppermute | solution.py:261

commit v3 on v2

--- a/solution.py
+++ b/solution.py
@@ -66,78 +66,95 @@
     return jnp.concatenate([high, middle, high, low, high, middle], axis=0).astype(jnp.bfloat16)
 
 
-def main_kernel(
-    n_seg, seg_bits, col_bits, n_far, emi, ref, low_half, high_half, out,
-    held, geo_all, centre, far_rep, near_pos, near_rep, near_leave, near_arrive, leave_even,
-    arrive_even, leave_odd, arrive_odd, tiles, sums, flag_vec, flag_sm, sems,
-):
-    bands, width = emi.shape
-    half = n_seg // 2
-    n_pairs = n_seg * (n_seg + 1) // 2
+def triangle(count):
+    return count * (count + 1) // 2
+
+
+def own_tile(k, count):
+    if k <= count // 2:
+        return k * count, 1
+    return (count - k) * count + k, 0
+
+
+def grow_kernel(n_old, n_new, bits, seg_bits, col_bits, n_far, last, *refs):
+    if last:
+        emi, ref, held, old_sums, old_tiles, out, tiles, sums, *scratch = refs
+    else:
+        held, sums, tiles, *scratch = refs
+    (
+        geo_all, centre, far_rep, near_pos, near_rep, near_leave, near_arrive,
+        leave_even, arrive_even, leave_odd, arrive_odd, flag_vec, flag_sm, sem,
+    ) = scratch
+    n_seg = n_old + n_new
+    bands, width = held.shape[1] // 2 - GEO_ROWS // 2, held.shape[2]
+    n_tri = triangle(n_new)
+    n_pairs = n_tri + n_new * n_old
     halves = width // BLOCK
-    first = pltpu.make_async_copy(low_half, held.at[0:half], sems.at[0])
-    second = pltpu.make_async_copy(high_half, held.at[half:n_seg], sems.at[1])
-    first.start()
-    second.start()
-    sums[...] = jnp.zeros_like(sums)
-    tiles[n_pairs] = jnp.zeros((width, width), jnp.bfloat16)
-    first.wait()
-    second.wait()
     geo_at = 2 * bands
     for k in range(n_seg):
         piece = held[k, geo_at : geo_at + GEO_ROWS, :].astype(jnp.float32)
         geo = (piece[0:8] + piece[8:16]) + piece[16:24]
         geo_all[k] = geo
         flag_vec[k : k + 1, :] = geo[FLAG_ROW : FLAG_ROW + 1, 0:BLOCK].astype(jnp.int32)
-    flag_copy = pltpu.make_async_copy(flag_vec, flag_sm, sems.at[2])
+    flag_copy = pltpu.make_async_copy(flag_vec, flag_sm, sem)
     flag_copy.start()
+    if n_old:
+        sums[0:n_old] = old_sums[...]
+    sums[n_old:n_seg] = jnp.zeros((n_new, bands, width), jnp.float32)
+    tiles[n_pairs] = jnp.zeros((width, width), jnp.bfloat16)
     row = lax.broadcasted_iota(jnp.int32, (8, width), 0)
     for k in range(n_seg):
         geo = geo_all[k]
         for c in range(3):
             far_rep[k, c] = jnp.broadcast_to(geo[c : c + 1], (8, width))
-        near_pos[k, :, 0:8] = jnp.transpose(geo)
+        if k < n_old:
+            continue
+        at = k - n_old
+        near_pos[at, :, 0:8] = jnp.transpose(geo)
         middle = jnp.broadcast_to(geo[:, 0:1], (8, width))
-        centre[k] = middle
+        centre[at] = middle
         offset = jnp.where(row < 3, geo - middle, 0.0)
         normal = jnp.where(row < 3, pltpu.roll(geo, 5, 0), 0.0)
         along = jnp.sum(normal * offset, axis=0, keepdims=True)
-        near_leave[k] = jnp.transpose(near_stack(jnp.where(row == 3, -along, normal))).astype(jnp.bfloat16)
-        near_arrive[k] = jnp.transpose(near_stack(jnp.where(row == 3, 1.0, -offset))).astype(jnp.bfloat16)
+        near_leave[at] = jnp.transpose(near_stack(jnp.where(row == 3, -along, normal))).astype(jnp.bfloat16)
+        near_arrive[at] = jnp.transpose(near_stack(jnp.where(row == 3, 1.0, -offset))).astype(jnp.bfloat16)
     flag_copy.wait()
     col_mask = (1 << col_bits) - 1
 
     def pair_of(t):
         t = jnp.int32(t)
-        shift = t // n_seg
-        near = t % n_seg
-        return near, (near + shift) % n_seg
+        near = t % n_new
+        far = (near + t // n_new) % n_new + n_old
+        if n_old:
+            far = jnp.where(t < n_tri, far, jnp.minimum((t - n_tri) // n_new, n_old - 1))
+            near = jnp.where(t < n_tri, near, (t - n_tri) % n_new)
+        return near, near + n_old, far
 
     def live(near_at, far_at, i, j):
-        near = bit_reverse(near_at, seg_bits)
-        far = bit_reverse(far_at, seg_bits)
+        near = bit_reverse(near_at, bits) << (seg_bits - bits)
+        far = bit_reverse(far_at, bits) << (seg_bits - bits)
         holder = (near & ~col_mask) | (far & col_mask)
         apart = near ^ far
         index = ((((apart & col_mask) << 1) | i) * n_far) + (((apart >> col_bits) << 1) | j)
-        return flag_sm[bit_reverse(holder, seg_bits), index]
+        return flag_sm[bit_reverse(holder >> (seg_bits - bits), bits), index]
 
     def project(t, leave, arrive):
-        near_at, far_at = pair_of(t)
+        local, near_at, far_at = pair_of(t)
         geo = geo_all[far_at]
-        offset = jnp.where(row < 3, geo - centre[near_at], 0.0)
+        offset = jnp.where(row < 3, geo - centre[local], 0.0)
         normal = jnp.where(row < 3, pltpu.roll(geo, 5, 0), 0.0) * (-1.0 / math.pi)
         along = jnp.sum(normal * offset, axis=0, keepdims=True)
         leave[...] = jnp.dot(
-            near_leave[near_at], far_stack(jnp.where(row == 3, 1.0, offset)),
+            near_leave[local], far_stack(jnp.where(row == 3, 1.0, offset)),
             preferred_element_type=jnp.float32,
         )
         arrive[...] = jnp.dot(
-            near_arrive[near_at], far_stack(jnp.where(row == 3, along, normal)),
+            near_arrive[local], far_stack(jnp.where(row == 3, along, normal)),
             preferred_element_type=jnp.float32,
         )
 
     def form(t, leave, arrive, fresh):
-        near_at, far_at = pair_of(t)
+        local, near_at, far_at = pair_of(t)
         flags = [
             [
                 (live(near_at, far_at, i, j) | live(far_at, near_at, j, i)).astype(jnp.float32)
@@ -155,12 +172,12 @@
             for part in range(2):
                 at = strip * 16 + part * 8
                 if fresh:
-                    cols_now = near_pos[near_at, at : at + 8, :]
+                    cols_now = near_pos[local, at : at + 8, :]
                     now = [jnp.broadcast_to(cols_now[:, c : c + 1], (8, BLOCK)) for c in range(3)]
                     for c in range(3):
-                        near_rep[near_at, c, at : at + 8, :] = now[c]
+                        near_rep[local, c, at : at + 8, :] = now[c]
                 else:
-                    now = [near_rep[near_at, c, at : at + 8, :] for c in range(3)]
+                    now = [near_rep[local, c, at : at + 8, :] for c in range(3)]
                 nears.append(now)
             for j in range(halves):
                 cols = slice(j * BLOCK, (j + 1) * BLOCK)
@@ -178,7 +195,7 @@
                 tiles[t, strip * 16 : strip * 16 + 16, cols] = strip_now * flags[i][j].astype(jnp.bfloat16)
 
     def apply(t):
-        near_at, far_at = pair_of(t)
+        local, near_at, far_at = pair_of(t)
         tile = tiles[t]
         to_near = lax.dot_general(
             held[far_at, 0:bands, :], tile, (((1,), (1,)), ((), ())), preferred_element_type=jnp.float32
@@ -200,42 +217,70 @@
 
     even, odd = (leave_even, arrive_even), (leave_odd, arrive_odd)
     project(0, *even)
-    lax.fori_loop(0, n_seg // 2, functools.partial(two_steps, True), 0)
-    lax.fori_loop(n_seg // 2, n_pairs // 2, functools.partial(two_steps, False), 0)
+    lax.fori_loop(0, n_new // 2, functools.partial(two_steps, True), 0)
+    lax.fori_loop(n_new // 2, n_pairs // 2, functools.partial(two_steps, False), 0)
     apply(n_pairs - 1)
+    if not last:
+        return
     total = jnp.zeros((bands, width), jnp.float32)
     for k in range(n_seg):
         base = held[k, 0:bands, :].astype(jnp.float32)
         gain = held[k, bands : 2 * bands, :].astype(jnp.float32)
         weighted = (base + gain * sums[k]).astype(jnp.bfloat16)
-        if k <= half:
-            tile, over = tiles[k * n_seg], 1
+        if k < n_old:
+            t, over = own_tile(k, n_old)
+            tile = old_tiles[t]
         else:
-            tile, over = tiles[(n_seg - k) * n_seg + k], 0
+            tile, over = tiles[n_tri + k - n_old], 0
         total += lax.dot_general(
             weighted, tile, (((1,), (over,)), ((), ())), preferred_element_type=jnp.float32
         )
     out[...] = emi[...] + ref[...] * total
 
 
-def main_scratch(n_seg, rows, bands, width):
-    n_pairs = n_seg * (n_seg + 1) // 2
-    return [
-        pltpu.VMEM((n_seg, rows, width), jnp.bfloat16),
-        pltpu.VMEM((n_seg, 8, width), jnp.float32),
-        pltpu.VMEM((n_seg, 8, width), jnp.float32),
-        pltpu.VMEM((n_seg, 3, 8, width), jnp.float32),
-        pltpu.VMEM((n_seg, width, BLOCK), jnp.float32),
-        pltpu.VMEM((n_seg, 3, width, BLOCK), jnp.float32),
-        pltpu.VMEM((n_seg, width, 48), jnp.bfloat16),
-        pltpu.VMEM((n_seg, width, 48), jnp.bfloat16),
-        *[pltpu.VMEM((width, width), jnp.float32)] * 4,
+def grow(n_old, n_new, seg_bits, col_bits, n_far, held, rest):
+    rows, width = held.shape[1:]
+    bands = (rows - GEO_ROWS) // 2
+    n_seg = n_old + n_new
+    bits = n_seg.bit_length() - 1
+    last = bits == seg_bits
+    n_pairs = triangle(n_new) + n_new * n_old
+    vmem = pl.BlockSpec(memory_space=pltpu.VMEM)
+    state = [
         pltpu.VMEM((n_pairs + 1, width, width), jnp.bfloat16),
         pltpu.VMEM((n_seg, bands, width), jnp.float32),
-        pltpu.VMEM((n_seg, BLOCK), jnp.int32),
-        pltpu.SMEM((n_seg, BLOCK), jnp.int32),
-        pltpu.SemaphoreType.DMA((3,)),
     ]
+    if last:
+        args = (rest[0], rest[1], held, rest[2], rest[3])
+        outs = jax.ShapeDtypeStruct((bands, width), jnp.float32)
+    else:
+        args, outs = (held,), state[::-1]
+    pieces = 48
+    work = n_pairs * width * width
+    return pl.pallas_call(
+        functools.partial(grow_kernel, n_old, n_new, bits, seg_bits, col_bits, n_far, last),
+        out_shape=outs,
+        in_specs=[vmem] * len(args),
+        out_specs=vmem if last else [vmem, vmem],
+        scratch_shapes=(state if last else [])
+        + [
+            pltpu.VMEM((n_seg, 8, width), jnp.float32),
+            pltpu.VMEM((n_new, 8, width), jnp.float32),
+            pltpu.VMEM((n_seg, 3, 8, width), jnp.float32),
+            pltpu.VMEM((n_new, width, BLOCK), jnp.float32),
+            pltpu.VMEM((n_new, 3, width, BLOCK), jnp.float32),
+            pltpu.VMEM((n_new, width, pieces), jnp.bfloat16),
+            pltpu.VMEM((n_new, width, pieces), jnp.bfloat16),
+            *[pltpu.VMEM((width, width), jnp.float32)] * 4,
+            pltpu.VMEM((n_seg, BLOCK), jnp.int32),
+            pltpu.SMEM((n_seg, BLOCK), jnp.int32),
+            pltpu.SemaphoreType.DMA,
+        ],
+        compiler_params=pltpu.CompilerParams(vmem_limit_bytes=32 * 1024 * 1024),
+        cost_estimate=pl.CostEstimate(
+            flops=work * (4 * pieces + 4 * bands), bytes_accessed=held.size * 2, transcendentals=work
+        ),
+    )(*args)
 
 
 def one_exchange(positions, normals, areas, emission, reflect, pair_row, pair_col, pair_live):
@@ -249,28 +294,23 @@
     rows = 2 * bands + GEO_ROWS
     vmem = pl.BlockSpec(memory_space=pltpu.VMEM)
     smem = pl.BlockSpec(memory_space=pltpu.SMEM)
-    hbm = pl.BlockSpec(memory_space=pl.ANY)
     packed = pl.pallas_call(
         functools.partial(pack_kernel, col_bits, n_far),
-        out_shape=jax.ShapeDtypeStruct((rows, width), jnp.bfloat16),
+        out_shape=pltpu.VMEM((rows, width), jnp.bfloat16),
         in_specs=[vmem] * 5 + [smem] * 3,
         out_specs=vmem,
     )(positions, normals, areas.reshape(1, width), emission, reflect, pair_row, pair_col, pair_live)
     gathered = packed[None]
+    state = ()
     for bit in reversed(range(seg_bits)):
         arrived = lax.ppermute(
             gathered, ("row", "col"), [(i, i ^ (1 << bit)) for i in range(n_seg)]
         )
-        if bit:
-            gathered = jnp.concatenate([gathered, arrived])
-    return pl.pallas_call(
-        functools.partial(main_kernel, n_seg, seg_bits, col_bits, n_far),
-        out_shape=jax.ShapeDtypeStruct((bands, width), jnp.float32),
-        in_specs=[vmem, vmem, hbm, hbm],
-        out_specs=vmem,
-        scratch_shapes=main_scratch(n_seg, rows, bands, width),
-        compiler_params=pltpu.CompilerParams(vmem_limit_bytes=40 * 1024 * 1024),
-    )(emission, reflect, gathered, arrived)
+        if bit == 0:
+            state = grow(0, n_seg // 2, seg_bits, col_bits, n_far, gathered, ())
+        gathered = jnp.concatenate([gathered, arrived])
+    half = n_seg // 2
+    return grow(half, half, seg_bits, col_bits, n_far, gathered, (emission, reflect, *state))
 
 
 def form_tiles(near, far):
@@ -354,7 +394,7 @@
     n_row, n_col = lax.axis_size("row"), lax.axis_size("col")
     n_seg = n_row * n_col
     powers = n_row & (n_row - 1) == 0 and n_col & (n_col - 1) == 0
-    small = areas.shape[0] == 2 * BLOCK and 4 <= n_seg <= 16
+    small = areas.shape[0] == 2 * BLOCK and 8 <= n_seg <= 16
     plan = one_exchange if powers and small else two_exchanges
     return plan(positions, normals, areas, emission, reflect, pair_row, pair_col, pair_live)
 

time: 32.4 us -> 27.5 us (0.85)
  waiting for transfers between devices: 10.2 us -> 5.92 us
  other arithmetic: 0.83 us -> 0.07 us
    ppermute x3, waiting for transfers between devices: 10.2 us -> 5.92 us  [one_exchange(): lax.ppermute(gathered, ('row', 'col'), [(i, i ^ 1 << bit) for i in range(...]
    concatenate x2 -> x3, other arithmetic: 0.83 us -> 0.07 us  [one_exchange(): gathered = jnp.concatenate([gathered, arrived])]
    pallas_call x1 -> x2, Pallas kernels: 12.3 us -> 13 us  [grow(): pl.pallas_call(functools.partial(grow_kernel, n_old, n_new, bits, seg_bit...]
    pallas_call x1, Pallas kernels: 1.63 us -> 1.03 us  [one_exchange(): pl.pallas_call(functools.partial(pack_kernel, col_bits, n_far), out_shape...]
  transfers between devices with their start and end apart: 3 -> 3, of which waited for: 3 -> 3; matrix products, arithmetic and copies ran while one was open for 0% -> 0% of each run, Pallas kernels for 0% -> 14%
where the time goes in v3:
time: 27.5 us; the launch traced here: 27.3 us
  Pallas kernels  14 us (51%)
  starting transfers between devices  7.31 us (27%)
  waiting for transfers between devices  5.92 us (22%)
    pallas_call x2, Pallas kernels, grow(): pl.pallas_call(functools.partial(grow_kernel, n_old, n_new, bits, seg_bit...  13 us
    ppermute x3, starting transfers between devices, one_exchange(): lax.ppermute(gathered, ('row', 'col'), [(i, i ^ 1 << bit) for i in range(...  7.31 us
    ppermute x3, waiting for transfers between devices, one_exchange(): lax.ppermute(gathered, ('row', 'col'), [(i, i ^ 1 << bit) for i in range(...  5.92 us
    pallas_call x1, Pallas kernels, one_exchange(): pl.pallas_call(functools.partial(pack_kernel, col_bits, n_far), out_shape...  1.03 us
  transfers between devices with their start and end apart: 3, of which 3 were waited for; matrix products, arithmetic and copies ran while one was open for 0% of the time, Pallas kernels for 14%

profile of v3, /device:TPU:0, one launch (start us, length us, event | category | flops | bytes accessed | tf_op | source)
XLA Modules:
  0.0 27.3 jit_solution(9986739871701750232)
XLA Ops:
  0.0 0.0 copy-start.1
  0.0 0.0 copy-start
  0.0 1.0 %shard_map.82 = bf16[96,256]{1,0:T(8,128)(2,1)S(1)} custom-call(f32[3,256]{1,0:T(4,128)} %pos.1, f32[3,256]{1,0:T(4,128)} %nrm.1, f32[1,256]{1,0:T(1,128)} %bitcast.6, f32[32,256]{1,0:T(8,128)} %refs_0_.1, f32[32,256]{1,0:T(8,128)} %refs_1_.1, s32[32]{0:T(128)} %prow.1, s32[32]{0:T(128)} %pcol.1, s32[32]{0:T(128)} %plive.1), custom_call_target="tpu_custom_call" | custom-call | tf_op jit(solution)/shard_map/pallas_call | solution.py:297
  1.0 4.1 %collective-permute-start = (bf16[1,96,256]{2,1,0:T(8,128)(2,1)S(1)}, bf16[1,96,256]{2,1,0:T(8,128)(2,1)S(1)}, u32[]{:S(2)}, u32[]{:S(2)}) collective-permute-start(bf16[1,96,256]{2,1,0:T(8,128)(2,1)S(1)} %bitcast.2), channel_id=1, source_target_pairs={{0,8},{2,10},{4,12},{6,14},{8,0},{10,2},{12,4},{14,6},{1,9},{3,11}... | collective-permute-start | bytes 147464 | tf_op jit(solution)/shard_map/ppermute | solution.py:306
  5.1 2.6 %collective-permute-done = bf16[1,96,256]{2,1,0:T(8,128)(2,1)S(1)} collective-permute-done((bf16[1,96,256]{2,1,0:T(8,128)(2,1)S(1)}, bf16[1,96,256]{2,1,0:T(8,128)(2,1)S(1)}, u32[]{:S(2)}, u32[]{:S(2)}) %collective-permute-start) | collective-permute-done | bytes 49184 | tf_op jit(solution)/shard_map/ppermute | solution.py:306
  7.7 1.4 %collective-permute-start.1 = (bf16[2,96,256]{2,1,0:T(8,128)(2,1)S(1)}, bf16[2,96,256]{2,1,0:T(8,128)(2,1)S(1)}, u32[]{:S(2)}, u32[]{:S(2)}) collective-permute-start(bf16[2,96,256]{2,1,0:T(8,128)(2,1)S(1)} %pad_maximum_fusion.2), channel_id=1, source_target_pairs={{0,4},{2,6},{4,0},{6,2},{8,12},{10,14},{12,8},{14,10},{1,5},{3,7},... | collective-permute-start | bytes 294920 | tf_op jit(solution)/shard_map/ppermute | solution.py:306
  9.2 3.2 %collective-permute-done.1 = bf16[2,96,256]{2,1,0:T(8,128)(2,1)S(1)} collective-permute-done((bf16[2,96,256]{2,1,0:T(8,128)(2,1)S(1)}, bf16[2,96,256]{2,1,0:T(8,128)(2,1)S(1)}, u32[]{:S(2)}, u32[]{:S(2)}) %collective-permute-start.1) | collective-permute-done | bytes 98336 | tf_op jit(solution)/shard_map/ppermute | solution.py:306
  12.5 1.8 %collective-permute-start.2 = (bf16[4,96,256]{2,1,0:T(8,128)(2,1)S(1)}, bf16[4,96,256]{2,1,0:T(8,128)(2,1)S(1)}, u32[]{:S(2)}, u32[]{:S(2)}) collective-permute-start(bf16[4,96,256]{2,1,0:T(8,128)(2,1)S(1)} %pad_maximum_fusion.1.refs_0_), channel_id=1, source_target_pairs={{0,2},{2,0},{4,6},{6,4},{8,10},{10,8},{12,14},{14,12},{1,3},{3,1},... | collective-permute-start | bytes 589832 | tf_op jit(solution)/shard_map/ppermute | solution.py:306
  14.2 3.9 %shard_map.83 = (f32[4,32,256]{2,1,0:T(8,128)S(1)}, bf16[11,256,256]{2,1,0:T(8,128)(2,1)S(1)}) custom-call(bf16[4,96,256]{2,1,0:T(8,128)(2,1)S(1)} %pad_maximum_fusion.1.refs_0_), custom_call_target="tpu_custom_call" | custom-call | flops 209715200 | bytes 196608 | tf_op jit(solution)/shard_map/pallas_call | solution.py:260
  18.1 0.1 collective-permute-done.2
  18.2 0.0 copy-done.1
  18.2 0.0 copy-done
  18.3 9.1 %shard_map.84 = f32[32,256]{1,0:T(8,128)} custom-call(f32[32,256]{1,0:T(8,128)S(1)} %copy-done, f32[32,256]{1,0:T(8,128)S(1)} %copy-done.1, bf16[8,96,256]{2,1,0:T(8,128)(2,1)S(1)} %pad_maximum_fusion.refs_2_, f32[4,32,256]{2,1,0:T(8,128)S(1)} %get-tuple-element.7.refs_3_, bf16[11,256,256]{2,1,0:T(8,128)(2,1)S(1)} %get-tuple-element.8.refs_4_), custom_call_target="tpu_custom_call" | custom-call | flops 545259520 | bytes 393216 | tf_op jit(solution)/shard_map/pallas_call | solution.py:260
  (3 shorter events, 0.1 us)
Async XLA Ops:
  0.0 18.2 %copy-start.1 = (f32[32,256]{1,0:T(8,128)S(1)}, f32[32,256]{1,0:T(8,128)}, u32[]{:S(2)}) copy-start(f32[32,256]{1,0:T(8,128)} %refs_1_.1) | copy-start | bytes 98308
  0.0 18.2 %copy-start = (f32[32,256]{1,0:T(8,128)S(1)}, f32[32,256]{1,0:T(8,128)}, u32[]{:S(2)}) copy-start(f32[32,256]{1,0:T(8,128)} %refs_0_.1) | copy-start | bytes 98308
  1.0 6.7 %collective-permute-start = (bf16[1,96,256]{2,1,0:T(8,128)(2,1)S(1)}, bf16[1,96,256]{2,1,0:T(8,128)(2,1)S(1)}, u32[]{:S(2)}, u32[]{:S(2)}) collective-permute-start(bf16[1,96,256]{2,1,0:T(8,128)(2,1)S(1)} %bitcast.2), channel_id=1, source_target_pairs={{0,8},{2,10},{4,12},{6,14},{8,0},{10,2},{12,4},{14,6},{1,9},{3,11}... | collective-permute-start | bytes 147464 | tf_op jit(solution)/shard_map/ppermute | solution.py:306
  7.7 4.7 %collective-permute-start.1 = (bf16[2,96,256]{2,1,0:T(8,128)(2,1)S(1)}, bf16[2,96,256]{2,1,0:T(8,128)(2,1)S(1)}, u32[]{:S(2)}, u32[]{:S(2)}) collective-permute-start(bf16[2,96,256]{2,1,0:T(8,128)(2,1)S(1)} %pad_maximum_fusion.2), channel_id=1, source_target_pairs={{0,4},{2,6},{4,0},{6,2},{8,12},{10,14},{12,8},{14,10},{1,5},{3,7},... | collective-permute-start | bytes 294920 | tf_op jit(solution)/shard_map/ppermute | solution.py:306
  12.5 5.7 %collective-permute-start.2 = (bf16[4,96,256]{2,1,0:T(8,128)(2,1)S(1)}, bf16[4,96,256]{2,1,0:T(8,128)(2,1)S(1)}, u32[]{:S(2)}, u32[]{:S(2)}) collective-permute-start(bf16[4,96,256]{2,1,0:T(8,128)(2,1)S(1)} %pad_maximum_fusion.1.refs_0_), channel_id=1, source_target_pairs={{0,2},{2,0},{4,6},{6,4},{8,10},{10,8},{12,14},{14,12},{1,3},{3,1},... | collective-permute-start | bytes 589832 | tf_op jit(solution)/shard_map/ppermute | solution.py:306

commit v4 on v3

--- a/solution.py
+++ b/solution.py
@@ -301,14 +301,16 @@
         out_specs=vmem,
     )(positions, normals, areas.reshape(1, width), emission, reflect, pair_row, pair_col, pair_live)
     gathered = packed[None]
-    state = ()
-    for bit in reversed(range(seg_bits)):
-        arrived = lax.ppermute(
-            gathered, ("row", "col"), [(i, i ^ (1 << bit)) for i in range(n_seg)]
-        )
-        if bit == 0:
-            state = grow(0, n_seg // 2, seg_bits, col_bits, n_far, gathered, ())
-        gathered = jnp.concatenate([gathered, arrived])
+
+    def swap(value, distance):
+        return lax.ppermute(value, ("row", "col"), [(i, i ^ distance) for i in range(n_seg)])
+
+    for bit in reversed(range(2, seg_bits)):
+        gathered = jnp.concatenate([gathered, swap(gathered, 1 << bit)])
+    beside, across, diagonal = (swap(gathered, distance) for distance in (2, 1, 3))
+    gathered = jnp.concatenate([gathered, beside])
+    state = grow(0, n_seg // 2, seg_bits, col_bits, n_far, gathered, ())
+    gathered = jnp.concatenate([gathered, across, diagonal])
     half = n_seg // 2
     return grow(half, half, seg_bits, col_bits, n_far, gathered, (emission, reflect, *state))
 

time: 27.5 us -> 28.5 us (1.036)
  waiting for transfers between devices: 5.92 us -> 6.56 us
  starting transfers between devices: 7.31 us -> 7.66 us
    ppermute x3 -> x4, waiting for transfers between devices: 5.92 us -> 6.56 us  [swap(): lax.ppermute(value, ('row', 'col'), [(i, i ^ distance) for i in range(n_s...]
    ppermute x3 -> x4, starting transfers between devices: 7.31 us -> 7.66 us  [swap(): lax.ppermute(value, ('row', 'col'), [(i, i ^ distance) for i in range(n_s...]
  transfers between devices with their start and end apart: 3 -> 4, of which waited for: 3 -> 2; matrix products, arithmetic and copies ran while one was open for 0% -> 0% of each run, Pallas kernels for 14% -> 14%
where the time goes in v4:
time: 28.5 us; the launch traced here: 28.4 us
  Pallas kernels  14 us (49%)
  starting transfers between devices  7.66 us (27%)
  waiting for transfers between devices  6.56 us (23%)
    pallas_call x2, Pallas kernels, grow(): pl.pallas_call(functools.partial(grow_kernel, n_old, n_new, bits, seg_bit...  13 us
    ppermute x4, starting transfers between devices, swap(): lax.ppermute(value, ('row', 'col'), [(i, i ^ distance) for i in range(n_s...  7.66 us
    ppermute x4, waiting for transfers between devices, swap(): lax.ppermute(value, ('row', 'col'), [(i, i ^ distance) for i in range(n_s...  6.56 us
    pallas_call x1, Pallas kernels, one_exchange(): pl.pallas_call(functools.partial(pack_kernel, col_bits, n_far), out_shape...  1.03 us
  transfers between devices with their start and end apart: 4, of which 2 were waited for; matrix products, arithmetic and copies ran while one was open for 0% of the time, Pallas kernels for 14%

profile of v4, /device:TPU:0, one launch (start us, length us, event | category | flops | bytes accessed | tf_op | source)
XLA Modules:
  0.0 28.4 jit_solution(9144990153341605774)
XLA Ops:
  0.0 0.0 copy-start.1
  0.0 0.0 copy-start
  0.0 1.0 %shard_map.82 = bf16[96,256]{1,0:T(8,128)(2,1)S(1)} custom-call(f32[3,256]{1,0:T(4,128)} %pos.1, f32[3,256]{1,0:T(4,128)} %nrm.1, f32[1,256]{1,0:T(1,128)} %bitcast.6, f32[32,256]{1,0:T(8,128)} %refs_0_.1, f32[32,256]{1,0:T(8,128)} %refs_1_.1, s32[32]{0:T(128)} %prow.1, s32[32]{0:T(128)} %pcol.1, s32[32]{0:T(128)} %plive.1), custom_call_target="tpu_custom_call" | custom-call | tf_op jit(solution)/shard_map/pallas_call | solution.py:297
  1.0 4.1 %collective-permute-start = (bf16[1,96,256]{2,1,0:T(8,128)(2,1)S(1)}, bf16[1,96,256]{2,1,0:T(8,128)(2,1)S(1)}, u32[]{:S(2)}, u32[]{:S(2)}) collective-permute-start(bf16[1,96,256]{2,1,0:T(8,128)(2,1)S(1)} %bitcast.3), channel_id=1, source_target_pairs={{0,8},{2,10},{4,12},{6,14},{8,0},{10,2},{12,4},{14,6},{1,9},{3,11}... | collective-permute-start | bytes 147464 | tf_op jit(solution)/shard_map/ppermute | solution.py:306
  5.1 2.6 %collective-permute-done = bf16[1,96,256]{2,1,0:T(8,128)(2,1)S(1)} collective-permute-done((bf16[1,96,256]{2,1,0:T(8,128)(2,1)S(1)}, bf16[1,96,256]{2,1,0:T(8,128)(2,1)S(1)}, u32[]{:S(2)}, u32[]{:S(2)}) %collective-permute-start) | collective-permute-done | bytes 49184 | tf_op jit(solution)/shard_map/ppermute | solution.py:306
  7.7 2.4 %collective-permute-start.3 = (bf16[2,96,256]{2,1,0:T(8,128)(2,1)S(1)}, bf16[2,96,256]{2,1,0:T(8,128)(2,1)S(1)}, u32[]{:S(2)}, u32[]{:S(2)}) collective-permute-start(bf16[2,96,256]{2,1,0:T(8,128)(2,1)S(1)} %pad_maximum_fusion.1), channel_id=1, source_target_pairs={{0,6},{2,4},{4,2},{6,0},{8,14},{10,12},{12,10},{14,8},{1,7},{3,5},... | collective-permute-start | bytes 294920 | tf_op jit(solution)/shard_map/ppermute | solution.py:306
  10.1 0.5 %collective-permute-start.2 = (bf16[2,96,256]{2,1,0:T(8,128)(2,1)S(1)}, bf16[2,96,256]{2,1,0:T(8,128)(2,1)S(1)}, u32[]{:S(2)}, u32[]{:S(2)}) collective-permute-start(bf16[2,96,256]{2,1,0:T(8,128)(2,1)S(1)} %pad_maximum_fusion.1), channel_id=1, source_target_pairs={{0,2},{2,0},{4,6},{6,4},{8,10},{10,8},{12,14},{14,12},{1,3},{3,1},... | collective-permute-start | bytes 294920 | tf_op jit(solution)/shard_map/ppermute | solution.py:306
  10.7 0.6 %collective-permute-start.1 = (bf16[2,96,256]{2,1,0:T(8,128)(2,1)S(1)}, bf16[2,96,256]{2,1,0:T(8,128)(2,1)S(1)}, u32[]{:S(2)}, u32[]{:S(2)}) collective-permute-start(bf16[2,96,256]{2,1,0:T(8,128)(2,1)S(1)} %pad_maximum_fusion.1), channel_id=1, source_target_pairs={{0,4},{2,6},{4,0},{6,2},{8,12},{10,14},{12,8},{14,10},{1,5},{3,7},... | collective-permute-start | bytes 294920 | tf_op jit(solution)/shard_map/ppermute | solution.py:306
  11.3 4.0 %collective-permute-done.1 = bf16[2,96,256]{2,1,0:T(8,128)(2,1)S(1)} collective-permute-done((bf16[2,96,256]{2,1,0:T(8,128)(2,1)S(1)}, bf16[2,96,256]{2,1,0:T(8,128)(2,1)S(1)}, u32[]{:S(2)}, u32[]{:S(2)}) %collective-permute-start.1) | collective-permute-done | bytes 98336 | tf_op jit(solution)/shard_map/ppermute | solution.py:306
  15.3 3.9 %shard_map.83 = (f32[4,32,256]{2,1,0:T(8,128)S(1)}, bf16[11,256,256]{2,1,0:T(8,128)(2,1)S(1)}) custom-call(bf16[4,96,256]{2,1,0:T(8,128)(2,1)S(1)} %pad_maximum_fusion.refs_0_), custom_call_target="tpu_custom_call" | custom-call | flops 209715200 | bytes 196608 | tf_op jit(solution)/shard_map/pallas_call | solution.py:260
  19.2 0.0 collective-permute-done.2
  19.2 0.0 collective-permute-done.3
  19.3 0.0 copy-done.1
  19.3 0.0 copy-done
  19.3 9.1 %shard_map.84 = f32[32,256]{1,0:T(8,128)} custom-call(f32[32,256]{1,0:T(8,128)S(1)} %copy-done, f32[32,256]{1,0:T(8,128)S(1)} %copy-done.1, bf16[8,96,256]{2,1,0:T(8,128)(2,1)S(1)} %constant_dynamic-update-slice_fusion.refs_2_, f32[4,32,256]{2,1,0:T(8,128)S(1)} %get-tuple-element.7.refs_3_, bf16[11,256,256]{2,1,0:T(8,128)(2,1)S(1)} %get-tuple-element.8.refs_4_), custom_call_target="tpu_custom_call" | custom-call | flops 545259520 | bytes 393216 | tf_op jit(solution)/shard_map/pallas_call | solution.py:260
  (7 shorter events, 0.1 us)
Async XLA Ops:
  0.0 19.3 %copy-start.1 = (f32[32,256]{1,0:T(8,128)S(1)}, f32[32,256]{1,0:T(8,128)}, u32[]{:S(2)}) copy-start(f32[32,256]{1,0:T(8,128)} %refs_1_.1) | copy-start | bytes 98308
  0.0 19.3 %copy-start = (f32[32,256]{1,0:T(8,128)S(1)}, f32[32,256]{1,0:T(8,128)}, u32[]{:S(2)}) copy-start(f32[32,256]{1,0:T(8,128)} %refs_0_.1) | copy-start | bytes 98308
  1.0 6.7 %collective-permute-start = (bf16[1,96,256]{2,1,0:T(8,128)(2,1)S(1)}, bf16[1,96,256]{2,1,0:T(8,128)(2,1)S(1)}, u32[]{:S(2)}, u32[]{:S(2)}) collective-permute-start(bf16[1,96,256]{2,1,0:T(8,128)(2,1)S(1)} %bitcast.3), channel_id=1, source_target_pairs={{0,8},{2,10},{4,12},{6,14},{8,0},{10,2},{12,4},{14,6},{1,9},{3,11}... | collective-permute-start | bytes 147464 | tf_op jit(solution)/shard_map/ppermute | solution.py:306
  7.7 11.5 %collective-permute-start.3 = (bf16[2,96,256]{2,1,0:T(8,128)(2,1)S(1)}, bf16[2,96,256]{2,1,0:T(8,128)(2,1)S(1)}, u32[]{:S(2)}, u32[]{:S(2)}) collective-permute-start(bf16[2,96,256]{2,1,0:T(8,128)(2,1)S(1)} %pad_maximum_fusion.1), channel_id=1, source_target_pairs={{0,6},{2,4},{4,2},{6,0},{8,14},{10,12},{12,10},{14,8},{1,7},{3,5},... | collective-permute-start | bytes 294920 | tf_op jit(solution)/shard_map/ppermute | solution.py:306
  10.1 9.1 %collective-permute-start.2 = (bf16[2,96,256]{2,1,0:T(8,128)(2,1)S(1)}, bf16[2,96,256]{2,1,0:T(8,128)(2,1)S(1)}, u32[]{:S(2)}, u32[]{:S(2)}) collective-permute-start(bf16[2,96,256]{2,1,0:T(8,128)(2,1)S(1)} %pad_maximum_fusion.1), channel_id=1, source_target_pairs={{0,2},{2,0},{4,6},{6,4},{8,10},{10,8},{12,14},{14,12},{1,3},{3,1},... | collective-permute-start | bytes 294920 | tf_op jit(solution)/shard_map/ppermute | solution.py:306
  10.7 4.6 %collective-permute-start.1 = (bf16[2,96,256]{2,1,0:T(8,128)(2,1)S(1)}, bf16[2,96,256]{2,1,0:T(8,128)(2,1)S(1)}, u32[]{:S(2)}, u32[]{:S(2)}) collective-permute-start(bf16[2,96,256]{2,1,0:T(8,128)(2,1)S(1)} %pad_maximum_fusion.1), channel_id=1, source_target_pairs={{0,4},{2,6},{4,0},{6,2},{8,12},{10,14},{12,8},{14,10},{1,5},{3,7},... | collective-permute-start | bytes 294920 | tf_op jit(solution)/shard_map/ppermute | solution.py:306

commit v5 on v4

--- a/solution.py
+++ b/solution.py
@@ -78,7 +78,11 @@
 
 def grow_kernel(n_old, n_new, bits, seg_bits, col_bits, n_far, last, *refs):
     if last:
-        emi, ref, held, old_sums, old_tiles, out, tiles, sums, *scratch = refs
+        diagonal, across, known, emi, ref, old_sums, old_tiles, out, tiles, sums, held, *scratch = refs
+        at = 0
+        for part in (known, across, diagonal):
+            held[at : at + part.shape[0]] = part[...]
+            at += part.shape[0]
     else:
         held, sums, tiles, *scratch = refs
     (
@@ -238,8 +242,8 @@
     out[...] = emi[...] + ref[...] * total
 
 
-def grow(n_old, n_new, seg_bits, col_bits, n_far, held, rest):
-    rows, width = held.shape[1:]
+def grow(n_old, n_new, seg_bits, col_bits, n_far, args):
+    rows, width = args[0].shape[1:]
     bands = (rows - GEO_ROWS) // 2
     n_seg = n_old + n_new
     bits = n_seg.bit_length() - 1
@@ -250,11 +254,7 @@
         pltpu.VMEM((n_pairs + 1, width, width), jnp.bfloat16),
         pltpu.VMEM((n_seg, bands, width), jnp.float32),
     ]
-    if last:
-        args = (rest[0], rest[1], held, rest[2], rest[3])
-        outs = jax.ShapeDtypeStruct((bands, width), jnp.float32)
-    else:
-        args, outs = (held,), state[::-1]
+    outs = jax.ShapeDtypeStruct((bands, width), jnp.float32) if last else state[::-1]
     pieces = 48
     work = n_pairs * width * width
     return pl.pallas_call(
@@ -262,7 +262,7 @@
         out_shape=outs,
         in_specs=[vmem] * len(args),
         out_specs=vmem if last else [vmem, vmem],
-        scratch_shapes=(state if last else [])
+        scratch_shapes=(state + [pltpu.VMEM((n_seg, rows, width), jnp.bfloat16)] if last else [])
         + [
             pltpu.VMEM((n_seg, 8, width), jnp.float32),
             pltpu.VMEM((n_new, 8, width), jnp.float32),
@@ -278,7 +278,7 @@
         ],
         compiler_params=pltpu.CompilerParams(vmem_limit_bytes=32 * 1024 * 1024),
         cost_estimate=pl.CostEstimate(
-            flops=work * (4 * pieces + 4 * bands), bytes_accessed=held.size * 2, transcendentals=work
+            flops=work * (4 * pieces + 4 * bands), bytes_accessed=n_seg * rows * width * 2, transcendentals=work
         ),
     )(*args)
 
@@ -309,10 +309,10 @@
         gathered = jnp.concatenate([gathered, swap(gathered, 1 << bit)])
     beside, across, diagonal = (swap(gathered, distance) for distance in (2, 1, 3))
     gathered = jnp.concatenate([gathered, beside])
-    state = grow(0, n_seg // 2, seg_bits, col_bits, n_far, gathered, ())
-    gathered = jnp.concatenate([gathered, across, diagonal])
+    state = grow(0, n_seg // 2, seg_bits, col_bits, n_far, (gathered,))
     half = n_seg // 2
-    return grow(half, half, seg_bits, col_bits, n_far, gathered, (emission, reflect, *state))
+    args = (diagonal, across, gathered, emission, reflect, *state)
+    return grow(half, half, seg_bits, col_bits, n_far, args)
 
 
 def form_tiles(near, far):

time: 28.5 us -> 26.6 us (0.933)
  waiting for transfers between devices: 6.56 us -> 4.68 us
    ppermute x4, waiting for transfers between devices: 6.56 us -> 4.68 us  [swap(): lax.ppermute(value, ('row', 'col'), [(i, i ^ distance) for i in range(n_s...]
  transfers between devices with their start and end apart: 4 -> 4, of which waited for: 2 -> 2; matrix products, arithmetic and copies ran while one was open for 0% -> 0% of each run, Pallas kernels for 14% -> 15%
where the time goes in v5:
time: 26.6 us; the launch traced here: 26.4 us
  Pallas kernels  14 us (53%)
  starting transfers between devices  7.65 us (29%)
  waiting for transfers between devices  4.68 us (18%)
    pallas_call x2, Pallas kernels, grow(): pl.pallas_call(functools.partial(grow_kernel, n_old, n_new, bits, seg_bit...  13 us
    ppermute x4, starting transfers between devices, swap(): lax.ppermute(value, ('row', 'col'), [(i, i ^ distance) for i in range(n_s...  7.65 us
    ppermute x4, waiting for transfers between devices, swap(): lax.ppermute(value, ('row', 'col'), [(i, i ^ distance) for i in range(n_s...  4.68 us
    pallas_call x1, Pallas kernels, one_exchange(): pl.pallas_call(functools.partial(pack_kernel, col_bits, n_far), out_shape...  1.03 us
  transfers between devices with their start and end apart: 4, of which 2 were waited for; matrix products, arithmetic and copies ran while one was open for 0% of the time, Pallas kernels for 15%

profile of v5, /device:TPU:0, one launch (start us, length us, event | category | flops | bytes accessed | tf_op | source)
XLA Modules:
  0.0 26.4 jit_solution(18024456375377248756)
XLA Ops:
  0.0 0.0 copy-start.1
  0.0 0.0 copy-start
  0.0 1.0 %shard_map.82 = bf16[96,256]{1,0:T(8,128)(2,1)S(1)} custom-call(f32[3,256]{1,0:T(4,128)} %pos.1, f32[3,256]{1,0:T(4,128)} %nrm.1, f32[1,256]{1,0:T(1,128)} %bitcast.5, f32[32,256]{1,0:T(8,128)} %refs_3_.1, f32[32,256]{1,0:T(8,128)} %refs_4_.1, s32[32]{0:T(128)} %prow.1, s32[32]{0:T(128)} %pcol.1, s32[32]{0:T(128)} %plive.1), custom_call_target="tpu_custom_call" | custom-call | tf_op jit(solution)/shard_map/pallas_call | solution.py:297
  1.0 4.1 %collective-permute-start = (bf16[1,96,256]{2,1,0:T(8,128)(2,1)S(1)}, bf16[1,96,256]{2,1,0:T(8,128)(2,1)S(1)}, u32[]{:S(2)}, u32[]{:S(2)}) collective-permute-start(bf16[1,96,256]{2,1,0:T(8,128)(2,1)S(1)} %bitcast.2), channel_id=1, source_target_pairs={{0,8},{2,10},{4,12},{6,14},{8,0},{10,2},{12,4},{14,6},{1,9},{3,11}... | collective-permute-start | bytes 147464 | tf_op jit(solution)/shard_map/ppermute | solution.py:306
  5.1 2.6 %collective-permute-done = bf16[1,96,256]{2,1,0:T(8,128)(2,1)S(1)} collective-permute-done((bf16[1,96,256]{2,1,0:T(8,128)(2,1)S(1)}, bf16[1,96,256]{2,1,0:T(8,128)(2,1)S(1)}, u32[]{:S(2)}, u32[]{:S(2)}) %collective-permute-start) | collective-permute-done | bytes 49184 | tf_op jit(solution)/shard_map/ppermute | solution.py:306
  7.7 1.4 %collective-permute-start.3 = (bf16[2,96,256]{2,1,0:T(8,128)(2,1)S(1)}, bf16[2,96,256]{2,1,0:T(8,128)(2,1)S(1)}, u32[]{:S(2)}, u32[]{:S(2)}) collective-permute-start(bf16[2,96,256]{2,1,0:T(8,128)(2,1)S(1)} %pad_maximum_fusion.1), channel_id=1, source_target_pairs={{0,4},{2,6},{4,0},{6,2},{8,12},{10,14},{12,8},{14,10},{1,5},{3,7},... | collective-permute-start | bytes 294920 | tf_op jit(solution)/shard_map/ppermute | solution.py:306
  9.2 1.5 %collective-permute-start.2 = (bf16[2,96,256]{2,1,0:T(8,128)(2,1)S(1)}, bf16[2,96,256]{2,1,0:T(8,128)(2,1)S(1)}, u32[]{:S(2)}, u32[]{:S(2)}) collective-permute-start(bf16[2,96,256]{2,1,0:T(8,128)(2,1)S(1)} %pad_maximum_fusion.1), channel_id=1, source_target_pairs={{0,2},{2,0},{4,6},{6,4},{8,10},{10,8},{12,14},{14,12},{1,3},{3,1},... | collective-permute-start | bytes 294920 | tf_op jit(solution)/shard_map/ppermute | solution.py:306
  10.7 0.6 %collective-permute-start.1 = (bf16[2,96,256]{2,1,0:T(8,128)(2,1)S(1)}, bf16[2,96,256]{2,1,0:T(8,128)(2,1)S(1)}, u32[]{:S(2)}, u32[]{:S(2)}) collective-permute-start(bf16[2,96,256]{2,1,0:T(8,128)(2,1)S(1)} %pad_maximum_fusion.1), channel_id=1, source_target_pairs={{0,6},{2,4},{4,2},{6,0},{8,14},{10,12},{12,10},{14,8},{1,7},{3,5},... | collective-permute-start | bytes 294920 | tf_op jit(solution)/shard_map/ppermute | solution.py:306
  11.3 2.1 %collective-permute-done.3 = bf16[2,96,256]{2,1,0:T(8,128)(2,1)S(1)} collective-permute-done((bf16[2,96,256]{2,1,0:T(8,128)(2,1)S(1)}, bf16[2,96,256]{2,1,0:T(8,128)(2,1)S(1)}, u32[]{:S(2)}, u32[]{:S(2)}) %collective-permute-start.3) | collective-permute-done | bytes 98336 | tf_op jit(solution)/shard_map/ppermute | solution.py:306
  13.4 3.9 %shard_map.83 = (f32[4,32,256]{2,1,0:T(8,128)S(1)}, bf16[11,256,256]{2,1,0:T(8,128)(2,1)S(1)}) custom-call(bf16[4,96,256]{2,1,0:T(8,128)(2,1)S(1)} %pad_maximum_fusion.refs_0_.refs_2_), custom_call_target="tpu_custom_call" | custom-call | flops 209715200 | bytes 196608 | tf_op jit(solution)/shard_map/pallas_call | solution.py:260
  17.3 0.0 collective-permute-done.2.refs_1_
  17.3 0.0 collective-permute-done.1.refs_0_
  17.3 0.0 copy-done.1
  17.3 0.0 copy-done
  17.3 9.1 %shard_map.84 = f32[32,256]{1,0:T(8,128)} custom-call(bf16[2,96,256]{2,1,0:T(8,128)(2,1)S(1)} %collective-permute-done.1.refs_0_, bf16[2,96,256]{2,1,0:T(8,128)(2,1)S(1)} %collective-permute-done.2.refs_1_, bf16[4,96,256]{2,1,0:T(8,128)(2,1)S(1)} %pad_maximum_fusion.refs_0_.refs_2_, f32[32,256]{1,0:T(8,128)S(1)} %copy-done, f32[32,256]{1,0:T(8,128)S(1)} %copy-done.1, ...), custom_call_target="tpu_custom_call" | custom-call | flops 545259520 | bytes 393216 | tf_op jit(solution)/shard_map/pallas_call | solution.py:260
  (2 shorter events, 0.0 us)
Async XLA Ops:
  0.0 17.3 %copy-start.1 = (f32[32,256]{1,0:T(8,128)S(1)}, f32[32,256]{1,0:T(8,128)}, u32[]{:S(2)}) copy-start(f32[32,256]{1,0:T(8,128)} %refs_4_.1) | copy-start | bytes 98308
  0.0 17.3 %copy-start = (f32[32,256]{1,0:T(8,128)S(1)}, f32[32,256]{1,0:T(8,128)}, u32[]{:S(2)}) copy-start(f32[32,256]{1,0:T(8,128)} %refs_3_.1) | copy-start | bytes 98308
  1.0 6.7 %collective-permute-start = (bf16[1,96,256]{2,1,0:T(8,128)(2,1)S(1)}, bf16[1,96,256]{2,1,0:T(8,128)(2,1)S(1)}, u32[]{:S(2)}, u32[]{:S(2)}) collective-permute-start(bf16[1,96,256]{2,1,0:T(8,128)(2,1)S(1)} %bitcast.2), channel_id=1, source_target_pairs={{0,8},{2,10},{4,12},{6,14},{8,0},{10,2},{12,4},{14,6},{1,9},{3,11}... | collective-permute-start | bytes 147464 | tf_op jit(solution)/shard_map/ppermute | solution.py:306
  7.7 5.6 %collective-permute-start.3 = (bf16[2,96,256]{2,1,0:T(8,128)(2,1)S(1)}, bf16[2,96,256]{2,1,0:T(8,128)(2,1)S(1)}, u32[]{:S(2)}, u32[]{:S(2)}) collective-permute-start(bf16[2,96,256]{2,1,0:T(8,128)(2,1)S(1)} %pad_maximum_fusion.1), channel_id=1, source_target_pairs={{0,4},{2,6},{4,0},{6,2},{8,12},{10,14},{12,8},{14,10},{1,5},{3,7},... | collective-permute-start | bytes 294920 | tf_op jit(solution)/shard_map/ppermute | solution.py:306
  9.2 8.1 %collective-permute-start.2 = (bf16[2,96,256]{2,1,0:T(8,128)(2,1)S(1)}, bf16[2,96,256]{2,1,0:T(8,128)(2,1)S(1)}, u32[]{:S(2)}, u32[]{:S(2)}) collective-permute-start(bf16[2,96,256]{2,1,0:T(8,128)(2,1)S(1)} %pad_maximum_fusion.1), channel_id=1, source_target_pairs={{0,2},{2,0},{4,6},{6,4},{8,10},{10,8},{12,14},{14,12},{1,3},{3,1},... | collective-permute-start | bytes 294920 | tf_op jit(solution)/shard_map/ppermute | solution.py:306
  10.7 6.6 %collective-permute-start.1 = (bf16[2,96,256]{2,1,0:T(8,128)(2,1)S(1)}, bf16[2,96,256]{2,1,0:T(8,128)(2,1)S(1)}, u32[]{:S(2)}, u32[]{:S(2)}) collective-permute-start(bf16[2,96,256]{2,1,0:T(8,128)(2,1)S(1)} %pad_maximum_fusion.1), channel_id=1, source_target_pairs={{0,6},{2,4},{4,2},{6,0},{8,14},{10,12},{12,10},{14,8},{1,7},{3,5},... | collective-permute-start | bytes 294920 | tf_op jit(solution)/shard_map/ppermute | solution.py:306

commit v6 on v5

--- a/solution.py
+++ b/solution.py
@@ -16,6 +16,8 @@
 
 GEO_ROWS = 32
 FLAG_ROW = 6
+CHUNK = 128
+PIECES = 48
 
 
 def bit_reverse(value, bits):
@@ -86,8 +88,8 @@
     else:
         held, sums, tiles, *scratch = refs
     (
-        geo_all, centre, far_rep, near_pos, near_rep, near_leave, near_arrive,
-        leave_even, arrive_even, leave_odd, arrive_odd, flag_vec, flag_sm, sem,
+        geo_all, far_leave, far_arrive, far_rep, near_pos, near_rep, near_leave, near_arrive,
+        even, odd, flag_rows,
     ) = scratch
     n_seg = n_old + n_new
     bands, width = held.shape[1] // 2 - GEO_ROWS // 2, held.shape[2]
@@ -99,30 +101,29 @@
         piece = held[k, geo_at : geo_at + GEO_ROWS, :].astype(jnp.float32)
         geo = (piece[0:8] + piece[8:16]) + piece[16:24]
         geo_all[k] = geo
-        flag_vec[k : k + 1, :] = geo[FLAG_ROW : FLAG_ROW + 1, 0:BLOCK].astype(jnp.int32)
-    flag_copy = pltpu.make_async_copy(flag_vec, flag_sm, sem)
-    flag_copy.start()
+        flag_rows[k] = geo[FLAG_ROW : FLAG_ROW + 1, 0:BLOCK]
     if n_old:
         sums[0:n_old] = old_sums[...]
     sums[n_old:n_seg] = jnp.zeros((n_new, bands, width), jnp.float32)
     tiles[n_pairs] = jnp.zeros((width, width), jnp.bfloat16)
     row = lax.broadcasted_iota(jnp.int32, (8, width), 0)
+    origin = jnp.broadcast_to(geo_all[0, :, 0:1], (8, width))
     for k in range(n_seg):
         geo = geo_all[k]
+        offset = jnp.where(row < 3, geo - origin, 0.0)
+        normal = jnp.where(row < 3, pltpu.roll(geo, 5, 0), 0.0)
+        along = jnp.sum(normal * offset, axis=0, keepdims=True)
         for c in range(3):
             far_rep[k, c] = jnp.broadcast_to(geo[c : c + 1], (8, width))
+        far_leave[k] = far_stack(jnp.where(row == 3, 1.0, offset))
+        far_arrive[k] = far_stack(jnp.where(row == 3, along, normal) * (-1.0 / math.pi))
         if k < n_old:
             continue
         at = k - n_old
         near_pos[at, :, 0:8] = jnp.transpose(geo)
-        middle = jnp.broadcast_to(geo[:, 0:1], (8, width))
-        centre[at] = middle
-        offset = jnp.where(row < 3, geo - middle, 0.0)
-        normal = jnp.where(row < 3, pltpu.roll(geo, 5, 0), 0.0)
-        along = jnp.sum(normal * offset, axis=0, keepdims=True)
         near_leave[at] = jnp.transpose(near_stack(jnp.where(row == 3, -along, normal))).astype(jnp.bfloat16)
         near_arrive[at] = jnp.transpose(near_stack(jnp.where(row == 3, 1.0, -offset))).astype(jnp.bfloat16)
-    flag_copy.wait()
+    lane = lax.broadcasted_iota(jnp.int32, (1, BLOCK), 1)
     col_mask = (1 << col_bits) - 1
 
     def pair_of(t):
@@ -140,38 +141,42 @@
         holder = (near & ~col_mask) | (far & col_mask)
         apart = near ^ far
         index = ((((apart & col_mask) << 1) | i) * n_far) + (((apart >> col_bits) << 1) | j)
-        return flag_sm[bit_reverse(holder >> (seg_bits - bits), bits), index]
-
-    def project(t, leave, arrive):
+        flags = flag_rows[bit_reverse(holder >> (seg_bits - bits), bits)]
+        return jnp.where(lane == index, flags, 0.0)
+
+    def project(t, cosines):
         local, near_at, far_at = pair_of(t)
-        geo = geo_all[far_at]
-        offset = jnp.where(row < 3, geo - centre[local], 0.0)
-        normal = jnp.where(row < 3, pltpu.roll(geo, 5, 0), 0.0) * (-1.0 / math.pi)
-        along = jnp.sum(normal * offset, axis=0, keepdims=True)
-        leave[...] = jnp.dot(
-            near_leave[local], far_stack(jnp.where(row == 3, 1.0, offset)),
-            preferred_element_type=jnp.float32,
-        )
-        arrive[...] = jnp.dot(
-            near_arrive[local], far_stack(jnp.where(row == 3, along, normal)),
-            preferred_element_type=jnp.float32,
-        )
-
-    def form(t, leave, arrive, fresh):
-        local, near_at, far_at = pair_of(t)
-        flags = [
-            [
-                (live(near_at, far_at, i, j) | live(far_at, near_at, j, i)).astype(jnp.float32)
+        masked = []
+        for i in range(halves):
+            flags = [
+                jnp.max(
+                    jnp.maximum(live(near_at, far_at, i, j), live(far_at, near_at, j, i)),
+                    axis=1, keepdims=True,
+                )
                 for j in range(halves)
             ]
-            for i in range(halves)
-        ]
+            flags = jnp.concatenate([jnp.broadcast_to(f, (PIECES, BLOCK)) for f in flags], axis=1)
+            masked.append(far_arrive[far_at] * flags.astype(jnp.bfloat16))
+        for at in range(0, width, CHUNK):
+            yield
+            rows = slice(at, at + CHUNK)
+            leaving = jnp.dot(
+                near_leave[local, rows], far_leave[far_at], preferred_element_type=jnp.float32
+            )
+            arriving = jnp.dot(
+                near_arrive[local, rows], masked[at // BLOCK], preferred_element_type=jnp.float32
+            )
+            cosines[rows] = jnp.maximum(leaving, 0.0) * jnp.maximum(arriving, 0.0)
+
+    def form(t, cosines, fresh):
+        local, near_at, far_at = pair_of(t)
         fars = [
             [far_rep[far_at, c, :, j * BLOCK : (j + 1) * BLOCK] for c in range(3)]
             for j in range(halves)
         ]
         for strip in range(width // 16):
-            i = strip * 16 // BLOCK
+            if strip * 16 % CHUNK == 0:
+                yield
             nears = []
             for part in range(2):
                 at = strip * 16 + part * 8
@@ -191,12 +196,10 @@
                     dx, dy, dz = (f - n for f, n in zip(fars[j], nears[part]))
                     spacing = dx * dx + dy * dy + dz * dz + SOFTEN
                     inverse = 1.0 / spacing
-                    product = jnp.maximum(leave[at : at + 8, cols], 0.0) * jnp.maximum(
-                        arrive[at : at + 8, cols], 0.0
-                    )
+                    product = cosines[at : at + 8, cols]
                     parts.append(product * inverse * inverse)
                 strip_now = jnp.concatenate(parts, axis=0).astype(jnp.bfloat16)
-                tiles[t, strip * 16 : strip * 16 + 16, cols] = strip_now * flags[i][j].astype(jnp.bfloat16)
+                tiles[t, strip * 16 : strip * 16 + 16, cols] = strip_now
 
     def apply(t):
         local, near_at, far_at = pair_of(t)
@@ -215,12 +218,12 @@
         for part, (now, later) in enumerate(((even, odd), (odd, even))):
             t = 2 * i + part
             apply(jnp.where(t == 0, n_pairs, t - 1))
-            project(t + 1, *later)
-            form(t, *now, fresh)
+            for _ in zip(project(t + 1, later), form(t, now, fresh), strict=True):
+                pass
         return carry
 
-    even, odd = (leave_even, arrive_even), (leave_odd, arrive_odd)
-    project(0, *even)
+    for _ in project(0, even):
+        pass
     lax.fori_loop(0, n_new // 2, functools.partial(two_steps, True), 0)
     lax.fori_loop(n_new // 2, n_pairs // 2, functools.partial(two_steps, False), 0)
     apply(n_pairs - 1)
@@ -255,7 +258,6 @@
         pltpu.VMEM((n_seg, bands, width), jnp.float32),
     ]
     outs = jax.ShapeDtypeStruct((bands, width), jnp.float32) if last else state[::-1]
-    pieces = 48
     work = n_pairs * width * width
     return pl.pallas_call(
         functools.partial(grow_kernel, n_old, n_new, bits, seg_bits, col_bits, n_far, last),
@@ -265,20 +267,19 @@
         scratch_shapes=(state + [pltpu.VMEM((n_seg, rows, width), jnp.bfloat16)] if last else [])
         + [
             pltpu.VMEM((n_seg, 8, width), jnp.float32),
-            pltpu.VMEM((n_new, 8, width), jnp.float32),
+            pltpu.VMEM((n_seg, PIECES, width), jnp.bfloat16),
+            pltpu.VMEM((n_seg, PIECES, width), jnp.bfloat16),
             pltpu.VMEM((n_seg, 3, 8, width), jnp.float32),
             pltpu.VMEM((n_new, width, BLOCK), jnp.float32),
             pltpu.VMEM((n_new, 3, width, BLOCK), jnp.float32),
-            pltpu.VMEM((n_new, width, pieces), jnp.bfloat16),
-            pltpu.VMEM((n_new, width, pieces), jnp.bfloat16),
-            *[pltpu.VMEM((width, width), jnp.float32)] * 4,
-            pltpu.VMEM((n_seg, BLOCK), jnp.int32),
-            pltpu.SMEM((n_seg, BLOCK), jnp.int32),
-            pltpu.SemaphoreType.DMA,
+            pltpu.VMEM((n_new, width, PIECES), jnp.bfloat16),
+            pltpu.VMEM((n_new, width, PIECES), jnp.bfloat16),
+            *[pltpu.VMEM((width, width), jnp.float32)] * 2,
+            pltpu.VMEM((n_seg, 1, BLOCK), jnp.float32),
         ],
         compiler_params=pltpu.CompilerParams(vmem_limit_bytes=32 * 1024 * 1024),
         cost_estimate=pl.CostEstimate(
-            flops=work * (4 * pieces + 4 * bands), bytes_accessed=n_seg * rows * width * 2, transcendentals=work
+            flops=work * (4 * PIECES + 4 * bands), bytes_accessed=n_seg * rows * width * 2, transcendentals=work
         ),
     )(*args)
 

time: 26.6 us -> 24.3 us (0.914)
  Pallas kernels: 14 us -> 11.7 us
    pallas_call x2, Pallas kernels: 13 us -> 10.7 us  [grow(): pl.pallas_call(functools.partial(grow_kernel, n_old, n_new, bits, seg_bit...]
  transfers between devices with their start and end apart: 4 -> 4, of which waited for: 2 -> 2; matrix products, arithmetic and copies ran while one was open for 0% -> 0% of each run, Pallas kernels for 15% -> 12%
where the time goes in v6:
time: 24.3 us; the launch traced here: 24.1 us
  Pallas kernels  11.7 us (48%)
  starting transfers between devices  7.65 us (31%)
  waiting for transfers between devices  4.7 us (19%)
    pallas_call x2, Pallas kernels, grow(): pl.pallas_call(functools.partial(grow_kernel, n_old, n_new, bits, seg_bit...  10.7 us
    ppermute x4, starting transfers between devices, swap(): lax.ppermute(value, ('row', 'col'), [(i, i ^ distance) for i in range(n_s...  7.65 us
    ppermute x4, waiting for transfers between devices, swap(): lax.ppermute(value, ('row', 'col'), [(i, i ^ distance) for i in range(n_s...  4.7 us
    pallas_call x1, Pallas kernels, one_exchange(): pl.pallas_call(functools.partial(pack_kernel, col_bits, n_far), out_shape...  1.03 us
  transfers between devices with their start and end apart: 4, of which 2 were waited for; matrix products, arithmetic and copies ran while one was open for 0% of the time, Pallas kernels for 12%

profile of v6, /device:TPU:0, one launch (start us, length us, event | category | flops | bytes accessed | tf_op | source)
XLA Modules:
  0.0 24.1 jit_solution(16147980337166315235)
XLA Ops:
  0.0 0.0 copy-start.1
  0.0 0.0 copy-start
  0.0 1.0 %shard_map.82 = bf16[96,256]{1,0:T(8,128)(2,1)S(1)} custom-call(f32[3,256]{1,0:T(4,128)} %pos.1, f32[3,256]{1,0:T(4,128)} %nrm.1, f32[1,256]{1,0:T(1,128)} %bitcast.5, f32[32,256]{1,0:T(8,128)} %refs_3_.1, f32[32,256]{1,0:T(8,128)} %refs_4_.1, s32[32]{0:T(128)} %prow.1, s32[32]{0:T(128)} %pcol.1, s32[32]{0:T(128)} %plive.1), custom_call_target="tpu_custom_call" | custom-call | tf_op jit(solution)/shard_map/pallas_call | solution.py:298
  1.0 4.1 %collective-permute-start = (bf16[1,96,256]{2,1,0:T(8,128)(2,1)S(1)}, bf16[1,96,256]{2,1,0:T(8,128)(2,1)S(1)}, u32[]{:S(2)}, u32[]{:S(2)}) collective-permute-start(bf16[1,96,256]{2,1,0:T(8,128)(2,1)S(1)} %bitcast.2), channel_id=1, source_target_pairs={{0,8},{2,10},{4,12},{6,14},{8,0},{10,2},{12,4},{14,6},{1,9},{3,11}... | collective-permute-start | bytes 147464 | tf_op jit(solution)/shard_map/ppermute | solution.py:307
  5.1 2.6 %collective-permute-done = bf16[1,96,256]{2,1,0:T(8,128)(2,1)S(1)} collective-permute-done((bf16[1,96,256]{2,1,0:T(8,128)(2,1)S(1)}, bf16[1,96,256]{2,1,0:T(8,128)(2,1)S(1)}, u32[]{:S(2)}, u32[]{:S(2)}) %collective-permute-start) | collective-permute-done | bytes 49184 | tf_op jit(solution)/shard_map/ppermute | solution.py:307
  7.7 1.4 %collective-permute-start.3 = (bf16[2,96,256]{2,1,0:T(8,128)(2,1)S(1)}, bf16[2,96,256]{2,1,0:T(8,128)(2,1)S(1)}, u32[]{:S(2)}, u32[]{:S(2)}) collective-permute-start(bf16[2,96,256]{2,1,0:T(8,128)(2,1)S(1)} %pad_maximum_fusion.1), channel_id=1, source_target_pairs={{0,4},{2,6},{4,0},{6,2},{8,12},{10,14},{12,8},{14,10},{1,5},{3,7},... | collective-permute-start | bytes 294920 | tf_op jit(solution)/shard_map/ppermute | solution.py:307
  9.2 1.5 %collective-permute-start.2 = (bf16[2,96,256]{2,1,0:T(8,128)(2,1)S(1)}, bf16[2,96,256]{2,1,0:T(8,128)(2,1)S(1)}, u32[]{:S(2)}, u32[]{:S(2)}) collective-permute-start(bf16[2,96,256]{2,1,0:T(8,128)(2,1)S(1)} %pad_maximum_fusion.1), channel_id=1, source_target_pairs={{0,2},{2,0},{4,6},{6,4},{8,10},{10,8},{12,14},{14,12},{1,3},{3,1},... | collective-permute-start | bytes 294920 | tf_op jit(solution)/shard_map/ppermute | solution.py:307
  10.7 0.6 %collective-permute-start.1 = (bf16[2,96,256]{2,1,0:T(8,128)(2,1)S(1)}, bf16[2,96,256]{2,1,0:T(8,128)(2,1)S(1)}, u32[]{:S(2)}, u32[]{:S(2)}) collective-permute-start(bf16[2,96,256]{2,1,0:T(8,128)(2,1)S(1)} %pad_maximum_fusion.1), channel_id=1, source_target_pairs={{0,6},{2,4},{4,2},{6,0},{8,14},{10,12},{12,10},{14,8},{1,7},{3,5},... | collective-permute-start | bytes 294920 | tf_op jit(solution)/shard_map/ppermute | solution.py:307
  11.3 2.1 %collective-permute-done.3 = bf16[2,96,256]{2,1,0:T(8,128)(2,1)S(1)} collective-permute-done((bf16[2,96,256]{2,1,0:T(8,128)(2,1)S(1)}, bf16[2,96,256]{2,1,0:T(8,128)(2,1)S(1)}, u32[]{:S(2)}, u32[]{:S(2)}) %collective-permute-start.3) | collective-permute-done | bytes 98336 | tf_op jit(solution)/shard_map/ppermute | solution.py:307
  13.4 3.0 %shard_map.83 = (f32[4,32,256]{2,1,0:T(8,128)S(1)}, bf16[11,256,256]{2,1,0:T(8,128)(2,1)S(1)}) custom-call(bf16[4,96,256]{2,1,0:T(8,128)(2,1)S(1)} %pad_maximum_fusion.refs_0_.refs_2_), custom_call_target="tpu_custom_call" | custom-call | flops 209715200 | bytes 196608 | tf_op jit(solution)/shard_map/pallas_call | solution.py:262
  16.4 0.0 collective-permute-done.2.refs_1_
  16.5 0.0 collective-permute-done.1.refs_0_
  16.5 0.0 copy-done.1
  16.5 0.0 copy-done
  16.5 7.7 %shard_map.84 = f32[32,256]{1,0:T(8,128)} custom-call(bf16[2,96,256]{2,1,0:T(8,128)(2,1)S(1)} %collective-permute-done.1.refs_0_, bf16[2,96,256]{2,1,0:T(8,128)(2,1)S(1)} %collective-permute-done.2.refs_1_, bf16[4,96,256]{2,1,0:T(8,128)(2,1)S(1)} %pad_maximum_fusion.refs_0_.refs_2_, f32[32,256]{1,0:T(8,128)S(1)} %copy-done, f32[32,256]{1,0:T(8,128)S(1)} %copy-done.1, ...), custom_call_target="tpu_custom_call" | custom-call | flops 545259520 | bytes 393216 | tf_op jit(solution)/shard_map/pallas_call | solution.py:262
  (2 shorter events, 0.0 us)
Async XLA Ops:
  0.0 16.5 %copy-start.1 = (f32[32,256]{1,0:T(8,128)S(1)}, f32[32,256]{1,0:T(8,128)}, u32[]{:S(2)}) copy-start(f32[32,256]{1,0:T(8,128)} %refs_4_.1) | copy-start | bytes 98308
  0.0 16.5 %copy-start = (f32[32,256]{1,0:T(8,128)S(1)}, f32[32,256]{1,0:T(8,128)}, u32[]{:S(2)}) copy-start(f32[32,256]{1,0:T(8,128)} %refs_3_.1) | copy-start | bytes 98308
  1.0 6.7 %collective-permute-start = (bf16[1,96,256]{2,1,0:T(8,128)(2,1)S(1)}, bf16[1,96,256]{2,1,0:T(8,128)(2,1)S(1)}, u32[]{:S(2)}, u32[]{:S(2)}) collective-permute-start(bf16[1,96,256]{2,1,0:T(8,128)(2,1)S(1)} %bitcast.2), channel_id=1, source_target_pairs={{0,8},{2,10},{4,12},{6,14},{8,0},{10,2},{12,4},{14,6},{1,9},{3,11}... | collective-permute-start | bytes 147464 | tf_op jit(solution)/shard_map/ppermute | solution.py:307
  7.7 5.6 %collective-permute-start.3 = (bf16[2,96,256]{2,1,0:T(8,128)(2,1)S(1)}, bf16[2,96,256]{2,1,0:T(8,128)(2,1)S(1)}, u32[]{:S(2)}, u32[]{:S(2)}) collective-permute-start(bf16[2,96,256]{2,1,0:T(8,128)(2,1)S(1)} %pad_maximum_fusion.1), channel_id=1, source_target_pairs={{0,4},{2,6},{4,0},{6,2},{8,12},{10,14},{12,8},{14,10},{1,5},{3,7},... | collective-permute-start | bytes 294920 | tf_op jit(solution)/shard_map/ppermute | solution.py:307
  9.2 7.3 %collective-permute-start.2 = (bf16[2,96,256]{2,1,0:T(8,128)(2,1)S(1)}, bf16[2,96,256]{2,1,0:T(8,128)(2,1)S(1)}, u32[]{:S(2)}, u32[]{:S(2)}) collective-permute-start(bf16[2,96,256]{2,1,0:T(8,128)(2,1)S(1)} %pad_maximum_fusion.1), channel_id=1, source_target_pairs={{0,2},{2,0},{4,6},{6,4},{8,10},{10,8},{12,14},{14,12},{1,3},{3,1},... | collective-permute-start | bytes 294920 | tf_op jit(solution)/shard_map/ppermute | solution.py:307
  10.7 5.8 %collective-permute-start.1 = (bf16[2,96,256]{2,1,0:T(8,128)(2,1)S(1)}, bf16[2,96,256]{2,1,0:T(8,128)(2,1)S(1)}, u32[]{:S(2)}, u32[]{:S(2)}) collective-permute-start(bf16[2,96,256]{2,1,0:T(8,128)(2,1)S(1)} %pad_maximum_fusion.1), channel_id=1, source_target_pairs={{0,6},{2,4},{4,2},{6,0},{8,14},{10,12},{12,10},{14,8},{1,7},{3,5},... | collective-permute-start | bytes 294920 | tf_op jit(solution)/shard_map/ppermute | solution.py:307

commit v7 on v6

--- a/solution.py
+++ b/solution.py
@@ -78,13 +78,18 @@
     return (count - k) * count + k, 0
 
 
-def grow_kernel(n_old, n_new, bits, seg_bits, col_bits, n_far, last, *refs):
+def grow_kernel(levels, seg_bits, col_bits, n_far, last, *refs):
+    n_old, n_new = levels[-1]
+    bits = (n_old + n_new).bit_length() - 1
     if last:
-        diagonal, across, known, emi, ref, old_sums, old_tiles, out, tiles, sums, held, *scratch = refs
+        diagonal, across, known, emi, ref, old_sums, *refs = refs
+        old_tiles, (out, tiles, sums, held, *scratch) = refs[: len(levels) - 1], refs[len(levels) - 1 :]
         at = 0
         for part in (known, across, diagonal):
             held[at : at + part.shape[0]] = part[...]
             at += part.shape[0]
+    elif n_old:
+        held, old_sums, sums, tiles, *scratch = refs
     else:
         held, sums, tiles, *scratch = refs
     (
@@ -225,8 +230,9 @@
     for _ in project(0, even):
         pass
     lax.fori_loop(0, n_new // 2, functools.partial(two_steps, True), 0)
-    lax.fori_loop(n_new // 2, n_pairs // 2, functools.partial(two_steps, False), 0)
-    apply(n_pairs - 1)
+    lax.fori_loop(n_new // 2, (n_pairs + 1) // 2, functools.partial(two_steps, False), 0)
+    if n_pairs % 2 == 0:
+        apply(n_pairs - 1)
     if not last:
         return
     total = jnp.zeros((bands, width), jnp.float32)
@@ -234,23 +240,22 @@
         base = held[k, 0:bands, :].astype(jnp.float32)
         gain = held[k, bands : 2 * bands, :].astype(jnp.float32)
         weighted = (base + gain * sums[k]).astype(jnp.bfloat16)
-        if k < n_old:
-            t, over = own_tile(k, n_old)
-            tile = old_tiles[t]
-        else:
-            tile, over = tiles[n_tri + k - n_old], 0
+        level = next(i for i, (old, new) in enumerate(levels) if k < old + new)
+        old, new = levels[level]
+        t, over = (triangle(new) + k - old, 0) if old else own_tile(k, new)
+        tile = tiles[t] if k >= n_old else old_tiles[level][t]
         total += lax.dot_general(
             weighted, tile, (((1,), (over,)), ((), ())), preferred_element_type=jnp.float32
         )
     out[...] = emi[...] + ref[...] * total
 
 
-def grow(n_old, n_new, seg_bits, col_bits, n_far, args):
+def grow(levels, seg_bits, col_bits, n_far, args):
+    n_old, n_new = levels[-1]
     rows, width = args[0].shape[1:]
     bands = (rows - GEO_ROWS) // 2
     n_seg = n_old + n_new
-    bits = n_seg.bit_length() - 1
-    last = bits == seg_bits
+    last = n_seg == 1 << seg_bits
     n_pairs = triangle(n_new) + n_new * n_old
     vmem = pl.BlockSpec(memory_space=pltpu.VMEM)
     state = [
@@ -260,7 +265,7 @@
     outs = jax.ShapeDtypeStruct((bands, width), jnp.float32) if last else state[::-1]
     work = n_pairs * width * width
     return pl.pallas_call(
-        functools.partial(grow_kernel, n_old, n_new, bits, seg_bits, col_bits, n_far, last),
+        functools.partial(grow_kernel, levels, seg_bits, col_bits, n_far, last),
         out_shape=outs,
         in_specs=[vmem] * len(args),
         out_specs=vmem if last else [vmem, vmem],
@@ -309,11 +314,13 @@
     for bit in reversed(range(2, seg_bits)):
         gathered = jnp.concatenate([gathered, swap(gathered, 1 << bit)])
     beside, across, diagonal = (swap(gathered, distance) for distance in (2, 1, 3))
+    quarter, half = n_seg // 4, n_seg // 2
+    levels = ((0, quarter), (quarter, quarter), (half, half))
+    sums, tiles = grow(levels[:1], seg_bits, col_bits, n_far, (gathered,))
     gathered = jnp.concatenate([gathered, beside])
-    state = grow(0, n_seg // 2, seg_bits, col_bits, n_far, (gathered,))
-    half = n_seg // 2
-    args = (diagonal, across, gathered, emission, reflect, *state)
-    return grow(half, half, seg_bits, col_bits, n_far, args)
+    sums, more_tiles = grow(levels[:2], seg_bits, col_bits, n_far, (gathered, sums))
+    args = (diagonal, across, gathered, emission, reflect, sums, tiles, more_tiles)
+    return grow(levels, seg_bits, col_bits, n_far, args)
 
 
 def form_tiles(near, far):

time: 24.3 us -> 24 us (0.988)
  waiting for transfers between devices: 4.7 us -> 4.02 us
  Pallas kernels: 11.7 us -> 12 us
    ppermute x4, waiting for transfers between devices: 4.7 us -> 4.02 us  [swap(): lax.ppermute(value, ('row', 'col'), [(i, i ^ distance) for i in range(n_s...]
    pallas_call x2 -> x3, Pallas kernels: 10.7 us -> 11 us  [grow(): pl.pallas_call(functools.partial(grow_kernel, levels, seg_bits, col_bits,...]
  transfers between devices with their start and end apart: 4 -> 4, of which waited for: 2 -> 3; matrix products, arithmetic and copies ran while one was open for 0% -> 0% of each run, Pallas kernels for 12% -> 14%
where the time goes in v7:
time: 24 us; the launch traced here: 23.8 us
  Pallas kernels  12 us (50%)
  starting transfers between devices  7.65 us (32%)
  waiting for transfers between devices  4.02 us (17%)
    pallas_call x3, Pallas kernels, grow(): pl.pallas_call(functools.partial(grow_kernel, levels, seg_bits, col_bits,...  11 us
    ppermute x4, starting transfers between devices, swap(): lax.ppermute(value, ('row', 'col'), [(i, i ^ distance) for i in range(n_s...  7.65 us
    ppermute x4, waiting for transfers between devices, swap(): lax.ppermute(value, ('row', 'col'), [(i, i ^ distance) for i in range(n_s...  4.02 us
    pallas_call x1, Pallas kernels, one_exchange(): pl.pallas_call(functools.partial(pack_kernel, col_bits, n_far), out_shape...  1.02 us
  transfers between devices with their start and end apart: 4, of which 3 were waited for; matrix products, arithmetic and copies ran while one was open for 0% of the time, Pallas kernels for 14%

profile of v7, /device:TPU:0, one launch (start us, length us, event | category | flops | bytes accessed | tf_op | source)
XLA Modules:
  0.0 23.8 jit_solution(10832413873036124211)
XLA Ops:
  0.0 1.0 %shard_map.82 = bf16[96,256]{1,0:T(8,128)(2,1)S(1)} custom-call(f32[3,256]{1,0:T(4,128)} %pos.1, f32[3,256]{1,0:T(4,128)} %nrm.1, f32[1,256]{1,0:T(1,128)} %bitcast.5, f32[32,256]{1,0:T(8,128)} %refs_3_.1, f32[32,256]{1,0:T(8,128)} %refs_4_.1, s32[32]{0:T(128)} %prow.1, s32[32]{0:T(128)} %pcol.1, s32[32]{0:T(128)} %plive.1), custom_call_target="tpu_custom_call" | custom-call | tf_op jit(solution)/shard_map/pallas_call | solution.py:303
  1.0 4.1 %collective-permute-start = (bf16[1,96,256]{2,1,0:T(8,128)(2,1)S(1)}, bf16[1,96,256]{2,1,0:T(8,128)(2,1)S(1)}, u32[]{:S(2)}, u32[]{:S(2)}) collective-permute-start(bf16[1,96,256]{2,1,0:T(8,128)(2,1)S(1)} %bitcast.2), channel_id=1, source_target_pairs={{0,8},{2,10},{4,12},{6,14},{8,0},{10,2},{12,4},{14,6},{1,9},{3,11}... | collective-permute-start | bytes 147464 | tf_op jit(solution)/shard_map/ppermute | solution.py:312
  5.1 2.6 %collective-permute-done = bf16[1,96,256]{2,1,0:T(8,128)(2,1)S(1)} collective-permute-done((bf16[1,96,256]{2,1,0:T(8,128)(2,1)S(1)}, bf16[1,96,256]{2,1,0:T(8,128)(2,1)S(1)}, u32[]{:S(2)}, u32[]{:S(2)}) %collective-permute-start) | collective-permute-done | bytes 49184 | tf_op jit(solution)/shard_map/ppermute | solution.py:312
  7.7 1.4 %collective-permute-start.3 = (bf16[2,96,256]{2,1,0:T(8,128)(2,1)S(1)}, bf16[2,96,256]{2,1,0:T(8,128)(2,1)S(1)}, u32[]{:S(2)}, u32[]{:S(2)}) collective-permute-start(bf16[2,96,256]{2,1,0:T(8,128)(2,1)S(1)} %pad_maximum_fusion.1.refs_0_), channel_id=1, source_target_pairs={{0,4},{2,6},{4,0},{6,2},{8,12},{10,14},{12,8},{14,10},{1,5},{3,7},... | collective-permute-start | bytes 294920 | tf_op jit(solution)/shard_map/ppermute | solution.py:312
  9.2 1.5 %collective-permute-start.2 = (bf16[2,96,256]{2,1,0:T(8,128)(2,1)S(1)}, bf16[2,96,256]{2,1,0:T(8,128)(2,1)S(1)}, u32[]{:S(2)}, u32[]{:S(2)}) collective-permute-start(bf16[2,96,256]{2,1,0:T(8,128)(2,1)S(1)} %pad_maximum_fusion.1.refs_0_), channel_id=1, source_target_pairs={{0,2},{2,0},{4,6},{6,4},{8,10},{10,8},{12,14},{14,12},{1,3},{3,1},... | collective-permute-start | bytes 294920 | tf_op jit(solution)/shard_map/ppermute | solution.py:312
  10.7 0.6 %collective-permute-start.1 = (bf16[2,96,256]{2,1,0:T(8,128)(2,1)S(1)}, bf16[2,96,256]{2,1,0:T(8,128)(2,1)S(1)}, u32[]{:S(2)}, u32[]{:S(2)}) collective-permute-start(bf16[2,96,256]{2,1,0:T(8,128)(2,1)S(1)} %pad_maximum_fusion.1.refs_0_), channel_id=1, source_target_pairs={{0,6},{2,4},{4,2},{6,0},{8,14},{10,12},{12,10},{14,8},{1,7},{3,5},... | collective-permute-start | bytes 294920 | tf_op jit(solution)/shard_map/ppermute | solution.py:312
  11.3 1.2 %shard_map.83 = (f32[2,32,256]{2,1,0:T(8,128)S(1)}, bf16[4,256,256]{2,1,0:T(8,128)(2,1)S(1)}) custom-call(bf16[2,96,256]{2,1,0:T(8,128)(2,1)S(1)} %pad_maximum_fusion.1.refs_0_), custom_call_target="tpu_custom_call" | custom-call | flops 62914560 | bytes 98304 | tf_op jit(solution)/shard_map/pallas_call | solution.py:267
  12.5 0.9 %collective-permute-done.3 = bf16[2,96,256]{2,1,0:T(8,128)(2,1)S(1)} collective-permute-done((bf16[2,96,256]{2,1,0:T(8,128)(2,1)S(1)}, bf16[2,96,256]{2,1,0:T(8,128)(2,1)S(1)}, u32[]{:S(2)}, u32[]{:S(2)}) %collective-permute-start.3) | collective-permute-done | bytes 98336 | tf_op jit(solution)/shard_map/ppermute | solution.py:312
  13.4 0.0 copy-start
  13.4 0.0 copy-start.1
  13.4 2.2 %shard_map.84 = (f32[4,32,256]{2,1,0:T(8,128)S(1)}, bf16[8,256,256]{2,1,0:T(8,128)(2,1)S(1)}) custom-call(bf16[4,96,256]{2,1,0:T(8,128)(2,1)S(1)} %pad_maximum_fusion.refs_0_.refs_2_, f32[2,32,256]{2,1,0:T(8,128)S(1)} %get-tuple-element.9.refs_1_), custom_call_target="tpu_custom_call" | custom-call | flops 146800640 | bytes 196608 | tf_op jit(solution)/shard_map/pallas_call | solution.py:267
  15.6 0.0 collective-permute-done.2.refs_1_
  15.6 0.5 %collective-permute-done.1.refs_0_ = bf16[2,96,256]{2,1,0:T(8,128)(2,1)S(1)} collective-permute-done((bf16[2,96,256]{2,1,0:T(8,128)(2,1)S(1)}, bf16[2,96,256]{2,1,0:T(8,128)(2,1)S(1)}, u32[]{:S(2)}, u32[]{:S(2)}) %collective-permute-start.1) | collective-permute-done | bytes 98336 | tf_op jit(solution)/shard_map/ppermute | solution.py:312
  16.2 0.0 copy-done
  16.2 0.0 copy-done.1
  16.2 7.6 %shard_map.85 = f32[32,256]{1,0:T(8,128)} custom-call(bf16[2,96,256]{2,1,0:T(8,128)(2,1)S(1)} %collective-permute-done.1.refs_0_, bf16[2,96,256]{2,1,0:T(8,128)(2,1)S(1)} %collective-permute-done.2.refs_1_, bf16[4,96,256]{2,1,0:T(8,128)(2,1)S(1)} %pad_maximum_fusion.refs_0_.refs_2_, f32[32,256]{1,0:T(8,128)S(1)} %copy-done, f32[32,256]{1,0:T(8,128)S(1)} %copy-done.1, ...), custom_call_target="tpu_custom_call" | custom-call | flops 545259520 | bytes 393216 | tf_op jit(solution)/shard_map/pallas_call | solution.py:267
  (2 shorter events, 0.0 us)
Async XLA Ops:
  1.0 6.7 %collective-permute-start = (bf16[1,96,256]{2,1,0:T(8,128)(2,1)S(1)}, bf16[1,96,256]{2,1,0:T(8,128)(2,1)S(1)}, u32[]{:S(2)}, u32[]{:S(2)}) collective-permute-start(bf16[1,96,256]{2,1,0:T(8,128)(2,1)S(1)} %bitcast.2), channel_id=1, source_target_pairs={{0,8},{2,10},{4,12},{6,14},{8,0},{10,2},{12,4},{14,6},{1,9},{3,11}... | collective-permute-start | bytes 147464 | tf_op jit(solution)/shard_map/ppermute | solution.py:312
  7.7 5.6 %collective-permute-start.3 = (bf16[2,96,256]{2,1,0:T(8,128)(2,1)S(1)}, bf16[2,96,256]{2,1,0:T(8,128)(2,1)S(1)}, u32[]{:S(2)}, u32[]{:S(2)}) collective-permute-start(bf16[2,96,256]{2,1,0:T(8,128)(2,1)S(1)} %pad_maximum_fusion.1.refs_0_), channel_id=1, source_target_pairs={{0,4},{2,6},{4,0},{6,2},{8,12},{10,14},{12,8},{14,10},{1,5},{3,7},... | collective-permute-start | bytes 294920 | tf_op jit(solution)/shard_map/ppermute | solution.py:312
  9.2 6.5 %collective-permute-start.2 = (bf16[2,96,256]{2,1,0:T(8,128)(2,1)S(1)}, bf16[2,96,256]{2,1,0:T(8,128)(2,1)S(1)}, u32[]{:S(2)}, u32[]{:S(2)}) collective-permute-start(bf16[2,96,256]{2,1,0:T(8,128)(2,1)S(1)} %pad_maximum_fusion.1.refs_0_), channel_id=1, source_target_pairs={{0,2},{2,0},{4,6},{6,4},{8,10},{10,8},{12,14},{14,12},{1,3},{3,1},... | collective-permute-start | bytes 294920 | tf_op jit(solution)/shard_map/ppermute | solution.py:312
  10.7 5.5 %collective-permute-start.1 = (bf16[2,96,256]{2,1,0:T(8,128)(2,1)S(1)}, bf16[2,96,256]{2,1,0:T(8,128)(2,1)S(1)}, u32[]{:S(2)}, u32[]{:S(2)}) collective-permute-start(bf16[2,96,256]{2,1,0:T(8,128)(2,1)S(1)} %pad_maximum_fusion.1.refs_0_), channel_id=1, source_target_pairs={{0,6},{2,4},{4,2},{6,0},{8,14},{10,12},{12,10},{14,8},{1,7},{3,5},... | collective-permute-start | bytes 294920 | tf_op jit(solution)/shard_map/ppermute | solution.py:312
  13.4 2.8 %copy-start = (f32[32,256]{1,0:T(8,128)S(1)}, f32[32,256]{1,0:T(8,128)}, u32[]{:S(2)}) copy-start(f32[32,256]{1,0:T(8,128)} %refs_3_.1) | copy-start | bytes 98308
  13.4 2.8 %copy-start.1 = (f32[32,256]{1,0:T(8,128)S(1)}, f32[32,256]{1,0:T(8,128)}, u32[]{:S(2)}) copy-start(f32[32,256]{1,0:T(8,128)} %refs_4_.1) | copy-start | bytes 98308

commit v8 on v7

--- a/solution.py
+++ b/solution.py
@@ -1,4 +1,5 @@
 import functools
+import itertools
 import math
 
 import jax
@@ -110,7 +111,6 @@
     if n_old:
         sums[0:n_old] = old_sums[...]
     sums[n_old:n_seg] = jnp.zeros((n_new, bands, width), jnp.float32)
-    tiles[n_pairs] = jnp.zeros((width, width), jnp.bfloat16)
     row = lax.broadcasted_iota(jnp.int32, (8, width), 0)
     origin = jnp.broadcast_to(geo_all[0, :, 0:1], (8, width))
     for k in range(n_seg):
@@ -128,16 +128,14 @@
         near_pos[at, :, 0:8] = jnp.transpose(geo)
         near_leave[at] = jnp.transpose(near_stack(jnp.where(row == 3, -along, normal))).astype(jnp.bfloat16)
         near_arrive[at] = jnp.transpose(near_stack(jnp.where(row == 3, 1.0, -offset))).astype(jnp.bfloat16)
-    lane = lax.broadcasted_iota(jnp.int32, (1, BLOCK), 1)
     col_mask = (1 << col_bits) - 1
 
     def pair_of(t):
-        t = jnp.int32(t)
-        near = t % n_new
-        far = (near + t // n_new) % n_new + n_old
-        if n_old:
-            far = jnp.where(t < n_tri, far, jnp.minimum((t - n_tri) // n_new, n_old - 1))
-            near = jnp.where(t < n_tri, near, (t - n_tri) % n_new)
+        if t >= n_tri:
+            near, far = (t - n_tri) % n_new, (t - n_tri) // n_new
+        else:
+            near = t % n_new
+            far = (near + t // n_new) % n_new + n_old
         return near, near + n_old, far
 
     def live(near_at, far_at, i, j):
@@ -146,18 +144,15 @@
         holder = (near & ~col_mask) | (far & col_mask)
         apart = near ^ far
         index = ((((apart & col_mask) << 1) | i) * n_far) + (((apart >> col_bits) << 1) | j)
-        flags = flag_rows[bit_reverse(holder >> (seg_bits - bits), bits)]
-        return jnp.where(lane == index, flags, 0.0)
+        held_at = bit_reverse(holder >> (seg_bits - bits), bits)
+        return flag_rows[held_at, :, index : index + 1]
 
     def project(t, cosines):
         local, near_at, far_at = pair_of(t)
         masked = []
         for i in range(halves):
             flags = [
-                jnp.max(
-                    jnp.maximum(live(near_at, far_at, i, j), live(far_at, near_at, j, i)),
-                    axis=1, keepdims=True,
-                )
+                jnp.maximum(live(near_at, far_at, i, j), live(far_at, near_at, j, i))
                 for j in range(halves)
             ]
             flags = jnp.concatenate([jnp.broadcast_to(f, (PIECES, BLOCK)) for f in flags], axis=1)
@@ -212,27 +207,23 @@
         to_near = lax.dot_general(
             held[far_at, 0:bands, :], tile, (((1,), (1,)), ((), ())), preferred_element_type=jnp.float32
         )
-        to_far = lax.dot_general(
-            held[near_at, 0:bands, :], tile, (((1,), (0,)), ((), ())), preferred_element_type=jnp.float32
-        )
         sums[near_at] = sums[near_at] + to_near
-        mirrored = (near_at != far_at).astype(jnp.float32)
-        sums[far_at] = sums[far_at] + to_far * mirrored
-
-    def two_steps(fresh, i, carry):
-        for part, (now, later) in enumerate(((even, odd), (odd, even))):
-            t = 2 * i + part
-            apply(jnp.where(t == 0, n_pairs, t - 1))
-            for _ in zip(project(t + 1, later), form(t, now, fresh), strict=True):
-                pass
-        return carry
-
+        if near_at != far_at:
+            to_far = lax.dot_general(
+                held[near_at, 0:bands, :], tile, (((1,), (0,)), ((), ())), preferred_element_type=jnp.float32
+            )
+            sums[far_at] = sums[far_at] + to_far
+
+    cosines = (even, odd)
     for _ in project(0, even):
         pass
-    lax.fori_loop(0, n_new // 2, functools.partial(two_steps, True), 0)
-    lax.fori_loop(n_new // 2, (n_pairs + 1) // 2, functools.partial(two_steps, False), 0)
-    if n_pairs % 2 == 0:
-        apply(n_pairs - 1)
+    for t in range(n_pairs):
+        later = project(t + 1, cosines[(t + 1) % 2]) if t + 1 < n_pairs else ()
+        for _ in itertools.zip_longest(later, form(t, cosines[t % 2], t < n_new)):
+            pass
+        if t:
+            apply(t - 1)
+    apply(n_pairs - 1)
     if not last:
         return
     total = jnp.zeros((bands, width), jnp.float32)
@@ -259,7 +250,7 @@
     n_pairs = triangle(n_new) + n_new * n_old
     vmem = pl.BlockSpec(memory_space=pltpu.VMEM)
     state = [
-        pltpu.VMEM((n_pairs + 1, width, width), jnp.bfloat16),
+        pltpu.VMEM((n_pairs, width, width), jnp.bfloat16),
         pltpu.VMEM((n_seg, bands, width), jnp.float32),
     ]
     outs = jax.ShapeDtypeStruct((bands, width), jnp.float32) if last else state[::-1]

time: 24 us -> 22.3 us (0.929)
  Pallas kernels: 12 us -> 9.78 us
  waiting for transfers between devices: 4.02 us -> 4.61 us
    pallas_call x3, Pallas kernels: 11 us -> 8.76 us  [grow(): pl.pallas_call(functools.partial(grow_kernel, levels, seg_bits, col_bits,...]
    ppermute x4, waiting for transfers between devices: 4.02 us -> 4.61 us  [swap(): lax.ppermute(value, ('row', 'col'), [(i, i ^ distance) for i in range(n_s...]
  transfers between devices with their start and end apart: 4 -> 4, of which waited for: 3 -> 3; matrix products, arithmetic and copies ran while one was open for 0% -> 0% of each run, Pallas kernels for 14% -> 13%
where the time goes in v8:
time: 22.3 us; the launch traced here: 22.1 us
  Pallas kernels  9.78 us (44%)
  starting transfers between devices  7.65 us (34%)
  waiting for transfers between devices  4.61 us (21%)
    pallas_call x3, Pallas kernels, grow(): pl.pallas_call(functools.partial(grow_kernel, levels, seg_bits, col_bits,...  8.76 us
    ppermute x4, starting transfers between devices, swap(): lax.ppermute(value, ('row', 'col'), [(i, i ^ distance) for i in range(n_s...  7.65 us
    ppermute x4, waiting for transfers between devices, swap(): lax.ppermute(value, ('row', 'col'), [(i, i ^ distance) for i in range(n_s...  4.61 us
    pallas_call x1, Pallas kernels, one_exchange(): pl.pallas_call(functools.partial(pack_kernel, col_bits, n_far), out_shape...  1.02 us
  transfers between devices with their start and end apart: 4, of which 3 were waited for; matrix products, arithmetic and copies ran while one was open for 0% of the time, Pallas kernels for 13%

profile of v8, /device:TPU:0, one launch (start us, length us, event | category | flops | bytes accessed | tf_op | source)
XLA Modules:
  0.0 22.1 jit_solution(7516496609296052195)
XLA Ops:
  0.0 1.0 %shard_map.82 = bf16[96,256]{1,0:T(8,128)(2,1)S(1)} custom-call(f32[3,256]{1,0:T(4,128)} %pos.1, f32[3,256]{1,0:T(4,128)} %nrm.1, f32[1,256]{1,0:T(1,128)} %bitcast.5, f32[32,256]{1,0:T(8,128)} %refs_3_.1, f32[32,256]{1,0:T(8,128)} %refs_4_.1, s32[32]{0:T(128)} %prow.1, s32[32]{0:T(128)} %pcol.1, s32[32]{0:T(128)} %plive.1), custom_call_target="tpu_custom_call" | custom-call | tf_op jit(solution)/shard_map/pallas_call | solution.py:294
  1.0 4.1 %collective-permute-start = (bf16[1,96,256]{2,1,0:T(8,128)(2,1)S(1)}, bf16[1,96,256]{2,1,0:T(8,128)(2,1)S(1)}, u32[]{:S(2)}, u32[]{:S(2)}) collective-permute-start(bf16[1,96,256]{2,1,0:T(8,128)(2,1)S(1)} %bitcast.2), channel_id=1, source_target_pairs={{0,8},{2,10},{4,12},{6,14},{8,0},{10,2},{12,4},{14,6},{1,9},{3,11}... | collective-permute-start | bytes 147464 | tf_op jit(solution)/shard_map/ppermute | solution.py:303
  5.1 2.6 %collective-permute-done = bf16[1,96,256]{2,1,0:T(8,128)(2,1)S(1)} collective-permute-done((bf16[1,96,256]{2,1,0:T(8,128)(2,1)S(1)}, bf16[1,96,256]{2,1,0:T(8,128)(2,1)S(1)}, u32[]{:S(2)}, u32[]{:S(2)}) %collective-permute-start) | collective-permute-done | bytes 49184 | tf_op jit(solution)/shard_map/ppermute | solution.py:303
  7.7 1.4 %collective-permute-start.3 = (bf16[2,96,256]{2,1,0:T(8,128)(2,1)S(1)}, bf16[2,96,256]{2,1,0:T(8,128)(2,1)S(1)}, u32[]{:S(2)}, u32[]{:S(2)}) collective-permute-start(bf16[2,96,256]{2,1,0:T(8,128)(2,1)S(1)} %pad_maximum_fusion.1.refs_0_), channel_id=1, source_target_pairs={{0,4},{2,6},{4,0},{6,2},{8,12},{10,14},{12,8},{14,10},{1,5},{3,7},... | collective-permute-start | bytes 294920 | tf_op jit(solution)/shard_map/ppermute | solution.py:303
  9.2 1.5 %collective-permute-start.2 = (bf16[2,96,256]{2,1,0:T(8,128)(2,1)S(1)}, bf16[2,96,256]{2,1,0:T(8,128)(2,1)S(1)}, u32[]{:S(2)}, u32[]{:S(2)}) collective-permute-start(bf16[2,96,256]{2,1,0:T(8,128)(2,1)S(1)} %pad_maximum_fusion.1.refs_0_), channel_id=1, source_target_pairs={{0,2},{2,0},{4,6},{6,4},{8,10},{10,8},{12,14},{14,12},{1,3},{3,1},... | collective-permute-start | bytes 294920 | tf_op jit(solution)/shard_map/ppermute | solution.py:303
  10.7 0.6 %collective-permute-start.1 = (bf16[2,96,256]{2,1,0:T(8,128)(2,1)S(1)}, bf16[2,96,256]{2,1,0:T(8,128)(2,1)S(1)}, u32[]{:S(2)}, u32[]{:S(2)}) collective-permute-start(bf16[2,96,256]{2,1,0:T(8,128)(2,1)S(1)} %pad_maximum_fusion.1.refs_0_), channel_id=1, source_target_pairs={{0,6},{2,4},{4,2},{6,0},{8,14},{10,12},{12,10},{14,8},{1,7},{3,5},... | collective-permute-start | bytes 294920 | tf_op jit(solution)/shard_map/ppermute | solution.py:303
  11.3 1.1 %shard_map.83 = (f32[2,32,256]{2,1,0:T(8,128)S(1)}, bf16[3,256,256]{2,1,0:T(8,128)(2,1)S(1)}) custom-call(bf16[2,96,256]{2,1,0:T(8,128)(2,1)S(1)} %pad_maximum_fusion.1.refs_0_), custom_call_target="tpu_custom_call" | custom-call | flops 62914560 | bytes 98304 | tf_op jit(solution)/shard_map/pallas_call | solution.py:258
  12.4 1.0 %collective-permute-done.3 = bf16[2,96,256]{2,1,0:T(8,128)(2,1)S(1)} collective-permute-done((bf16[2,96,256]{2,1,0:T(8,128)(2,1)S(1)}, bf16[2,96,256]{2,1,0:T(8,128)(2,1)S(1)}, u32[]{:S(2)}, u32[]{:S(2)}) %collective-permute-start.3) | collective-permute-done | bytes 98336 | tf_op jit(solution)/shard_map/ppermute | solution.py:303
  13.4 0.0 copy-start
  13.4 0.0 copy-start.1
  13.4 1.7 %shard_map.84 = (f32[4,32,256]{2,1,0:T(8,128)S(1)}, bf16[7,256,256]{2,1,0:T(8,128)(2,1)S(1)}) custom-call(bf16[4,96,256]{2,1,0:T(8,128)(2,1)S(1)} %pad_maximum_fusion.refs_0_.refs_2_, f32[2,32,256]{2,1,0:T(8,128)S(1)} %get-tuple-element.9.refs_1_), custom_call_target="tpu_custom_call" | custom-call | flops 146800640 | bytes 196608 | tf_op jit(solution)/shard_map/pallas_call | solution.py:258
  15.2 0.0 collective-permute-done.2.refs_1_
  15.2 1.0 %collective-permute-done.1.refs_0_ = bf16[2,96,256]{2,1,0:T(8,128)(2,1)S(1)} collective-permute-done((bf16[2,96,256]{2,1,0:T(8,128)(2,1)S(1)}, bf16[2,96,256]{2,1,0:T(8,128)(2,1)S(1)}, u32[]{:S(2)}, u32[]{:S(2)}) %collective-permute-start.1) | collective-permute-done | bytes 98336 | tf_op jit(solution)/shard_map/ppermute | solution.py:303
  16.2 0.0 copy-done
  16.2 0.0 copy-done.1
  16.2 5.9 %shard_map.85 = f32[32,256]{1,0:T(8,128)} custom-call(bf16[2,96,256]{2,1,0:T(8,128)(2,1)S(1)} %collective-permute-done.1.refs_0_, bf16[2,96,256]{2,1,0:T(8,128)(2,1)S(1)} %collective-permute-done.2.refs_1_, bf16[4,96,256]{2,1,0:T(8,128)(2,1)S(1)} %pad_maximum_fusion.refs_0_.refs_2_, f32[32,256]{1,0:T(8,128)S(1)} %copy-done, f32[32,256]{1,0:T(8,128)S(1)} %copy-done.1, ...), custom_call_target="tpu_custom_call" | custom-call | flops 545259520 | bytes 393216 | tf_op jit(solution)/shard_map/pallas_call | solution.py:258
  (2 shorter events, 0.0 us)
Async XLA Ops:
  1.0 6.7 %collective-permute-start = (bf16[1,96,256]{2,1,0:T(8,128)(2,1)S(1)}, bf16[1,96,256]{2,1,0:T(8,128)(2,1)S(1)}, u32[]{:S(2)}, u32[]{:S(2)}) collective-permute-start(bf16[1,96,256]{2,1,0:T(8,128)(2,1)S(1)} %bitcast.2), channel_id=1, source_target_pairs={{0,8},{2,10},{4,12},{6,14},{8,0},{10,2},{12,4},{14,6},{1,9},{3,11}... | collective-permute-start | bytes 147464 | tf_op jit(solution)/shard_map/ppermute | solution.py:303
  7.7 5.6 %collective-permute-start.3 = (bf16[2,96,256]{2,1,0:T(8,128)(2,1)S(1)}, bf16[2,96,256]{2,1,0:T(8,128)(2,1)S(1)}, u32[]{:S(2)}, u32[]{:S(2)}) collective-permute-start(bf16[2,96,256]{2,1,0:T(8,128)(2,1)S(1)} %pad_maximum_fusion.1.refs_0_), channel_id=1, source_target_pairs={{0,4},{2,6},{4,0},{6,2},{8,12},{10,14},{12,8},{14,10},{1,5},{3,7},... | collective-permute-start | bytes 294920 | tf_op jit(solution)/shard_map/ppermute | solution.py:303
  9.2 6.0 %collective-permute-start.2 = (bf16[2,96,256]{2,1,0:T(8,128)(2,1)S(1)}, bf16[2,96,256]{2,1,0:T(8,128)(2,1)S(1)}, u32[]{:S(2)}, u32[]{:S(2)}) collective-permute-start(bf16[2,96,256]{2,1,0:T(8,128)(2,1)S(1)} %pad_maximum_fusion.1.refs_0_), channel_id=1, source_target_pairs={{0,2},{2,0},{4,6},{6,4},{8,10},{10,8},{12,14},{14,12},{1,3},{3,1},... | collective-permute-start | bytes 294920 | tf_op jit(solution)/shard_map/ppermute | solution.py:303
  10.7 5.5 %collective-permute-start.1 = (bf16[2,96,256]{2,1,0:T(8,128)(2,1)S(1)}, bf16[2,96,256]{2,1,0:T(8,128)(2,1)S(1)}, u32[]{:S(2)}, u32[]{:S(2)}) collective-permute-start(bf16[2,96,256]{2,1,0:T(8,128)(2,1)S(1)} %pad_maximum_fusion.1.refs_0_), channel_id=1, source_target_pairs={{0,6},{2,4},{4,2},{6,0},{8,14},{10,12},{12,10},{14,8},{1,7},{3,5},... | collective-permute-start | bytes 294920 | tf_op jit(solution)/shard_map/ppermute | solution.py:303
  13.4 2.8 %copy-start = (f32[32,256]{1,0:T(8,128)S(1)}, f32[32,256]{1,0:T(8,128)}, u32[]{:S(2)}) copy-start(f32[32,256]{1,0:T(8,128)} %refs_3_.1) | copy-start | bytes 98308
  13.4 2.8 %copy-start.1 = (f32[32,256]{1,0:T(8,128)S(1)}, f32[32,256]{1,0:T(8,128)}, u32[]{:S(2)}) copy-start(f32[32,256]{1,0:T(8,128)} %refs_4_.1) | copy-start | bytes 98308

commit v9 on v8

--- a/solution.py
+++ b/solution.py
@@ -15,7 +15,7 @@
 
 SOFTEN = 0.02
 
-GEO_ROWS = 32
+GEO_ROWS = 16
 FLAG_ROW = 6
 CHUNK = 128
 PIECES = 48
@@ -51,11 +51,10 @@
         return flags + jnp.where(lane == near * n_far + far, plive[i], 0)
 
     flags = lax.fori_loop(0, prow.shape[0], add_slot, jnp.zeros((1, width), jnp.int32), unroll=True)
-    geo = jnp.concatenate(
-        [pos[...], nrm[...], flags.astype(jnp.float32), jnp.zeros((1, width), jnp.float32)], axis=0
-    )
+    high, middle, low = three_pieces(pos[...])
+    nrm_high, nrm_rest, _ = three_pieces(nrm[...])
     out[2 * bands : 2 * bands + GEO_ROWS, :] = jnp.concatenate(
-        [*three_pieces(geo), jnp.zeros((8, width), jnp.float32)], axis=0
+        [high, nrm_high, flags.astype(jnp.float32), low[0:1], middle, nrm_rest, low[1:3]], axis=0
     ).astype(jnp.bfloat16)
 
 
@@ -83,7 +82,7 @@
     n_old, n_new = levels[-1]
     bits = (n_old + n_new).bit_length() - 1
     if last:
-        diagonal, across, known, emi, ref, old_sums, *refs = refs
+        across, diagonal, known, emi, ref, old_sums, *refs = refs
         old_tiles, (out, tiles, sums, held, *scratch) = refs[: len(levels) - 1], refs[len(levels) - 1 :]
         at = 0
         for part in (known, across, diagonal):
@@ -102,16 +101,16 @@
     n_tri = triangle(n_new)
     n_pairs = n_tri + n_new * n_old
     halves = width // BLOCK
+    row = lax.broadcasted_iota(jnp.int32, (8, width), 0)
     geo_at = 2 * bands
     for k in range(n_seg):
         piece = held[k, geo_at : geo_at + GEO_ROWS, :].astype(jnp.float32)
-        geo = (piece[0:8] + piece[8:16]) + piece[16:24]
-        geo_all[k] = geo
-        flag_rows[k] = geo[FLAG_ROW : FLAG_ROW + 1, 0:BLOCK]
+        low = jnp.where(row == 0, piece[7:8], jnp.where(row == 1, piece[14:15], piece[15:16]))
+        geo_all[k] = (piece[0:8] + piece[8:16]) + jnp.where(row < 3, low, 0.0)
+        flag_rows[k] = piece[FLAG_ROW : FLAG_ROW + 1, 0:BLOCK]
     if n_old:
         sums[0:n_old] = old_sums[...]
     sums[n_old:n_seg] = jnp.zeros((n_new, bands, width), jnp.float32)
-    row = lax.broadcasted_iota(jnp.int32, (8, width), 0)
     origin = jnp.broadcast_to(geo_all[0, :, 0:1], (8, width))
     for k in range(n_seg):
         geo = geo_all[k]
@@ -310,7 +309,7 @@
     sums, tiles = grow(levels[:1], seg_bits, col_bits, n_far, (gathered,))
     gathered = jnp.concatenate([gathered, beside])
     sums, more_tiles = grow(levels[:2], seg_bits, col_bits, n_far, (gathered, sums))
-    args = (diagonal, across, gathered, emission, reflect, sums, tiles, more_tiles)
+    args = (across, diagonal, gathered, emission, reflect, sums, tiles, more_tiles)
     return grow(levels, seg_bits, col_bits, n_far, args)
 
 

time: 22.3 us -> 21.5 us (0.964)
  waiting for transfers between devices: 4.61 us -> 3.75 us
    ppermute x4, waiting for transfers between devices: 4.61 us -> 3.75 us  [swap(): lax.ppermute(value, ('row', 'col'), [(i, i ^ distance) for i in range(n_s...]
where the time goes in v9:
time: 21.5 us; the launch traced here: 21.3 us
  Pallas kernels  9.79 us (46%)
  starting transfers between devices  7.66 us (36%)
  waiting for transfers between devices  3.75 us (17%)
    pallas_call x3, Pallas kernels, grow(): pl.pallas_call(functools.partial(grow_kernel, levels, seg_bits, col_bits,...  8.78 us
    ppermute x4, starting transfers between devices, swap(): lax.ppermute(value, ('row', 'col'), [(i, i ^ distance) for i in range(n_s...  7.66 us
    ppermute x4, waiting for transfers between devices, swap(): lax.ppermute(value, ('row', 'col'), [(i, i ^ distance) for i in range(n_s...  3.75 us
    pallas_call x1, Pallas kernels, one_exchange(): pl.pallas_call(functools.partial(pack_kernel, col_bits, n_far), out_shape...  1.01 us
  transfers between devices with their start and end apart: 4, of which 3 were waited for; matrix products, arithmetic and copies ran while one was open for 0% of the time, Pallas kernels for 13%

profile of v9, /device:TPU:0, one launch (start us, length us, event | category | flops | bytes accessed | tf_op | source)
XLA Modules:
  0.0 21.3 jit_solution(12020790929260064291)
XLA Ops:
  0.0 1.0 %shard_map.82 = bf16[80,256]{1,0:T(8,128)(2,1)S(1)} custom-call(f32[3,256]{1,0:T(4,128)} %pos.1, f32[3,256]{1,0:T(4,128)} %nrm.1, f32[1,256]{1,0:T(1,128)} %bitcast.5, f32[32,256]{1,0:T(8,128)} %refs_3_.1, f32[32,256]{1,0:T(8,128)} %refs_4_.1, s32[32]{0:T(128)} %prow.1, s32[32]{0:T(128)} %pcol.1, s32[32]{0:T(128)} %plive.1), custom_call_target="tpu_custom_call" | custom-call | tf_op jit(solution)/shard_map/pallas_call | solution.py:293
  1.0 4.1 %collective-permute-start = (bf16[1,80,256]{2,1,0:T(8,128)(2,1)S(1)}, bf16[1,80,256]{2,1,0:T(8,128)(2,1)S(1)}, u32[]{:S(2)}, u32[]{:S(2)}) collective-permute-start(bf16[1,80,256]{2,1,0:T(8,128)(2,1)S(1)} %bitcast.2), channel_id=1, source_target_pairs={{0,8},{2,10},{4,12},{6,14},{8,0},{10,2},{12,4},{14,6},{1,9},{3,11}... | collective-permute-start | bytes 122888 | tf_op jit(solution)/shard_map/ppermute | solution.py:302
  5.1 2.4 %collective-permute-done = bf16[1,80,256]{2,1,0:T(8,128)(2,1)S(1)} collective-permute-done((bf16[1,80,256]{2,1,0:T(8,128)(2,1)S(1)}, bf16[1,80,256]{2,1,0:T(8,128)(2,1)S(1)}, u32[]{:S(2)}, u32[]{:S(2)}) %collective-permute-start) | collective-permute-done | bytes 40992 | tf_op jit(solution)/shard_map/ppermute | solution.py:302
  7.6 1.5 %collective-permute-start.3 = (bf16[2,80,256]{2,1,0:T(8,128)(2,1)S(1)}, bf16[2,80,256]{2,1,0:T(8,128)(2,1)S(1)}, u32[]{:S(2)}, u32[]{:S(2)}) collective-permute-start(bf16[2,80,256]{2,1,0:T(8,128)(2,1)S(1)} %pad_maximum_fusion.1.refs_0_), channel_id=1, source_target_pairs={{0,4},{2,6},{4,0},{6,2},{8,12},{10,14},{12,8},{14,10},{1,5},{3,7},... | collective-permute-start | bytes 245768 | tf_op jit(solution)/shard_map/ppermute | solution.py:302
  9.1 1.7 %collective-permute-start.2 = (bf16[2,80,256]{2,1,0:T(8,128)(2,1)S(1)}, bf16[2,80,256]{2,1,0:T(8,128)(2,1)S(1)}, u32[]{:S(2)}, u32[]{:S(2)}) collective-permute-start(bf16[2,80,256]{2,1,0:T(8,128)(2,1)S(1)} %pad_maximum_fusion.1.refs_0_), channel_id=1, source_target_pairs={{0,6},{2,4},{4,2},{6,0},{8,14},{10,12},{12,10},{14,8},{1,7},{3,5},... | collective-permute-start | bytes 245768 | tf_op jit(solution)/shard_map/ppermute | solution.py:302
  10.8 0.3 %collective-permute-start.1 = (bf16[2,80,256]{2,1,0:T(8,128)(2,1)S(1)}, bf16[2,80,256]{2,1,0:T(8,128)(2,1)S(1)}, u32[]{:S(2)}, u32[]{:S(2)}) collective-permute-start(bf16[2,80,256]{2,1,0:T(8,128)(2,1)S(1)} %pad_maximum_fusion.1.refs_0_), channel_id=1, source_target_pairs={{0,2},{2,0},{4,6},{6,4},{8,10},{10,8},{12,14},{14,12},{1,3},{3,1},... | collective-permute-start | bytes 245768 | tf_op jit(solution)/shard_map/ppermute | solution.py:302
  11.1 1.0 %shard_map.83 = (f32[2,32,256]{2,1,0:T(8,128)S(1)}, bf16[3,256,256]{2,1,0:T(8,128)(2,1)S(1)}) custom-call(bf16[2,80,256]{2,1,0:T(8,128)(2,1)S(1)} %pad_maximum_fusion.1.refs_0_), custom_call_target="tpu_custom_call" | custom-call | flops 62914560 | bytes 81920 | tf_op jit(solution)/shard_map/pallas_call | solution.py:257
  12.2 0.6 %collective-permute-done.3 = bf16[2,80,256]{2,1,0:T(8,128)(2,1)S(1)} collective-permute-done((bf16[2,80,256]{2,1,0:T(8,128)(2,1)S(1)}, bf16[2,80,256]{2,1,0:T(8,128)(2,1)S(1)}, u32[]{:S(2)}, u32[]{:S(2)}) %collective-permute-start.3) | collective-permute-done | bytes 81952 | tf_op jit(solution)/shard_map/ppermute | solution.py:302
  12.8 0.0 copy-start
  12.8 0.0 copy-start.1
  12.8 1.8 %shard_map.84 = (f32[4,32,256]{2,1,0:T(8,128)S(1)}, bf16[7,256,256]{2,1,0:T(8,128)(2,1)S(1)}) custom-call(bf16[4,80,256]{2,1,0:T(8,128)(2,1)S(1)} %pad_maximum_fusion.refs_0_.refs_2_, f32[2,32,256]{2,1,0:T(8,128)S(1)} %get-tuple-element.9.refs_1_), custom_call_target="tpu_custom_call" | custom-call | flops 146800640 | bytes 163840 | tf_op jit(solution)/shard_map/pallas_call | solution.py:257
  14.6 0.0 collective-permute-done.2.refs_1_
  14.6 0.7 %collective-permute-done.1.refs_0_ = bf16[2,80,256]{2,1,0:T(8,128)(2,1)S(1)} collective-permute-done((bf16[2,80,256]{2,1,0:T(8,128)(2,1)S(1)}, bf16[2,80,256]{2,1,0:T(8,128)(2,1)S(1)}, u32[]{:S(2)}, u32[]{:S(2)}) %collective-permute-start.1) | collective-permute-done | bytes 81952 | tf_op jit(solution)/shard_map/ppermute | solution.py:302
  15.3 0.0 copy-done
  15.3 0.0 copy-done.1
  15.3 6.0 %shard_map.85 = f32[32,256]{1,0:T(8,128)} custom-call(bf16[2,80,256]{2,1,0:T(8,128)(2,1)S(1)} %collective-permute-done.1.refs_0_, bf16[2,80,256]{2,1,0:T(8,128)(2,1)S(1)} %collective-permute-done.2.refs_1_, bf16[4,80,256]{2,1,0:T(8,128)(2,1)S(1)} %pad_maximum_fusion.refs_0_.refs_2_, f32[32,256]{1,0:T(8,128)S(1)} %copy-done, f32[32,256]{1,0:T(8,128)S(1)} %copy-done.1, ...), custom_call_target="tpu_custom_call" | custom-call | flops 545259520 | bytes 327680 | tf_op jit(solution)/shard_map/pallas_call | solution.py:257
  (2 shorter events, 0.0 us)
Async XLA Ops:
  1.0 6.5 %collective-permute-start = (bf16[1,80,256]{2,1,0:T(8,128)(2,1)S(1)}, bf16[1,80,256]{2,1,0:T(8,128)(2,1)S(1)}, u32[]{:S(2)}, u32[]{:S(2)}) collective-permute-start(bf16[1,80,256]{2,1,0:T(8,128)(2,1)S(1)} %bitcast.2), channel_id=1, source_target_pairs={{0,8},{2,10},{4,12},{6,14},{8,0},{10,2},{12,4},{14,6},{1,9},{3,11}... | collective-permute-start | bytes 122888 | tf_op jit(solution)/shard_map/ppermute | solution.py:302
  7.6 5.2 %collective-permute-start.3 = (bf16[2,80,256]{2,1,0:T(8,128)(2,1)S(1)}, bf16[2,80,256]{2,1,0:T(8,128)(2,1)S(1)}, u32[]{:S(2)}, u32[]{:S(2)}) collective-permute-start(bf16[2,80,256]{2,1,0:T(8,128)(2,1)S(1)} %pad_maximum_fusion.1.refs_0_), channel_id=1, source_target_pairs={{0,4},{2,6},{4,0},{6,2},{8,12},{10,14},{12,8},{14,10},{1,5},{3,7},... | collective-permute-start | bytes 245768 | tf_op jit(solution)/shard_map/ppermute | solution.py:302
  9.1 5.5 %collective-permute-start.2 = (bf16[2,80,256]{2,1,0:T(8,128)(2,1)S(1)}, bf16[2,80,256]{2,1,0:T(8,128)(2,1)S(1)}, u32[]{:S(2)}, u32[]{:S(2)}) collective-permute-start(bf16[2,80,256]{2,1,0:T(8,128)(2,1)S(1)} %pad_maximum_fusion.1.refs_0_), channel_id=1, source_target_pairs={{0,6},{2,4},{4,2},{6,0},{8,14},{10,12},{12,10},{14,8},{1,7},{3,5},... | collective-permute-start | bytes 245768 | tf_op jit(solution)/shard_map/ppermute | solution.py:302
  10.8 4.5 %collective-permute-start.1 = (bf16[2,80,256]{2,1,0:T(8,128)(2,1)S(1)}, bf16[2,80,256]{2,1,0:T(8,128)(2,1)S(1)}, u32[]{:S(2)}, u32[]{:S(2)}) collective-permute-start(bf16[2,80,256]{2,1,0:T(8,128)(2,1)S(1)} %pad_maximum_fusion.1.refs_0_), channel_id=1, source_target_pairs={{0,2},{2,0},{4,6},{6,4},{8,10},{10,8},{12,14},{14,12},{1,3},{3,1},... | collective-permute-start | bytes 245768 | tf_op jit(solution)/shard_map/ppermute | solution.py:302
  12.8 2.5 %copy-start = (f32[32,256]{1,0:T(8,128)S(1)}, f32[32,256]{1,0:T(8,128)}, u32[]{:S(2)}) copy-start(f32[32,256]{1,0:T(8,128)} %refs_3_.1) | copy-start | bytes 98308
  12.8 2.5 %copy-start.1 = (f32[32,256]{1,0:T(8,128)S(1)}, f32[32,256]{1,0:T(8,128)}, u32[]{:S(2)}) copy-start(f32[32,256]{1,0:T(8,128)} %refs_4_.1) | copy-start | bytes 98308

commit v10 on v9

--- a/solution.py
+++ b/solution.py
@@ -76,6 +76,23 @@
     if k <= count // 2:
         return k * count, 1
     return (count - k) * count + k, 0
+
+
+def diagonal_product(weights, tiles, t):
+    width = weights.shape[1]
+    blocks = []
+    for at in range(0, width, BLOCK):
+        block = slice(at, at + BLOCK)
+        total = lax.dot_general(
+            weights[:, at:], tiles[t, block, at:], (((1,), (1,)), ((), ())),
+            preferred_element_type=jnp.float32,
+        )
+        if at:
+            total += jnp.dot(
+                weights[:, :at], tiles[t, :at, block], preferred_element_type=jnp.float32
+            )
+        blocks.append(total)
+    return jnp.concatenate(blocks, axis=1)
 
 
 def grow_kernel(levels, seg_bits, col_bits, n_far, last, *refs):
@@ -159,13 +176,14 @@
         for at in range(0, width, CHUNK):
             yield
             rows = slice(at, at + CHUNK)
+            cols = slice(at // BLOCK * BLOCK if near_at == far_at else 0, width)
             leaving = jnp.dot(
-                near_leave[local, rows], far_leave[far_at], preferred_element_type=jnp.float32
+                near_leave[local, rows], far_leave[far_at, :, cols], preferred_element_type=jnp.float32
             )
             arriving = jnp.dot(
-                near_arrive[local, rows], masked[at // BLOCK], preferred_element_type=jnp.float32
+                near_arrive[local, rows], masked[at // BLOCK][:, cols], preferred_element_type=jnp.float32
             )
-            cosines[rows] = jnp.maximum(leaving, 0.0) * jnp.maximum(arriving, 0.0)
+            cosines[rows, cols] = jnp.maximum(leaving, 0.0) * jnp.maximum(arriving, 0.0)
 
     def form(t, cosines, fresh):
         local, near_at, far_at = pair_of(t)
@@ -187,7 +205,7 @@
                 else:
                     now = [near_rep[local, c, at : at + 8, :] for c in range(3)]
                 nears.append(now)
-            for j in range(halves):
+            for j in range(strip * 16 // BLOCK if near_at == far_at else 0, halves):
                 cols = slice(j * BLOCK, (j + 1) * BLOCK)
                 parts = []
                 for part in range(2):
@@ -202,16 +220,18 @@
 
     def apply(t):
         local, near_at, far_at = pair_of(t)
+        if near_at == far_at:
+            sums[near_at] = sums[near_at] + diagonal_product(held[far_at, 0:bands, :], tiles, t)
+            return
         tile = tiles[t]
         to_near = lax.dot_general(
             held[far_at, 0:bands, :], tile, (((1,), (1,)), ((), ())), preferred_element_type=jnp.float32
         )
         sums[near_at] = sums[near_at] + to_near
-        if near_at != far_at:
-            to_far = lax.dot_general(
-                held[near_at, 0:bands, :], tile, (((1,), (0,)), ((), ())), preferred_element_type=jnp.float32
-            )
-            sums[far_at] = sums[far_at] + to_far
+        to_far = lax.dot_general(
+            held[near_at, 0:bands, :], tile, (((1,), (0,)), ((), ())), preferred_element_type=jnp.float32
+        )
+        sums[far_at] = sums[far_at] + to_far
 
     cosines = (even, odd)
     for _ in project(0, even):
@@ -233,6 +253,9 @@
         level = next(i for i, (old, new) in enumerate(levels) if k < old + new)
         old, new = levels[level]
         t, over = (triangle(new) + k - old, 0) if old else own_tile(k, new)
+        if k == 0:
+            total += diagonal_product(weighted, old_tiles[level], t)
+            continue
         tile = tiles[t] if k >= n_old else old_tiles[level][t]
         total += lax.dot_general(
             weighted, tile, (((1,), (over,)), ((), ())), preferred_element_type=jnp.float32

time: 21.5 us -> 21 us (0.977)
  Pallas kernels: 9.79 us -> 9.08 us
    pallas_call x3, Pallas kernels: 8.78 us -> 8.07 us  [grow(): pl.pallas_call(functools.partial(grow_kernel, levels, seg_bits, col_bits,...]
where the time goes in v10:
time: 21 us; the launch traced here: 20.8 us
  Pallas kernels  9.08 us (43%)
  starting transfers between devices  7.66 us (36%)
  waiting for transfers between devices  3.94 us (19%)
    pallas_call x3, Pallas kernels, grow(): pl.pallas_call(functools.partial(grow_kernel, levels, seg_bits, col_bits,...  8.07 us
    ppermute x4, starting transfers between devices, swap(): lax.ppermute(value, ('row', 'col'), [(i, i ^ distance) for i in range(n_s...  7.66 us
    ppermute x4, waiting for transfers between devices, swap(): lax.ppermute(value, ('row', 'col'), [(i, i ^ distance) for i in range(n_s...  3.94 us
    pallas_call x1, Pallas kernels, one_exchange(): pl.pallas_call(functools.partial(pack_kernel, col_bits, n_far), out_shape...  1.01 us
  transfers between devices with their start and end apart: 4, of which 3 were waited for; matrix products, arithmetic and copies ran while one was open for 0% of the time, Pallas kernels for 13%

profile of v10, /device:TPU:0, one launch (start us, length us, event | category | flops | bytes accessed | tf_op | source)
XLA Modules:
  0.0 20.8 jit_solution(7046207114279517282)
XLA Ops:
  0.0 1.0 %shard_map.82 = bf16[80,256]{1,0:T(8,128)(2,1)S(1)} custom-call(f32[3,256]{1,0:T(4,128)} %pos.1, f32[3,256]{1,0:T(4,128)} %nrm.1, f32[1,256]{1,0:T(1,128)} %bitcast.5, f32[32,256]{1,0:T(8,128)} %refs_3_.1, f32[32,256]{1,0:T(8,128)} %refs_4_.1, s32[32]{0:T(128)} %prow.1, s32[32]{0:T(128)} %pcol.1, s32[32]{0:T(128)} %plive.1), custom_call_target="tpu_custom_call" | custom-call | tf_op jit(solution)/shard_map/pallas_call | solution.py:316
  1.0 4.1 %collective-permute-start = (bf16[1,80,256]{2,1,0:T(8,128)(2,1)S(1)}, bf16[1,80,256]{2,1,0:T(8,128)(2,1)S(1)}, u32[]{:S(2)}, u32[]{:S(2)}) collective-permute-start(bf16[1,80,256]{2,1,0:T(8,128)(2,1)S(1)} %bitcast.2), channel_id=1, source_target_pairs={{0,8},{2,10},{4,12},{6,14},{8,0},{10,2},{12,4},{14,6},{1,9},{3,11}... | collective-permute-start | bytes 122888 | tf_op jit(solution)/shard_map/ppermute | solution.py:325
  5.1 2.4 %collective-permute-done = bf16[1,80,256]{2,1,0:T(8,128)(2,1)S(1)} collective-permute-done((bf16[1,80,256]{2,1,0:T(8,128)(2,1)S(1)}, bf16[1,80,256]{2,1,0:T(8,128)(2,1)S(1)}, u32[]{:S(2)}, u32[]{:S(2)}) %collective-permute-start) | collective-permute-done | bytes 40992 | tf_op jit(solution)/shard_map/ppermute | solution.py:325
  7.6 1.5 %collective-permute-start.3 = (bf16[2,80,256]{2,1,0:T(8,128)(2,1)S(1)}, bf16[2,80,256]{2,1,0:T(8,128)(2,1)S(1)}, u32[]{:S(2)}, u32[]{:S(2)}) collective-permute-start(bf16[2,80,256]{2,1,0:T(8,128)(2,1)S(1)} %pad_maximum_fusion.1.refs_0_), channel_id=1, source_target_pairs={{0,4},{2,6},{4,0},{6,2},{8,12},{10,14},{12,8},{14,10},{1,5},{3,7},... | collective-permute-start | bytes 245768 | tf_op jit(solution)/shard_map/ppermute | solution.py:325
  9.1 1.7 %collective-permute-start.2 = (bf16[2,80,256]{2,1,0:T(8,128)(2,1)S(1)}, bf16[2,80,256]{2,1,0:T(8,128)(2,1)S(1)}, u32[]{:S(2)}, u32[]{:S(2)}) collective-permute-start(bf16[2,80,256]{2,1,0:T(8,128)(2,1)S(1)} %pad_maximum_fusion.1.refs_0_), channel_id=1, source_target_pairs={{0,6},{2,4},{4,2},{6,0},{8,14},{10,12},{12,10},{14,8},{1,7},{3,5},... | collective-permute-start | bytes 245768 | tf_op jit(solution)/shard_map/ppermute | solution.py:325
  10.8 0.3 %collective-permute-start.1 = (bf16[2,80,256]{2,1,0:T(8,128)(2,1)S(1)}, bf16[2,80,256]{2,1,0:T(8,128)(2,1)S(1)}, u32[]{:S(2)}, u32[]{:S(2)}) collective-permute-start(bf16[2,80,256]{2,1,0:T(8,128)(2,1)S(1)} %pad_maximum_fusion.1.refs_0_), channel_id=1, source_target_pairs={{0,2},{2,0},{4,6},{6,4},{8,10},{10,8},{12,14},{14,12},{1,3},{3,1},... | collective-permute-start | bytes 245768 | tf_op jit(solution)/shard_map/ppermute | solution.py:325
  11.1 1.0 %shard_map.83 = (f32[2,32,256]{2,1,0:T(8,128)S(1)}, bf16[3,256,256]{2,1,0:T(8,128)(2,1)S(1)}) custom-call(bf16[2,80,256]{2,1,0:T(8,128)(2,1)S(1)} %pad_maximum_fusion.1.refs_0_), custom_call_target="tpu_custom_call" | custom-call | flops 62914560 | bytes 81920 | tf_op jit(solution)/shard_map/pallas_call | solution.py:280
  12.1 0.7 %collective-permute-done.3 = bf16[2,80,256]{2,1,0:T(8,128)(2,1)S(1)} collective-permute-done((bf16[2,80,256]{2,1,0:T(8,128)(2,1)S(1)}, bf16[2,80,256]{2,1,0:T(8,128)(2,1)S(1)}, u32[]{:S(2)}, u32[]{:S(2)}) %collective-permute-start.3) | collective-permute-done | bytes 81952 | tf_op jit(solution)/shard_map/ppermute | solution.py:325
  12.8 0.0 copy-start
  12.8 0.0 copy-start.1
  12.8 1.7 %shard_map.84 = (f32[4,32,256]{2,1,0:T(8,128)S(1)}, bf16[7,256,256]{2,1,0:T(8,128)(2,1)S(1)}) custom-call(bf16[4,80,256]{2,1,0:T(8,128)(2,1)S(1)} %pad_maximum_fusion.refs_0_.refs_2_, f32[2,32,256]{2,1,0:T(8,128)S(1)} %get-tuple-element.9.refs_1_), custom_call_target="tpu_custom_call" | custom-call | flops 146800640 | bytes 163840 | tf_op jit(solution)/shard_map/pallas_call | solution.py:280
  14.5 0.0 collective-permute-done.2.refs_1_
  14.5 0.8 %collective-permute-done.1.refs_0_ = bf16[2,80,256]{2,1,0:T(8,128)(2,1)S(1)} collective-permute-done((bf16[2,80,256]{2,1,0:T(8,128)(2,1)S(1)}, bf16[2,80,256]{2,1,0:T(8,128)(2,1)S(1)}, u32[]{:S(2)}, u32[]{:S(2)}) %collective-permute-start.1) | collective-permute-done | bytes 81952 | tf_op jit(solution)/shard_map/ppermute | solution.py:325
  15.3 0.0 copy-done
  15.3 0.0 copy-done.1
  15.3 5.5 %shard_map.85 = f32[32,256]{1,0:T(8,128)} custom-call(bf16[2,80,256]{2,1,0:T(8,128)(2,1)S(1)} %collective-permute-done.1.refs_0_, bf16[2,80,256]{2,1,0:T(8,128)(2,1)S(1)} %collective-permute-done.2.refs_1_, bf16[4,80,256]{2,1,0:T(8,128)(2,1)S(1)} %pad_maximum_fusion.refs_0_.refs_2_, f32[32,256]{1,0:T(8,128)S(1)} %copy-done, f32[32,256]{1,0:T(8,128)S(1)} %copy-done.1, ...), custom_call_target="tpu_custom_call" | custom-call | flops 545259520 | bytes 327680 | tf_op jit(solution)/shard_map/pallas_call | solution.py:280
  (2 shorter events, 0.0 us)
Async XLA Ops:
  1.0 6.5 %collective-permute-start = (bf16[1,80,256]{2,1,0:T(8,128)(2,1)S(1)}, bf16[1,80,256]{2,1,0:T(8,128)(2,1)S(1)}, u32[]{:S(2)}, u32[]{:S(2)}) collective-permute-start(bf16[1,80,256]{2,1,0:T(8,128)(2,1)S(1)} %bitcast.2), channel_id=1, source_target_pairs={{0,8},{2,10},{4,12},{6,14},{8,0},{10,2},{12,4},{14,6},{1,9},{3,11}... | collective-permute-start | bytes 122888 | tf_op jit(solution)/shard_map/ppermute | solution.py:325
  7.6 5.2 %collective-permute-start.3 = (bf16[2,80,256]{2,1,0:T(8,128)(2,1)S(1)}, bf16[2,80,256]{2,1,0:T(8,128)(2,1)S(1)}, u32[]{:S(2)}, u32[]{:S(2)}) collective-permute-start(bf16[2,80,256]{2,1,0:T(8,128)(2,1)S(1)} %pad_maximum_fusion.1.refs_0_), channel_id=1, source_target_pairs={{0,4},{2,6},{4,0},{6,2},{8,12},{10,14},{12,8},{14,10},{1,5},{3,7},... | collective-permute-start | bytes 245768 | tf_op jit(solution)/shard_map/ppermute | solution.py:325
  9.1 5.4 %collective-permute-start.2 = (bf16[2,80,256]{2,1,0:T(8,128)(2,1)S(1)}, bf16[2,80,256]{2,1,0:T(8,128)(2,1)S(1)}, u32[]{:S(2)}, u32[]{:S(2)}) collective-permute-start(bf16[2,80,256]{2,1,0:T(8,128)(2,1)S(1)} %pad_maximum_fusion.1.refs_0_), channel_id=1, source_target_pairs={{0,6},{2,4},{4,2},{6,0},{8,14},{10,12},{12,10},{14,8},{1,7},{3,5},... | collective-permute-start | bytes 245768 | tf_op jit(solution)/shard_map/ppermute | solution.py:325
  10.8 4.5 %collective-permute-start.1 = (bf16[2,80,256]{2,1,0:T(8,128)(2,1)S(1)}, bf16[2,80,256]{2,1,0:T(8,128)(2,1)S(1)}, u32[]{:S(2)}, u32[]{:S(2)}) collective-permute-start(bf16[2,80,256]{2,1,0:T(8,128)(2,1)S(1)} %pad_maximum_fusion.1.refs_0_), channel_id=1, source_target_pairs={{0,2},{2,0},{4,6},{6,4},{8,10},{10,8},{12,14},{14,12},{1,3},{3,1},... | collective-permute-start | bytes 245768 | tf_op jit(solution)/shard_map/ppermute | solution.py:325
  12.8 2.5 %copy-start = (f32[32,256]{1,0:T(8,128)S(1)}, f32[32,256]{1,0:T(8,128)}, u32[]{:S(2)}) copy-start(f32[32,256]{1,0:T(8,128)} %refs_3_.1) | copy-start | bytes 98308
  12.8 2.5 %copy-start.1 = (f32[32,256]{1,0:T(8,128)S(1)}, f32[32,256]{1,0:T(8,128)}, u32[]{:S(2)}) copy-start(f32[32,256]{1,0:T(8,128)} %refs_4_.1) | copy-start | bytes 98308

commit v11 on v10

--- a/solution.py
+++ b/solution.py
@@ -41,20 +41,22 @@
     a = area[...]
     out[0:bands, :] = (a * emi[...]).astype(jnp.bfloat16)
     out[bands : 2 * bands, :] = (a * ref[...]).astype(jnp.bfloat16)
-    lane = lax.broadcasted_iota(jnp.int32, (1, width), 1)
     col_mask = (1 << col_bits) - 1
-
-    def add_slot(i, flags):
-        p, q = prow[i], pcol[i]
-        near = ((((p >> 1) ^ seg) & col_mask) << 1) | (p & 1)
-        far = ((((q >> 1) ^ seg) >> col_bits) << 1) | (q & 1)
-        return flags + jnp.where(lane == near * n_far + far, plive[i], 0)
-
-    flags = lax.fori_loop(0, prow.shape[0], add_slot, jnp.zeros((1, width), jnp.int32), unroll=True)
+    p, q = prow[...], pcol[...]
+    near = ((((p >> 1) ^ seg) & col_mask) << 1) | (p & 1)
+    far = ((((q >> 1) ^ seg) >> col_bits) << 1) | (q & 1)
+    slots = p.shape[1]
+    place = lax.broadcasted_iota(jnp.int32, (BLOCK, slots), 0)
+    chosen = jnp.where(place == near * n_far + far, plive[...], 0).astype(jnp.float32)
+    flags = lax.dot_general(
+        jnp.ones((8, slots), jnp.float32), chosen, (((1,), (1,)), ((), ())),
+        preferred_element_type=jnp.float32,
+    )
+    flags = jnp.concatenate([flags[0:1], jnp.zeros((1, width - BLOCK), jnp.float32)], axis=1)
     high, middle, low = three_pieces(pos[...])
     nrm_high, nrm_rest, _ = three_pieces(nrm[...])
     out[2 * bands : 2 * bands + GEO_ROWS, :] = jnp.concatenate(
-        [high, nrm_high, flags.astype(jnp.float32), low[0:1], middle, nrm_rest, low[1:3]], axis=0
+        [high, nrm_high, flags, low[0:1], middle, nrm_rest, low[1:3]], axis=0
     ).astype(jnp.bfloat16)
 
 
@@ -312,13 +314,13 @@
     n_far = width // BLOCK * n_row
     rows = 2 * bands + GEO_ROWS
     vmem = pl.BlockSpec(memory_space=pltpu.VMEM)
-    smem = pl.BlockSpec(memory_space=pltpu.SMEM)
+    pairs = [pair.reshape(1, -1) for pair in (pair_row, pair_col, pair_live)]
     packed = pl.pallas_call(
         functools.partial(pack_kernel, col_bits, n_far),
         out_shape=pltpu.VMEM((rows, width), jnp.bfloat16),
-        in_specs=[vmem] * 5 + [smem] * 3,
+        in_specs=[vmem] * 8,
         out_specs=vmem,
-    )(positions, normals, areas.reshape(1, width), emission, reflect, pair_row, pair_col, pair_live)
+    )(positions, normals, areas.reshape(1, width), emission, reflect, *pairs)
     gathered = packed[None]
 
     def swap(value, distance):

time: 21 us -> 20.9 us (level)
  no operation moved by 1% of the time
where the time goes in v11:
time: 20.9 us; the launch traced here: 20.7 us
  Pallas kernels  9.08 us (43%)
  starting transfers between devices  7.6 us (36%)
  waiting for transfers between devices  3.94 us (19%)
    pallas_call x3, Pallas kernels, grow(): pl.pallas_call(functools.partial(grow_kernel, levels, seg_bits, col_bits,...  8.08 us
    ppermute x4, starting transfers between devices, swap(): lax.ppermute(value, ('row', 'col'), [(i, i ^ distance) for i in range(n_s...  7.6 us
    ppermute x4, waiting for transfers between devices, swap(): lax.ppermute(value, ('row', 'col'), [(i, i ^ distance) for i in range(n_s...  3.94 us
    pallas_call x1, Pallas kernels, one_exchange(): pl.pallas_call(functools.partial(pack_kernel, col_bits, n_far), out_shape...  1 us
  transfers between devices with their start and end apart: 4, of which 3 were waited for; matrix products, arithmetic and copies ran while one was open for 0% of the time, Pallas kernels for 13%

profile of v11, /device:TPU:0, one launch (start us, length us, event | category | flops | bytes accessed | tf_op | source)
XLA Modules:
  0.0 20.7 jit_solution(16051842831354336019)
XLA Ops:
  0.0 1.0 %shard_map.82 = bf16[80,256]{1,0:T(8,128)(2,1)S(1)} custom-call(f32[3,256]{1,0:T(4,128)} %pos.1, f32[3,256]{1,0:T(4,128)} %nrm.1, f32[1,256]{1,0:T(1,128)} %bitcast.8, f32[32,256]{1,0:T(8,128)} %refs_3_.1, f32[32,256]{1,0:T(8,128)} %refs_4_.1, s32[1,32]{1,0:T(1,128)} %bitcast.9, s32[1,32]{1,0:T(1,128)} %bitcast.10, s32[1,32]{1,0:T(1,128)} %bitcast.11), custom_call_target="tpu_custom_call" | custom-call | tf_op jit(solution)/shard_map/pallas_call | solution.py:318
  1.0 4.1 %collective-permute-start = (bf16[1,80,256]{2,1,0:T(8,128)(2,1)S(1)}, bf16[1,80,256]{2,1,0:T(8,128)(2,1)S(1)}, u32[]{:S(2)}, u32[]{:S(2)}) collective-permute-start(bf16[1,80,256]{2,1,0:T(8,128)(2,1)S(1)} %bitcast.5), channel_id=1, source_target_pairs={{0,8},{2,10},{4,12},{6,14},{8,0},{10,2},{12,4},{14,6},{1,9},{3,11}... | collective-permute-start | bytes 122888 | tf_op jit(solution)/shard_map/ppermute | solution.py:327
  5.1 2.4 %collective-permute-done = bf16[1,80,256]{2,1,0:T(8,128)(2,1)S(1)} collective-permute-done((bf16[1,80,256]{2,1,0:T(8,128)(2,1)S(1)}, bf16[1,80,256]{2,1,0:T(8,128)(2,1)S(1)}, u32[]{:S(2)}, u32[]{:S(2)}) %collective-permute-start) | collective-permute-done | bytes 40992 | tf_op jit(solution)/shard_map/ppermute | solution.py:327
  7.5 1.5 %collective-permute-start.3 = (bf16[2,80,256]{2,1,0:T(8,128)(2,1)S(1)}, bf16[2,80,256]{2,1,0:T(8,128)(2,1)S(1)}, u32[]{:S(2)}, u32[]{:S(2)}) collective-permute-start(bf16[2,80,256]{2,1,0:T(8,128)(2,1)S(1)} %pad_maximum_fusion.1.refs_0_), channel_id=1, source_target_pairs={{0,4},{2,6},{4,0},{6,2},{8,12},{10,14},{12,8},{14,10},{1,5},{3,7},... | collective-permute-start | bytes 245768 | tf_op jit(solution)/shard_map/ppermute | solution.py:327
  9.0 1.7 %collective-permute-start.2 = (bf16[2,80,256]{2,1,0:T(8,128)(2,1)S(1)}, bf16[2,80,256]{2,1,0:T(8,128)(2,1)S(1)}, u32[]{:S(2)}, u32[]{:S(2)}) collective-permute-start(bf16[2,80,256]{2,1,0:T(8,128)(2,1)S(1)} %pad_maximum_fusion.1.refs_0_), channel_id=1, source_target_pairs={{0,6},{2,4},{4,2},{6,0},{8,14},{10,12},{12,10},{14,8},{1,7},{3,5},... | collective-permute-start | bytes 245768 | tf_op jit(solution)/shard_map/ppermute | solution.py:327
  10.7 0.3 %collective-permute-start.1 = (bf16[2,80,256]{2,1,0:T(8,128)(2,1)S(1)}, bf16[2,80,256]{2,1,0:T(8,128)(2,1)S(1)}, u32[]{:S(2)}, u32[]{:S(2)}) collective-permute-start(bf16[2,80,256]{2,1,0:T(8,128)(2,1)S(1)} %pad_maximum_fusion.1.refs_0_), channel_id=1, source_target_pairs={{0,2},{2,0},{4,6},{6,4},{8,10},{10,8},{12,14},{14,12},{1,3},{3,1},... | collective-permute-start | bytes 245768 | tf_op jit(solution)/shard_map/ppermute | solution.py:327
  11.0 1.0 %shard_map.83 = (f32[2,32,256]{2,1,0:T(8,128)S(1)}, bf16[3,256,256]{2,1,0:T(8,128)(2,1)S(1)}) custom-call(bf16[2,80,256]{2,1,0:T(8,128)(2,1)S(1)} %pad_maximum_fusion.1.refs_0_), custom_call_target="tpu_custom_call" | custom-call | flops 62914560 | bytes 81920 | tf_op jit(solution)/shard_map/pallas_call | solution.py:282
  12.0 0.7 %collective-permute-done.3 = bf16[2,80,256]{2,1,0:T(8,128)(2,1)S(1)} collective-permute-done((bf16[2,80,256]{2,1,0:T(8,128)(2,1)S(1)}, bf16[2,80,256]{2,1,0:T(8,128)(2,1)S(1)}, u32[]{:S(2)}, u32[]{:S(2)}) %collective-permute-start.3) | collective-permute-done | bytes 81952 | tf_op jit(solution)/shard_map/ppermute | solution.py:327
  12.8 0.0 copy-start
  12.8 0.0 copy-start.1
  12.8 1.7 %shard_map.84 = (f32[4,32,256]{2,1,0:T(8,128)S(1)}, bf16[7,256,256]{2,1,0:T(8,128)(2,1)S(1)}) custom-call(bf16[4,80,256]{2,1,0:T(8,128)(2,1)S(1)} %pad_maximum_fusion.refs_0_.refs_2_, f32[2,32,256]{2,1,0:T(8,128)S(1)} %get-tuple-element.9.refs_1_), custom_call_target="tpu_custom_call" | custom-call | flops 146800640 | bytes 163840 | tf_op jit(solution)/shard_map/pallas_call | solution.py:282
  14.4 0.0 collective-permute-done.2.refs_1_
  14.5 0.8 %collective-permute-done.1.refs_0_ = bf16[2,80,256]{2,1,0:T(8,128)(2,1)S(1)} collective-permute-done((bf16[2,80,256]{2,1,0:T(8,128)(2,1)S(1)}, bf16[2,80,256]{2,1,0:T(8,128)(2,1)S(1)}, u32[]{:S(2)}, u32[]{:S(2)}) %collective-permute-start.1) | collective-permute-done | bytes 81952 | tf_op jit(solution)/shard_map/ppermute | solution.py:327
  15.2 0.0 copy-done
  15.2 0.0 copy-done.1
  15.2 5.5 %shard_map.85 = f32[32,256]{1,0:T(8,128)} custom-call(bf16[2,80,256]{2,1,0:T(8,128)(2,1)S(1)} %collective-permute-done.1.refs_0_, bf16[2,80,256]{2,1,0:T(8,128)(2,1)S(1)} %collective-permute-done.2.refs_1_, bf16[4,80,256]{2,1,0:T(8,128)(2,1)S(1)} %pad_maximum_fusion.refs_0_.refs_2_, f32[32,256]{1,0:T(8,128)S(1)} %copy-done, f32[32,256]{1,0:T(8,128)S(1)} %copy-done.1, ...), custom_call_target="tpu_custom_call" | custom-call | flops 545259520 | bytes 327680 | tf_op jit(solution)/shard_map/pallas_call | solution.py:282
  (2 shorter events, 0.0 us)
Async XLA Ops:
  1.0 6.5 %collective-permute-start = (bf16[1,80,256]{2,1,0:T(8,128)(2,1)S(1)}, bf16[1,80,256]{2,1,0:T(8,128)(2,1)S(1)}, u32[]{:S(2)}, u32[]{:S(2)}) collective-permute-start(bf16[1,80,256]{2,1,0:T(8,128)(2,1)S(1)} %bitcast.5), channel_id=1, source_target_pairs={{0,8},{2,10},{4,12},{6,14},{8,0},{10,2},{12,4},{14,6},{1,9},{3,11}... | collective-permute-start | bytes 122888 | tf_op jit(solution)/shard_map/ppermute | solution.py:327
  7.5 5.3 %collective-permute-start.3 = (bf16[2,80,256]{2,1,0:T(8,128)(2,1)S(1)}, bf16[2,80,256]{2,1,0:T(8,128)(2,1)S(1)}, u32[]{:S(2)}, u32[]{:S(2)}) collective-permute-start(bf16[2,80,256]{2,1,0:T(8,128)(2,1)S(1)} %pad_maximum_fusion.1.refs_0_), channel_id=1, source_target_pairs={{0,4},{2,6},{4,0},{6,2},{8,12},{10,14},{12,8},{14,10},{1,5},{3,7},... | collective-permute-start | bytes 245768 | tf_op jit(solution)/shard_map/ppermute | solution.py:327
  9.0 5.4 %collective-permute-start.2 = (bf16[2,80,256]{2,1,0:T(8,128)(2,1)S(1)}, bf16[2,80,256]{2,1,0:T(8,128)(2,1)S(1)}, u32[]{:S(2)}, u32[]{:S(2)}) collective-permute-start(bf16[2,80,256]{2,1,0:T(8,128)(2,1)S(1)} %pad_maximum_fusion.1.refs_0_), channel_id=1, source_target_pairs={{0,6},{2,4},{4,2},{6,0},{8,14},{10,12},{12,10},{14,8},{1,7},{3,5},... | collective-permute-start | bytes 245768 | tf_op jit(solution)/shard_map/ppermute | solution.py:327
  10.7 4.5 %collective-permute-start.1 = (bf16[2,80,256]{2,1,0:T(8,128)(2,1)S(1)}, bf16[2,80,256]{2,1,0:T(8,128)(2,1)S(1)}, u32[]{:S(2)}, u32[]{:S(2)}) collective-permute-start(bf16[2,80,256]{2,1,0:T(8,128)(2,1)S(1)} %pad_maximum_fusion.1.refs_0_), channel_id=1, source_target_pairs={{0,2},{2,0},{4,6},{6,4},{8,10},{10,8},{12,14},{14,12},{1,3},{3,1},... | collective-permute-start | bytes 245768 | tf_op jit(solution)/shard_map/ppermute | solution.py:327
  12.8 2.5 %copy-start = (f32[32,256]{1,0:T(8,128)S(1)}, f32[32,256]{1,0:T(8,128)}, u32[]{:S(2)}) copy-start(f32[32,256]{1,0:T(8,128)} %refs_3_.1) | copy-start | bytes 98308
  12.8 2.5 %copy-start.1 = (f32[32,256]{1,0:T(8,128)S(1)}, f32[32,256]{1,0:T(8,128)}, u32[]{:S(2)}) copy-start(f32[32,256]{1,0:T(8,128)} %refs_4_.1) | copy-start | bytes 98308

commit v12 on v11

--- a/solution.py
+++ b/solution.py
@@ -216,7 +216,7 @@
                     spacing = dx * dx + dy * dy + dz * dz + SOFTEN
                     inverse = 1.0 / spacing
                     product = cosines[at : at + 8, cols]
-                    parts.append(product * inverse * inverse)
+                    parts.append(product * (inverse * inverse))
                 strip_now = jnp.concatenate(parts, axis=0).astype(jnp.bfloat16)
                 tiles[t, strip * 16 : strip * 16 + 16, cols] = strip_now
 

time: 20.9 us -> 20.9 us (level)
  transfers between devices with their start and end apart: 4 -> 4, of which waited for: 3 -> 3; matrix products, arithmetic and copies ran while one was open for 0% -> 0% of each run, Pallas kernels for 13% -> 12%
where the time goes in v12:
time: 20.9 us; the launch traced here: 20.7 us
  Pallas kernels  8.98 us (43%)
  starting transfers between devices  7.6 us (36%)
  waiting for transfers between devices  4.02 us (19%)
    pallas_call x3, Pallas kernels, grow(): pl.pallas_call(functools.partial(grow_kernel, levels, seg_bits, col_bits,...  7.98 us
    ppermute x4, starting transfers between devices, swap(): lax.ppermute(value, ('row', 'col'), [(i, i ^ distance) for i in range(n_s...  7.6 us
    ppermute x4, waiting for transfers between devices, swap(): lax.ppermute(value, ('row', 'col'), [(i, i ^ distance) for i in range(n_s...  4.02 us
    pallas_call x1, Pallas kernels, one_exchange(): pl.pallas_call(functools.partial(pack_kernel, col_bits, n_far), out_shape...  1 us
  transfers between devices with their start and end apart: 4, of which 3 were waited for; matrix products, arithmetic and copies ran while one was open for 0% of the time, Pallas kernels for 12%

profile of v12, /device:TPU:0, one launch (start us, length us, event | category | flops | bytes accessed | tf_op | source)
XLA Modules:
  0.0 20.7 jit_solution(16042284019062485375)
XLA Ops:
  0.0 1.0 %shard_map.82 = bf16[80,256]{1,0:T(8,128)(2,1)S(1)} custom-call(f32[3,256]{1,0:T(4,128)} %pos.1, f32[3,256]{1,0:T(4,128)} %nrm.1, f32[1,256]{1,0:T(1,128)} %bitcast.8, f32[32,256]{1,0:T(8,128)} %refs_3_.1, f32[32,256]{1,0:T(8,128)} %refs_4_.1, s32[1,32]{1,0:T(1,128)} %bitcast.9, s32[1,32]{1,0:T(1,128)} %bitcast.10, s32[1,32]{1,0:T(1,128)} %bitcast.11), custom_call_target="tpu_custom_call" | custom-call | tf_op jit(solution)/shard_map/pallas_call | solution.py:318
  1.0 4.1 %collective-permute-start = (bf16[1,80,256]{2,1,0:T(8,128)(2,1)S(1)}, bf16[1,80,256]{2,1,0:T(8,128)(2,1)S(1)}, u32[]{:S(2)}, u32[]{:S(2)}) collective-permute-start(bf16[1,80,256]{2,1,0:T(8,128)(2,1)S(1)} %bitcast.5), channel_id=1, source_target_pairs={{0,8},{2,10},{4,12},{6,14},{8,0},{10,2},{12,4},{14,6},{1,9},{3,11}... | collective-permute-start | bytes 122888 | tf_op jit(solution)/shard_map/ppermute | solution.py:327
  5.1 2.4 %collective-permute-done = bf16[1,80,256]{2,1,0:T(8,128)(2,1)S(1)} collective-permute-done((bf16[1,80,256]{2,1,0:T(8,128)(2,1)S(1)}, bf16[1,80,256]{2,1,0:T(8,128)(2,1)S(1)}, u32[]{:S(2)}, u32[]{:S(2)}) %collective-permute-start) | collective-permute-done | bytes 40992 | tf_op jit(solution)/shard_map/ppermute | solution.py:327
  7.5 1.5 %collective-permute-start.3 = (bf16[2,80,256]{2,1,0:T(8,128)(2,1)S(1)}, bf16[2,80,256]{2,1,0:T(8,128)(2,1)S(1)}, u32[]{:S(2)}, u32[]{:S(2)}) collective-permute-start(bf16[2,80,256]{2,1,0:T(8,128)(2,1)S(1)} %pad_maximum_fusion.1.refs_0_), channel_id=1, source_target_pairs={{0,4},{2,6},{4,0},{6,2},{8,12},{10,14},{12,8},{14,10},{1,5},{3,7},... | collective-permute-start | bytes 245768 | tf_op jit(solution)/shard_map/ppermute | solution.py:327
  9.0 1.7 %collective-permute-start.2 = (bf16[2,80,256]{2,1,0:T(8,128)(2,1)S(1)}, bf16[2,80,256]{2,1,0:T(8,128)(2,1)S(1)}, u32[]{:S(2)}, u32[]{:S(2)}) collective-permute-start(bf16[2,80,256]{2,1,0:T(8,128)(2,1)S(1)} %pad_maximum_fusion.1.refs_0_), channel_id=1, source_target_pairs={{0,6},{2,4},{4,2},{6,0},{8,14},{10,12},{12,10},{14,8},{1,7},{3,5},... | collective-permute-start | bytes 245768 | tf_op jit(solution)/shard_map/ppermute | solution.py:327
  10.7 0.3 %collective-permute-start.1 = (bf16[2,80,256]{2,1,0:T(8,128)(2,1)S(1)}, bf16[2,80,256]{2,1,0:T(8,128)(2,1)S(1)}, u32[]{:S(2)}, u32[]{:S(2)}) collective-permute-start(bf16[2,80,256]{2,1,0:T(8,128)(2,1)S(1)} %pad_maximum_fusion.1.refs_0_), channel_id=1, source_target_pairs={{0,2},{2,0},{4,6},{6,4},{8,10},{10,8},{12,14},{14,12},{1,3},{3,1},... | collective-permute-start | bytes 245768 | tf_op jit(solution)/shard_map/ppermute | solution.py:327
  11.0 0.9 %shard_map.83 = (f32[2,32,256]{2,1,0:T(8,128)S(1)}, bf16[3,256,256]{2,1,0:T(8,128)(2,1)S(1)}) custom-call(bf16[2,80,256]{2,1,0:T(8,128)(2,1)S(1)} %pad_maximum_fusion.1.refs_0_), custom_call_target="tpu_custom_call" | custom-call | flops 62914560 | bytes 81920 | tf_op jit(solution)/shard_map/pallas_call | solution.py:282
  12.0 0.7 %collective-permute-done.3 = bf16[2,80,256]{2,1,0:T(8,128)(2,1)S(1)} collective-permute-done((bf16[2,80,256]{2,1,0:T(8,128)(2,1)S(1)}, bf16[2,80,256]{2,1,0:T(8,128)(2,1)S(1)}, u32[]{:S(2)}, u32[]{:S(2)}) %collective-permute-start.3) | collective-permute-done | bytes 81952 | tf_op jit(solution)/shard_map/ppermute | solution.py:327
  12.8 0.0 copy-start
  12.8 0.0 copy-start.1
  12.8 1.6 %shard_map.84 = (f32[4,32,256]{2,1,0:T(8,128)S(1)}, bf16[7,256,256]{2,1,0:T(8,128)(2,1)S(1)}) custom-call(bf16[4,80,256]{2,1,0:T(8,128)(2,1)S(1)} %pad_maximum_fusion.refs_0_.refs_2_, f32[2,32,256]{2,1,0:T(8,128)S(1)} %get-tuple-element.9.refs_1_), custom_call_target="tpu_custom_call" | custom-call | flops 146800640 | bytes 163840 | tf_op jit(solution)/shard_map/pallas_call | solution.py:282
  14.4 0.0 collective-permute-done.2.refs_1_
  14.4 0.9 %collective-permute-done.1.refs_0_ = bf16[2,80,256]{2,1,0:T(8,128)(2,1)S(1)} collective-permute-done((bf16[2,80,256]{2,1,0:T(8,128)(2,1)S(1)}, bf16[2,80,256]{2,1,0:T(8,128)(2,1)S(1)}, u32[]{:S(2)}, u32[]{:S(2)}) %collective-permute-start.1) | collective-permute-done | bytes 81952 | tf_op jit(solution)/shard_map/ppermute | solution.py:327
  15.2 0.0 copy-done
  15.2 0.0 copy-done.1
  15.2 5.5 %shard_map.85 = f32[32,256]{1,0:T(8,128)} custom-call(bf16[2,80,256]{2,1,0:T(8,128)(2,1)S(1)} %collective-permute-done.1.refs_0_, bf16[2,80,256]{2,1,0:T(8,128)(2,1)S(1)} %collective-permute-done.2.refs_1_, bf16[4,80,256]{2,1,0:T(8,128)(2,1)S(1)} %pad_maximum_fusion.refs_0_.refs_2_, f32[32,256]{1,0:T(8,128)S(1)} %copy-done, f32[32,256]{1,0:T(8,128)S(1)} %copy-done.1, ...), custom_call_target="tpu_custom_call" | custom-call | flops 545259520 | bytes 327680 | tf_op jit(solution)/shard_map/pallas_call | solution.py:282
  (2 shorter events, 0.0 us)
Async XLA Ops:
  1.0 6.5 %collective-permute-start = (bf16[1,80,256]{2,1,0:T(8,128)(2,1)S(1)}, bf16[1,80,256]{2,1,0:T(8,128)(2,1)S(1)}, u32[]{:S(2)}, u32[]{:S(2)}) collective-permute-start(bf16[1,80,256]{2,1,0:T(8,128)(2,1)S(1)} %bitcast.5), channel_id=1, source_target_pairs={{0,8},{2,10},{4,12},{6,14},{8,0},{10,2},{12,4},{14,6},{1,9},{3,11}... | collective-permute-start | bytes 122888 | tf_op jit(solution)/shard_map/ppermute | solution.py:327
  7.5 5.3 %collective-permute-start.3 = (bf16[2,80,256]{2,1,0:T(8,128)(2,1)S(1)}, bf16[2,80,256]{2,1,0:T(8,128)(2,1)S(1)}, u32[]{:S(2)}, u32[]{:S(2)}) collective-permute-start(bf16[2,80,256]{2,1,0:T(8,128)(2,1)S(1)} %pad_maximum_fusion.1.refs_0_), channel_id=1, source_target_pairs={{0,4},{2,6},{4,0},{6,2},{8,12},{10,14},{12,8},{14,10},{1,5},{3,7},... | collective-permute-start | bytes 245768 | tf_op jit(solution)/shard_map/ppermute | solution.py:327
  9.0 5.4 %collective-permute-start.2 = (bf16[2,80,256]{2,1,0:T(8,128)(2,1)S(1)}, bf16[2,80,256]{2,1,0:T(8,128)(2,1)S(1)}, u32[]{:S(2)}, u32[]{:S(2)}) collective-permute-start(bf16[2,80,256]{2,1,0:T(8,128)(2,1)S(1)} %pad_maximum_fusion.1.refs_0_), channel_id=1, source_target_pairs={{0,6},{2,4},{4,2},{6,0},{8,14},{10,12},{12,10},{14,8},{1,7},{3,5},... | collective-permute-start | bytes 245768 | tf_op jit(solution)/shard_map/ppermute | solution.py:327
  10.7 4.5 %collective-permute-start.1 = (bf16[2,80,256]{2,1,0:T(8,128)(2,1)S(1)}, bf16[2,80,256]{2,1,0:T(8,128)(2,1)S(1)}, u32[]{:S(2)}, u32[]{:S(2)}) collective-permute-start(bf16[2,80,256]{2,1,0:T(8,128)(2,1)S(1)} %pad_maximum_fusion.1.refs_0_), channel_id=1, source_target_pairs={{0,2},{2,0},{4,6},{6,4},{8,10},{10,8},{12,14},{14,12},{1,3},{3,1},... | collective-permute-start | bytes 245768 | tf_op jit(solution)/shard_map/ppermute | solution.py:327
  12.8 2.5 %copy-start = (f32[32,256]{1,0:T(8,128)S(1)}, f32[32,256]{1,0:T(8,128)}, u32[]{:S(2)}) copy-start(f32[32,256]{1,0:T(8,128)} %refs_3_.1) | copy-start | bytes 98308
  12.8 2.5 %copy-start.1 = (f32[32,256]{1,0:T(8,128)S(1)}, f32[32,256]{1,0:T(8,128)}, u32[]{:S(2)}) copy-start(f32[32,256]{1,0:T(8,128)} %refs_4_.1) | copy-start | bytes 98308
